TPU v7x, 512 devices: a whole 4x8x8 slice. The times are simulated.
512 devices in a mesh: dp: 32 (over y, x), expert: 16 (over z, core).
Axes of the slice: x: 4, y: 8, z: 8, core: 2. Of those that a mesh axis runs over, the one named last changes fastest.
Arguments:
- hidden_in: bfloat16 [2048, 4096], P(('dp', 'expert')), may hold values from -6 to 6
- norm_gain: bfloat16 [4096], replicated, may hold values from 0.099609375 to 1.8984375
- expert_ids: int32 [2048, 8], P(('dp', 'expert')), may hold values from 0 to 63, all different within a row; in each aligned block of 64 rows (0 to 63, 64 to 127, ...) at most 16 rows name the same one
- gate_share: bfloat16 [2048, 8], P(('dp', 'expert')), may hold values from 0.049804688 to 0.25
- w_gate: bfloat16 [512, 192, 4096], P(('dp', 'expert')), may hold values from -0.09375 to 0.09375
- w_up: bfloat16 [512, 192, 4096], P(('dp', 'expert')), may hold values from -0.09375 to 0.09375
- w_down: bfloat16 [512, 192, 4096], P(('dp', 'expert')), may hold values from -0.15625 to 0.15625
Outputs:
- layer_out: bfloat16 [2048, 4096], P(('dp', 'expert'))
Inputs may be any that keep to these rules, and one draw needn't show every extreme that they name: `expert_ids`: each row names 8 different experts. Among the 64 rows of one request group (aligned blocks of 64 rows), no expert is named by more than 16 rows.
All inputs are finite; a program needn't handle non-finite values.
Results may differ from a plain program's by a relative error of at most 0.01.
Values may be sent and summed in bfloat16 or wider, within the bound.
No kernel may reach another device: no remote copies, remote signals or barrier semaphores. Data moves between devices by JAX's collectives and lax.ppermute only.
A program may use at most 64 MiB of HBM per device.

v0:
```python
import jax
import jax.numpy as jnp
from jax import lax
from jax.sharding import PartitionSpec as P

EXPERTS = 64
SPLIT = 8


def body(hidden_in, norm_gain, expert_ids, gate_share, w_gate, w_up, w_down):
    dp_count = lax.axis_size("dp")
    col_count = lax.axis_size("expert")
    row_index = lax.axis_index("dp")
    column = lax.axis_index("expert")
    tok_dev = hidden_in.shape[0]
    model_width = hidden_in.shape[1]
    slot_dev = w_gate.shape[0]
    block_units = w_gate.shape[1]
    experts_row = EXPERTS // dp_count
    per_dev = max(1, slot_dev // SPLIT)
    runs_dev = slot_dev // per_dev
    capacity = tok_dev * col_count // 4
    resid = hidden_in.astype(jnp.float32)
    inv_rms = lax.rsqrt(jnp.mean(resid * resid, axis=1, keepdims=True) + 1e-06)
    normed = (resid * inv_rms * norm_gain.astype(jnp.float32)[None, :]).astype(jnp.bfloat16)
    row_x, row_share, row_ids = (
        lax.all_gather(normed, "expert", axis=0, tiled=True),
        lax.all_gather(gate_share, "expert", axis=0, tiled=True),
        lax.all_gather(expert_ids, "expert", axis=0, tiled=True),
    )
    tok_row = row_x.shape[0]
    flat_ids = row_ids.reshape(-1)
    onehot = (flat_ids[:, None] == jnp.arange(EXPERTS, dtype=jnp.int32)[None, :]).astype(jnp.int32)
    order_pos = jnp.sum((jnp.cumsum(onehot, axis=0) - onehot) * onehot, axis=1)
    slot_keys = (flat_ids * capacity + order_pos).reshape(tok_row, row_ids.shape[1])
    dest_rows = jnp.arange(dp_count, dtype=jnp.int32)[:, None]
    held = (dest_rows * col_count + column) * slot_dev // SPLIT + jnp.arange(
        per_dev, dtype=jnp.int32
    )[None, :]
    targets = held[:, :, None] * capacity + jnp.arange(capacity, dtype=jnp.int32)[None, None, :]
    matches = slot_keys[None, None, None, :, :] == targets[:, :, :, None, None]
    share_f = row_share.astype(jnp.float32)[None, None, None, :, :]
    weighted = jnp.sum(jnp.where(matches, share_f, 0.0), axis=4).astype(jnp.bfloat16)
    gate_w = w_gate.reshape(per_dev, runs_dev, block_units, model_width)
    up_w = w_up.reshape(per_dev, runs_dev, block_units, model_width)
    down_w = w_down.reshape(per_dev, runs_dev, block_units, model_width)
    part_rows = capacity // col_count
    row_experts = dest_rows * experts_row + jnp.arange(experts_row, dtype=jnp.int32)[None, :]
    section_targets = (
        row_experts[:, :, None] * capacity
        + column * part_rows
        + jnp.arange(part_rows, dtype=jnp.int32)[None, None, :]
    )
    section_hits = jnp.any(
        slot_keys[None, None, None, :, :] == section_targets[:, :, :, None, None], axis=4
    )
    section_blocks = jnp.einsum(
        "qmst,td->qmsd",
        section_hits.astype(jnp.bfloat16),
        row_x,
        preferred_element_type=jnp.float32,
    ).astype(jnp.bfloat16)
    landed = lax.all_to_all(section_blocks, "dp", split_axis=0, concat_axis=0, tiled=True)
    own_first = (row_index * col_count + column) * slot_dev // SPLIT - row_index * experts_row
    own_rows = lax.dynamic_slice_in_dim(
        lax.all_gather(landed, "expert", axis=2, tiled=True), own_first, per_dev, 1
    )
    gate_vals = jnp.einsum("qisd,igfd->qisgf", own_rows, gate_w, preferred_element_type=jnp.float32)
    up_vals = jnp.einsum("qisd,igfd->qisgf", own_rows, up_w, preferred_element_type=jnp.float32)
    activated = (jax.nn.silu(gate_vals) * up_vals).astype(jnp.bfloat16)
    projected = jnp.einsum(
        "qisgf,igfd->qisd", activated, down_w, preferred_element_type=jnp.float32
    )
    partial_value = projected.astype(jnp.bfloat16)
    returned = lax.all_to_all(partial_value, "dp", split_axis=0, concat_axis=0, tiled=True)
    routed = lax.psum_scatter(
        jnp.einsum("qist,qisd->td", weighted, returned, preferred_element_type=jnp.float32).astype(
            jnp.bfloat16
        ),
        "expert",
        scatter_dimension=0,
        tiled=True,
    ).astype(jnp.float32)
    return (resid + routed).astype(jnp.bfloat16)


def solution(mesh):
    placed = (
        P(("dp", "expert"), None),
        P(),
        P(("dp", "expert"), None),
        P(("dp", "expert"), None),
        P(("dp", "expert"), None, None),
        P(("dp", "expert"), None, None),
        P(("dp", "expert"), None, None),
    )
    return jax.shard_map(
        body, mesh=mesh, in_specs=placed, out_specs=P(("dp", "expert"), None), check_vma=False
    )
```

profile of v0, /device:TPU:1, one launch (start us, length us, event | category | flops | bytes accessed | tf_op | source)
XLA Modules:
  0.0 379.1 jit_solution(21856899312096482)
XLA Ops:
  6.5 24.9 %all-gather = s32[16,4,8]{2,1,0:T(4,128)S(1)} all-gather(s32[1,4,8]{2,1,0:T(4,128)} %bitcast.112), channel_id=1, replica_groups=mesh['dp'=32,'expert'=16] {'expert'}, dimensions={0}, use_global_device_ids=true | all-gather | bytes 2176 | tf_op jit(solution)/shard_map/all_gather | solution.py:29
  31.7 1.2 reduce-window.6
  32.9 0.2 slice_reduce_fusion
  33.5 0.7 convert_element_type.65
  34.2 0.9 fusion.37
  35.1 0.8 fusion.41
  36.0 15.9 %all-gather.2 = bf16[16,4,4096]{2,1,0:T(4,128)(2,1)S(1)} all-gather(bf16[1,4,4096]{2,1,0:T(4,128)(2,1)S(1)} %fusion.41), channel_id=1, replica_groups=mesh['dp'=32,'expert'=16] {'expert'}, dimensions={0}, use_global_device_ids=true | all-gather | bytes 557056 | tf_op jit(solution)/shard_map/all_gather | solution.py:27
  52.3 0.3 fusion.2
  52.6 0.5 copy.23
  53.1 26.2 %all_to_all.10 = bf16[32,2,1,4096]{3,1,2,0:T(2,128)(2,1)S(1)} all-to-all(bf16[32,2,1,4096]{3,1,2,0:T(2,128)(2,1)S(1)} %copy.23), channel_id=1, replica_groups=mesh['dp'=32,'expert'=16] {'dp'}, dimensions={0} | all-to-all | bytes 1048576 | tf_op jit(solution)/shard_map/all_to_all | solution.py:63
  79.3 1.1 copy.24
  80.5 53.2 %all-gather.5.cloned.1.call-done = bf16[32,2,16,4096]{3,0,1,2:T(8,128)(2,1)} async-done(((bf16[32,2,1,4096]{3,0,1,2:T(8,128)(2,1)}), bf16[32,2,16,4096]{3,0,1,2:T(8,128)(2,1)}) %all-gather.5.cloned.1.call-update) | async-done | bytes 8388624 | tf_op jit(solution)/shard_map/all_gather | solution.py:66
  133.7 2.5 constant_dynamic-slice_fusion
  136.2 2.0 copy-done.1
  138.1 3.4 fusion.9
  141.5 9.4 %fusion = bf16[32,1,16,4096]{3,2,1,0:T(8,128)(2,1)} fusion(bf16[1,192,4096]{2,1,0:T(8,128)(2,1)S(1)} %copy-done, bf16[1,192,4096]{2,1,0:T(8,128)(2,1)} %param.12, bf16[32,1,16,4096]{3,0,1,2:T(8,128)(2,1)} %copy-done.1, f32[32,1,16,1,192]{4,2,0,3,1:T(8,128)} %fusion.9), kind=kOutput, calls=%fused_computation.1 | convolution fusion | flops 1613299712 | bytes 11927552 | tf_op jit(solution)/shard_map/qisgf,igfd->qisd/dot_general | solution.py:71
  150.8 9.5 %all-to-all-start.1 = ((bf16[32,1,16,4096]{3,2,1,0:T(8,128)(2,1)}), bf16[32,1,16,4096]{3,2,1,0:T(8,128)(2,1)}, u32[]{:S(2)}, u32[]{:S(2)}) async-start(bf16[32,1,16,4096]{3,2,1,0:T(8,128)(2,1)} %fusion), calls=%async_computation.1 | async-start | bytes 8388608 | tf_op jit(solution)/shard_map/all_to_all | solution.py:75
  160.4 15.8 %all-gather.1 = bf16[16,4,8]{2,1,0:T(4,128)(2,1)S(1)} all-gather(bf16[1,4,8]{2,1,0:T(4,128)(2,1)S(1)} %bitcast.113), channel_id=1, replica_groups=mesh['dp'=32,'expert'=16] {'expert'}, dimensions={0}, use_global_device_ids=true | all-gather | bytes 1088 | tf_op jit(solution)/shard_map/all_gather | solution.py:28
  176.4 0.9 select_reduce_fusion
  177.3 76.7 %all-to-all-done.1 = bf16[32,1,16,4096]{3,2,1,0:T(8,128)(2,1)} async-done(((bf16[32,1,16,4096]{3,2,1,0:T(8,128)(2,1)}), bf16[32,1,16,4096]{3,2,1,0:T(8,128)(2,1)}, u32[]{:S(2)}, u32[]{:S(2)}) %all-to-all-start.1) | async-done | bytes 4194336 | tf_op jit(solution)/shard_map/all_to_all | solution.py:75
  253.9 3.9 %fusion.1 = bf16[64,4096]{1,0:T(8,128)(2,1)} fusion(bf16[32,1,16,4096]{3,2,1,0:T(8,128)(2,1)} %all-to-all-done.1, bf16[32,16,64]{2,1,0:T(8,128)(2,1)S(1)} %select_reduce_fusion), kind=kOutput, calls=%fused_computation.3 | convolution fusion | flops 268697600 | bytes 4784128 | tf_op jit(solution)/shard_map/qist,qisd->td/dot_general | solution.py:77
  257.8 1.3 dynamic-slice
  259.7 111.0 %all-reduce.3.cloned.1.call-done = bf16[64,4096]{1,0:T(8,128)(2,1)} async-done(((bf16[64,4096]{1,0:T(8,128)(2,1)}), bf16[64,4096]{1,0:T(8,128)(2,1)}) %all-reduce.3.cloned.1.call-update) | async-done | bytes 524304
  370.7 1.5 fusion.40
  (31 shorter events, 1.2 us)
Async XLA Ops:
  6.5 134.9 %copy-start = (bf16[1,192,4096]{2,1,0:T(8,128)(2,1)S(1)}, bf16[1,192,4096]{2,1,0:T(8,128)(2,1)}, u32[]{:S(2)}) copy-start(bf16[1,192,4096]{2,1,0:T(8,128)(2,1)} %param.13) | copy-start | bytes 4718596
  6.5 127.2 %all-gather.5.cloned.1.call-start = ((), (), s32[]{:S(2)}) async-start(), calls=%async_computation.2 | async-start | bytes 8912896 | tf_op jit(solution)/shard_map/all_gather | solution.py:66
  80.5 57.6 %copy-start.4 = (bf16[1,192,4096]{2,1,0:T(8,128)(2,1)S(1)}, bf16[1,192,4096]{2,1,0:T(8,128)(2,1)}, u32[]{:S(2)}) copy-start(bf16[1,192,4096]{2,1,0:T(8,128)(2,1)} %param.11) | copy-start | bytes 4718596
  136.2 2.0 copy-start.1
  150.8 9.6 %copy-start.3 = (bf16[4,8]{1,0:T(4,128)(2,1)S(1)}, bf16[4,8]{1,0:T(4,128)(2,1)}, u32[]{:S(2)}) copy-start(bf16[4,8]{1,0:T(4,128)(2,1)} %param.10) | copy-start | bytes 196
  150.8 103.1 %all-to-all-start.1 = ((bf16[32,1,16,4096]{3,2,1,0:T(8,128)(2,1)}), bf16[32,1,16,4096]{3,2,1,0:T(8,128)(2,1)}, u32[]{:S(2)}, u32[]{:S(2)}) async-start(bf16[32,1,16,4096]{3,2,1,0:T(8,128)(2,1)} %fusion), calls=%async_computation.1 | async-start | bytes 8388608 | tf_op jit(solution)/shard_map/all_to_all | solution.py:75
  160.4 210.4 %copy-start.2 = (bf16[4,4096]{1,0:T(4,128)(2,1)S(1)}, bf16[4,4096]{1,0:T(4,128)(2,1)}, u32[]{:S(2)}) copy-start(bf16[4,4096]{1,0:T(4,128)(2,1)} %param.7) | copy-start | bytes 98308
  160.4 210.3 %all-reduce.3.cloned.1.call-start = ((), (), s32[]{:S(2)}) async-start(), calls=%async_computation.3 | async-start | bytes 1048576
Sparse Core Ops, SparseCore 0:
  80.6 53.0 all-gather.4
  257.9 112.7 all-reduce.2
where the time goes:
time: 380 us; the launch traced here: 379 us
  waiting for transfers between devices  241 us (63%)
  blocking collectives  82.8 us (22%)
  matrix products  16.8 us (4%)
  between operations  14.2 us (4%)
  starting transfers between devices  9.57 us (3%)
  local copies, waits for them, and re-layouts  8.15 us (2%)
  other arithmetic  6.59 us (2%)
    unnamed x3, waiting for transfers between devices  111 us
    all_to_all x1, waiting for transfers between devices, body(): lax.all_to_all(partial_value, 'dp', split_axis=0, concat_axis=0, tiled=True)  76.7 us
    all_gather x1, waiting for transfers between devices, body(): lax.all_gather(landed, 'expert', axis=2, tiled=True)  53.2 us
    all_to_all x1, blocking collectives, body(): lax.all_to_all(section_blocks, 'dp', split_axis=0, concat_axis=0, tiled=T...  26.2 us
    all_gather x1, blocking collectives, body(): lax.all_gather(expert_ids, 'expert', axis=0, tiled=True)  24.9 us
    all_gather x1, blocking collectives, body(): lax.all_gather(normed, 'expert', axis=0, tiled=True)  15.9 us
    all_gather x1, blocking collectives, body(): lax.all_gather(gate_share, 'expert', axis=0, tiled=True)  15.8 us
    all_to_all x1, starting transfers between devices, body(): lax.all_to_all(partial_value, 'dp', split_axis=0, concat_axis=0, tiled=True)  9.53 us
  transfers between devices with their start and end apart: 3, of which 3 were waited for; matrix products, arithmetic and copies ran while one was open for 1% of the time, Pallas kernels for 0%

commit v1 on v0

v1 whole, which is shorter than its diff:
```python
import functools

import jax
import jax.numpy as jnp
from jax import lax
from jax.experimental import pallas as pl
from jax.experimental.pallas import tpu as pltpu
from jax.sharding import PartitionSpec as P

EXPERTS = 64
SPLIT = 8
TOP = 8
CHUNKS = 2
VMEM = pl.BlockSpec(memory_space=pltpu.VMEM)
SMEM = pl.BlockSpec(memory_space=pltpu.SMEM)
PARAMS = pltpu.CompilerParams(vmem_limit_bytes=48 * 1024 * 1024)
NT = (((1,), (1,)), ((), ()))


def dot_nt(a, b):
    return lax.dot_general(a, b, NT, preferred_element_type=jnp.float32)


def norm_kernel(x_ref, gain_ref, meta_ref, out_ref):
    width = x_ref.shape[1]
    x = x_ref[...].astype(jnp.float32)
    inv = lax.rsqrt(jnp.mean(x * x, axis=1, keepdims=True) + 1e-06)
    out_ref[:, :width] = (x * inv * gain_ref[...].astype(jnp.float32)).astype(jnp.bfloat16)
    out_ref[:, width:] = meta_ref[...]


def pack_kernel(place_ref, row_ref, *outs):
    packed, weights = outs[:CHUNKS], outs[CHUNKS:]
    core, half = place_ref[0], place_ref[1]
    tokens = row_ref.shape[0]
    width = row_ref.shape[1] - 128
    part = width // 2
    rows = packed[0].shape[0]
    per = rows // (EXPERTS // 2)
    meta = row_ref[:, width:].astype(jnp.float32)
    lanes = lax.broadcasted_iota(jnp.int32, (tokens, EXPERTS), 1).astype(jnp.float32)
    named = jnp.zeros((tokens, EXPERTS), jnp.float32)
    share = jnp.zeros((tokens, EXPERTS), jnp.float32)
    for k in range(TOP):
        hit = meta[:, k : k + 1] == lanes
        named = jnp.where(hit, 1.0, named)
        share = jnp.where(hit, meta[:, TOP + k : TOP + k + 1], share)
    t_row = lax.broadcasted_iota(jnp.int32, (tokens, tokens), 0)
    t_col = lax.broadcasted_iota(jnp.int32, (tokens, tokens), 1)
    lower = (t_col < t_row).astype(jnp.bfloat16)
    before = jnp.dot(lower, named.astype(jnp.bfloat16), preferred_element_type=jnp.float32)
    rank = jnp.where(named > 0.0, before, -1.0).astype(jnp.bfloat16)
    slot = lax.broadcasted_iota(jnp.int32, (rows, EXPERTS), 0)
    expert = lax.broadcasted_iota(jnp.int32, (rows, EXPERTS), 1)
    pick = (expert == 2 * (slot // per) + half).astype(jnp.bfloat16)
    rank_of = dot_nt(pick, rank)
    rank_by = dot_nt(rank, pick)
    share_by = dot_nt(share.astype(jnp.bfloat16), pick)
    slot_of = (lax.broadcasted_iota(jnp.int32, (rows, tokens), 0) % per).astype(jnp.float32)
    slot_by = (lax.broadcasted_iota(jnp.int32, (tokens, rows), 1) % per).astype(jnp.float32)
    mine = row_ref[:, pl.ds(pl.multiple_of(core * part, 128), part)]
    for n in range(CHUNKS):
        first = float(n * per)
        chosen = (rank_of == slot_of + first).astype(jnp.bfloat16)
        packed[n][...] = jnp.dot(chosen, mine, preferred_element_type=jnp.float32).astype(jnp.bfloat16)
        weights[n][...] = jnp.where(rank_by == slot_by + first, share_by, 0.0).astype(jnp.bfloat16)


def up_kernel(place_ref, own_ref, other_ref, gate_ref, up_ref, down_ref, act_ref, give_ref):
    core = place_ref[0]
    part = own_ref.shape[1]
    mine = pl.ds(pl.multiple_of(core * part, 128), part)
    theirs = pl.ds(pl.multiple_of((1 - core) * part, 128), part)
    own, other = own_ref[...], other_ref[...]
    gate = dot_nt(own, gate_ref[:, mine]) + dot_nt(other, gate_ref[:, theirs])
    up = dot_nt(own, up_ref[:, mine]) + dot_nt(other, up_ref[:, theirs])
    act = (gate / (1.0 + jnp.exp(-gate)) * up).astype(jnp.bfloat16)
    act_ref[...] = act
    give_ref[...] = jnp.dot(act, down_ref[:, theirs], preferred_element_type=jnp.float32).astype(jnp.bfloat16)


def down_kernel(place_ref, act_ref, down_ref, got_ref, out_ref):
    part = got_ref.shape[1]
    mine = pl.ds(pl.multiple_of(place_ref[0] * part, 128), part)
    value = jnp.dot(act_ref[...], down_ref[:, mine], preferred_element_type=jnp.float32)
    out_ref[...] = (value + got_ref[...].astype(jnp.float32)).astype(jnp.bfloat16)


def combine_kernel(*refs):
    out_ref = refs[-1]
    total = None
    for n in range(CHUNKS):
        part = jnp.dot(refs[n][...], refs[CHUNKS + n][...], preferred_element_type=jnp.float32)
        total = part if total is None else total + part
    out_ref[...] = total.astype(jnp.bfloat16)


def final_kernel(resid_ref, got_ref, out_ref):
    tokens, part = got_ref.shape[1], got_ref.shape[2]
    for core in range(2):
        total = resid_ref[:, core * part : (core + 1) * part].astype(jnp.float32)
        for z in range(got_ref.shape[0] // 2):
            total = total + got_ref[2 * z + core].astype(jnp.float32)
        out_ref[:, core * part : (core + 1) * part] = total.astype(jnp.bfloat16)


def call(kernel, out_shape, *args, scalars=0):
    return pl.pallas_call(
        kernel,
        out_shape=out_shape,
        in_specs=[SMEM] * scalars + [VMEM] * (len(args) - scalars),
        out_specs=jax.tree.map(lambda _: VMEM, out_shape),
        compiler_params=PARAMS,
    )(*args)


def bf16(*shape):
    return jax.ShapeDtypeStruct(shape, jnp.bfloat16)


def body(hidden_in, norm_gain, expert_ids, gate_share, w_gate, w_up, w_down):
    dp_count = lax.axis_size("dp")
    col_count = lax.axis_size("expert")
    column = lax.axis_index("expert")
    tok_dev, width = hidden_in.shape
    units = w_gate.shape[1]
    tok_row = tok_dev * col_count
    part = width // 2
    per = tok_row // 4 // CHUNKS
    rows = dp_count * per
    place = jnp.stack([column % 2, column // (col_count // 2)]).astype(jnp.int32)
    partner = [(i, i ^ 1) for i in range(col_count)]
    gate_w, up_w, down_w = (w.reshape(units, width) for w in (w_gate, w_up, w_down))

    meta = jnp.concatenate([expert_ids.astype(jnp.bfloat16), gate_share], axis=1)
    meta = jnp.pad(meta, ((0, 0), (0, 128 - 2 * TOP)))
    normed = call(norm_kernel, bf16(tok_dev, width + 128), hidden_in, norm_gain.reshape(1, width), meta)
    row = lax.all_gather(normed, "expert", axis=0, tiled=True)
    outs = call(pack_kernel, [bf16(rows, part)] * CHUNKS + [bf16(tok_row, rows)] * CHUNKS, place, row, scalars=1)
    packed, weights = outs[:CHUNKS], outs[CHUNKS:]

    landed = [
        lax.all_to_all(p.reshape(dp_count, per, part), "dp", split_axis=0, concat_axis=0, tiled=True).reshape(rows, part)
        for p in packed
    ]
    returned = []
    for own in landed:
        other = lax.ppermute(own, "expert", partner)
        act, give = call(
            up_kernel, [bf16(rows, units), bf16(rows, part)], place, own, other, gate_w, up_w, down_w, scalars=1
        )
        got = lax.ppermute(give, "expert", partner)
        value = call(down_kernel, bf16(rows, part), place, act, down_w, got, scalars=1)
        back = lax.all_to_all(value.reshape(dp_count, per, part), "dp", split_axis=0, concat_axis=0, tiled=True)
        returned.append(back.reshape(rows, part))
    routed = call(combine_kernel, bf16(tok_row, part), *weights, *returned)
    shares = lax.all_to_all(
        routed.reshape(col_count, tok_dev, part), "expert", split_axis=0, concat_axis=0, tiled=True
    )
    return call(final_kernel, bf16(tok_dev, width), hidden_in, shares)


def solution(mesh):
    rows = P(("dp", "expert"), None)
    blocks = P(("dp", "expert"), None, None)
    return jax.shard_map(
        body, mesh=mesh, in_specs=(rows, P(), rows, rows, blocks, blocks, blocks), out_specs=rows, check_vma=False
    )
```

time: 380 us -> 194 us (0.51)
  waiting for transfers between devices: 241 us -> 38.6 us
  blocking collectives: 82.8 us -> 111 us
  matrix products: 16.8 us -> 0 us
  Pallas kernels: 0 us -> 14.7 us
  between operations: 14.2 us -> 0.22 us
  starting transfers between devices: 9.57 us -> 22.9 us
  other arithmetic: 6.59 us -> 1.52 us
  local copies, waits for them, and re-layouts: 8.15 us -> 3.9 us
    unnamed x3 -> x0, waiting for transfers between devices: 111 us -> none
    all_to_all x1 -> x3, blocking collectives: 26.2 us -> 85.2 us  [the longest x1 36.6 us: body(): lax.all_to_all(p.reshape(dp_count, per, part), 'dp', split_axis=0, concat...]
    all_gather x1 -> x0, waiting for transfers between devices: 53.2 us -> none  [body(): lax.all_gather(landed, 'expert', axis=2, tiled=True)]
    all_to_all x1 -> x2, waiting for transfers between devices: 76.7 us -> 36.3 us  [the longest x1 18.8 us: body(): lax.all_to_all(p.reshape(dp_count, per, part), 'dp', split_axis=0, concat...]
    all_gather x3 -> x1, blocking collectives: 56.6 us -> 26 us  [body(): row = lax.all_gather(normed, 'expert', axis=0, tiled=True)]
    dot_general x4 -> x0, matrix products: 16.8 us -> none  [the longest x1 9.36 us: body(): jnp.einsum('qisgf,igfd->qisd', activated, down_w, preferred_element_type=...]
    pallas_call x0 -> x8, Pallas kernels: none -> 14.7 us  [call(): pl.pallas_call(kernel, out_shape=out_shape, in_specs=[SMEM] * scalars + [...]
    ppermute x0 -> x4, starting transfers between devices: none -> 12.1 us  [the longest x2 7.72 us: body(): other = lax.ppermute(own, 'expert', partner)]
  transfers between devices with their start and end apart: 3 -> 6, of which waited for: 3 -> 3; matrix products, arithmetic and copies ran while one was open for 1% -> 0% of each run, Pallas kernels for 0% -> 6%
where the time goes in v1:
time: 194 us; the launch traced here: 193 us
  blocking collectives  111 us (57%)
  waiting for transfers between devices  38.6 us (20%)
  starting transfers between devices  22.9 us (12%)
  Pallas kernels  14.7 us (8%)
  local copies, waits for them, and re-layouts  3.9 us (2%)
    all_to_all x1, blocking collectives, body(): lax.all_to_all(p.reshape(dp_count, per, part), 'dp', split_axis=0, concat...  36.6 us
    all_to_all x1, blocking collectives, body(): lax.all_to_all(value.reshape(dp_count, per, part), 'dp', split_axis=0, co...  31.1 us
    all_gather x1, blocking collectives, body(): row = lax.all_gather(normed, 'expert', axis=0, tiled=True)  26 us
    all_to_all x1, waiting for transfers between devices, body(): lax.all_to_all(p.reshape(dp_count, per, part), 'dp', split_axis=0, concat...  18.8 us
    all_to_all x1, blocking collectives, body(): lax.all_to_all(routed.reshape(col_count, tok_dev, part), 'expert', split_...  17.6 us
    all_to_all x1, waiting for transfers between devices, body(): lax.all_to_all(value.reshape(dp_count, per, part), 'dp', split_axis=0, co...  17.4 us
    pallas_call x8, Pallas kernels, call(): pl.pallas_call(kernel, out_shape=out_shape, in_specs=[SMEM] * scalars + [...  14.7 us
    ppermute x2, starting transfers between devices, body(): other = lax.ppermute(own, 'expert', partner)  7.72 us
  transfers between devices with their start and end apart: 6, of which 3 were waited for; matrix products, arithmetic and copies ran while one was open for 0% of the time, Pallas kernels for 6%

profile of v1, /device:TPU:1, one launch (start us, length us, event | category | flops | bytes accessed | tf_op | source)
XLA Modules:
  0.0 193.1 jit_solution(2065096080966835287)
XLA Ops:
  0.0 0.7 convert_element_type.5
  0.7 0.7 reshape.39.gain_ref
  1.4 0.8 fusion.2.meta_ref
  2.2 0.8 copy-done.7
  3.0 26.0 %all-gather = bf16[16,4,4224]{2,1,0:T(4,128)(2,1)S(1)} all-gather(bf16[1,4,4224]{2,1,0:T(4,128)(2,1)S(1)} %bitcast.28), channel_id=1, replica_groups=mesh['dp'=32,'expert'=16] {'expert'}, dimensions={0}, use_global_device_ids=true | all-gather | bytes 574464 | tf_op jit(solution)/shard_map/all_gather | solution.py:138
  29.3 1.6 shard_map.74
  30.9 36.6 %all_to_all.25 = bf16[32,8,2048]{2,1,0:T(8,128)(2,1)S(1)} all-to-all(bf16[32,8,2048]{2,1,0:T(8,128)(2,1)S(1)} %bitcast.27), channel_id=1, replica_groups=mesh['dp'=32,'expert'=16] {'dp'}, dimensions={0} | all-to-all | bytes 2097152 | tf_op jit(solution)/shard_map/all_to_all | solution.py:143
  67.4 4.1 %collective-permute-start.2 = (bf16[256,2048]{1,0:T(8,128)(2,1)S(1)}, bf16[256,2048]{1,0:T(8,128)(2,1)}, u32[]{:S(2)}, u32[]{:S(2)}) collective-permute-start(bf16[256,2048]{1,0:T(8,128)(2,1)S(1)} %bitcast.23), channel_id=1, source_target_pairs={{0,1},{1,0},{2,3},{3,2},{4,5},{5,4},{6,7},{7,6},{8,9},{9,8},{10,11... | collective-permute-start | bytes 3145736 | tf_op jit(solution)/shard_map/ppermute | solution.py:148
  71.5 5.4 %all-to-all-start = ((bf16[32,8,2048]{2,1,0:T(8,128)(2,1)}), bf16[32,8,2048]{2,1,0:T(8,128)(2,1)}, u32[]{:S(2)}, u32[]{:S(2)}) async-start(bf16[32,8,2048]{2,1,0:T(8,128)(2,1)} %bitcast.26), calls=%async_computation | async-start | bytes 2097152 | tf_op jit(solution)/shard_map/all_to_all | solution.py:143
  77.0 1.2 copy-done.5
  78.2 4.9 %shard_map.77 = (bf16[256,192]{1,0:T(8,128)(2,1)S(1)}, bf16[256,2048]{1,0:T(8,128)(2,1)}) custom-call(s32[2]{0:T(128)S(1)} %pad_add_fusion.place_ref, bf16[256,2048]{1,0:T(8,128)(2,1)S(1)} %bitcast.24, bf16[256,2048]{1,0:T(8,128)(2,1)} %collective-permute-done.2.other_ref, bf16[192,4096]{1,0:T(8,128)(2,1)S(1)} %bitcast.18, bf16[192,4096]{1,0:T(8,128)(2,1)} %bitcast.29, ...), custom_call_target="tpu_custom_call" | custom-call | tf_op jit(solution)/shard_map/pallas_call | solution.py:108
  83.2 2.2 %collective-permute-start.3 = (bf16[256,2048]{1,0:T(8,128)(2,1)}, bf16[256,2048]{1,0:T(8,128)(2,1)}, u32[]{:S(2)}, u32[]{:S(2)}) collective-permute-start(bf16[256,2048]{1,0:T(8,128)(2,1)} %get-tuple-element.20), channel_id=1, source_target_pairs={{0,1},{1,0},{2,3},{3,2},{4,5},{5,4},{6,7},{7,6},{8,9},{9,8},{10,11... | collective-permute-start | bytes 3145736 | tf_op jit(solution)/shard_map/ppermute | solution.py:152
  85.4 18.8 %all-to-all-done = bf16[32,8,2048]{2,1,0:T(8,128)(2,1)} async-done(((bf16[32,8,2048]{2,1,0:T(8,128)(2,1)}), bf16[32,8,2048]{2,1,0:T(8,128)(2,1)}, u32[]{:S(2)}, u32[]{:S(2)}) %all-to-all-start) | async-done | bytes 1048608 | tf_op jit(solution)/shard_map/all_to_all | solution.py:143
  104.2 3.6 %collective-permute-start = (bf16[256,2048]{1,0:T(8,128)(2,1)}, bf16[256,2048]{1,0:T(8,128)(2,1)}, u32[]{:S(2)}, u32[]{:S(2)}) collective-permute-start(bf16[256,2048]{1,0:T(8,128)(2,1)} %bitcast.4.own_ref), channel_id=1, source_target_pairs={{0,1},{1,0},{2,3},{3,2},{4,5},{5,4},{6,7},{7,6},{8,9},{9,8},{10,11... | collective-permute-start | bytes 3145736 | tf_op jit(solution)/shard_map/ppermute | solution.py:148
  107.9 1.7 shard_map.78
  109.6 1.0 copy-done.3
  110.5 5.3 %all-to-all-start.3 = ((bf16[32,8,2048]{2,1,0:T(8,128)(2,1)}), bf16[32,8,2048]{2,1,0:T(8,128)(2,1)S(1)}, u32[]{:S(2)}, u32[]{:S(2)}) async-start(bf16[32,8,2048]{2,1,0:T(8,128)(2,1)} %bitcast.22), calls=%async_computation.3 | async-start | bytes 2097152 | tf_op jit(solution)/shard_map/all_to_all | solution.py:154
  115.9 4.3 %shard_map.75 = (bf16[256,192]{1,0:T(8,128)(2,1)S(1)}, bf16[256,2048]{1,0:T(8,128)(2,1)S(1)}) custom-call(s32[2]{0:T(128)S(1)} %pad_add_fusion.place_ref, bf16[256,2048]{1,0:T(8,128)(2,1)} %bitcast.4.own_ref, bf16[256,2048]{1,0:T(8,128)(2,1)} %collective-permute-done.other_ref, bf16[192,4096]{1,0:T(8,128)(2,1)S(1)} %bitcast.19, bf16[192,4096]{1,0:T(8,128)(2,1)} %bitcast.30, ...), custom_call_target="tpu_custom_call" | custom-call | tf_op jit(solution)/shard_map/pallas_call | solution.py:108
  120.2 2.2 %collective-permute-start.1 = (bf16[256,2048]{1,0:T(8,128)(2,1)S(1)}, bf16[256,2048]{1,0:T(8,128)(2,1)S(1)}, u32[]{:S(2)}, u32[]{:S(2)}) collective-permute-start(bf16[256,2048]{1,0:T(8,128)(2,1)S(1)} %get-tuple-element.17), channel_id=1, source_target_pairs={{0,1},{1,0},{2,3},{3,2},{4,5},{5,4},{6,7},{7,6},{8,9},{9,8},{10,11... | collective-permute-start | bytes 3145736 | tf_op jit(solution)/shard_map/ppermute | solution.py:152
  122.4 2.4 %collective-permute-done.1.got_ref = bf16[256,2048]{1,0:T(8,128)(2,1)S(1)} collective-permute-done((bf16[256,2048]{1,0:T(8,128)(2,1)S(1)}, bf16[256,2048]{1,0:T(8,128)(2,1)S(1)}, u32[]{:S(2)}, u32[]{:S(2)}) %collective-permute-start.1) | collective-permute-done | bytes 1048608 | tf_op jit(solution)/shard_map/ppermute | solution.py:152
  124.7 1.0 shard_map.76
  125.7 17.4 %all-to-all-done.3 = bf16[32,8,2048]{2,1,0:T(8,128)(2,1)S(1)} async-done(((bf16[32,8,2048]{2,1,0:T(8,128)(2,1)}), bf16[32,8,2048]{2,1,0:T(8,128)(2,1)S(1)}, u32[]{:S(2)}, u32[]{:S(2)}) %all-to-all-start.3) | async-done | bytes 1048608 | tf_op jit(solution)/shard_map/all_to_all | solution.py:154
  143.1 31.1 %all_to_all.26 = bf16[32,8,2048]{2,1,0:T(8,128)(2,1)S(1)} all-to-all(bf16[32,8,2048]{2,1,0:T(8,128)(2,1)S(1)} %bitcast.25), channel_id=1, replica_groups=mesh['dp'=32,'expert'=16] {'dp'}, dimensions={0} | all-to-all | bytes 2097152 | tf_op jit(solution)/shard_map/all_to_all | solution.py:154
  174.8 17.6 %all_to_all.27.got_ref = bf16[16,4,2048]{2,1,0:T(4,128)(2,1)S(1)} all-to-all(bf16[16,4,2048]{2,1,0:T(4,128)(2,1)S(1)} %reshape.51), channel_id=1, replica_groups=mesh['dp'=32,'expert'=16] {'expert'}, dimensions={0} | all-to-all | bytes 524288 | tf_op jit(solution)/shard_map/all_to_all | solution.py:157
  (24 shorter events, 1.6 us)
Async XLA Ops:
  2.2 0.8 copy-start.7
  30.9 40.7 %copy-start.6 = (bf16[256,2048]{1,0:T(8,128)(2,1)}, bf16[256,2048]{1,0:T(8,128)(2,1)S(1)}, u32[]{:S(2)}) copy-start(bf16[256,2048]{1,0:T(8,128)(2,1)S(1)} %get-tuple-element.15) | copy-start | bytes 3145732
  67.4 9.6 %copy-start.4 = (bf16[32,8,2048]{2,1,0:T(8,128)(2,1)}, bf16[32,8,2048]{2,1,0:T(8,128)(2,1)S(1)}, u32[]{:S(2)}) copy-start(bf16[32,8,2048]{2,1,0:T(8,128)(2,1)S(1)} %all_to_all.25) | copy-start | bytes 3145732
  67.4 9.6 %copy-start.2 = (bf16[1,192,4096]{2,1,0:T(8,128)(2,1)S(1)}, bf16[1,192,4096]{2,1,0:T(8,128)(2,1)}, u32[]{:S(2)}) copy-start(bf16[1,192,4096]{2,1,0:T(8,128)(2,1)} %param.11) | copy-start | bytes 4718596
  67.4 9.6 %collective-permute-start.2 = (bf16[256,2048]{1,0:T(8,128)(2,1)S(1)}, bf16[256,2048]{1,0:T(8,128)(2,1)}, u32[]{:S(2)}, u32[]{:S(2)}) collective-permute-start(bf16[256,2048]{1,0:T(8,128)(2,1)S(1)} %bitcast.23), channel_id=1, source_target_pairs={{0,1},{1,0},{2,3},{3,2},{4,5},{5,4},{6,7},{7,6},{8,9},{9,8},{10,11... | collective-permute-start | bytes 3145736 | tf_op jit(solution)/shard_map/ppermute | solution.py:148
  71.5 32.7 %all-to-all-start = ((bf16[32,8,2048]{2,1,0:T(8,128)(2,1)}), bf16[32,8,2048]{2,1,0:T(8,128)(2,1)}, u32[]{:S(2)}, u32[]{:S(2)}) async-start(bf16[32,8,2048]{2,1,0:T(8,128)(2,1)} %bitcast.26), calls=%async_computation | async-start | bytes 2097152 | tf_op jit(solution)/shard_map/all_to_all | solution.py:143
  77.0 1.2 copy-start.5
  78.2 29.6 %copy-start = (bf16[1,192,4096]{2,1,0:T(8,128)(2,1)S(1)}, bf16[1,192,4096]{2,1,0:T(8,128)(2,1)}, u32[]{:S(2)}) copy-start(bf16[1,192,4096]{2,1,0:T(8,128)(2,1)} %param.13) | copy-start | bytes 4718596
  83.2 24.7 %collective-permute-start.3 = (bf16[256,2048]{1,0:T(8,128)(2,1)}, bf16[256,2048]{1,0:T(8,128)(2,1)}, u32[]{:S(2)}, u32[]{:S(2)}) collective-permute-start(bf16[256,2048]{1,0:T(8,128)(2,1)} %get-tuple-element.20), channel_id=1, source_target_pairs={{0,1},{1,0},{2,3},{3,2},{4,5},{5,4},{6,7},{7,6},{8,9},{9,8},{10,11... | collective-permute-start | bytes 3145736 | tf_op jit(solution)/shard_map/ppermute | solution.py:152
  104.2 11.6 %collective-permute-start = (bf16[256,2048]{1,0:T(8,128)(2,1)}, bf16[256,2048]{1,0:T(8,128)(2,1)}, u32[]{:S(2)}, u32[]{:S(2)}) collective-permute-start(bf16[256,2048]{1,0:T(8,128)(2,1)} %bitcast.4.own_ref), channel_id=1, source_target_pairs={{0,1},{1,0},{2,3},{3,2},{4,5},{5,4},{6,7},{7,6},{8,9},{9,8},{10,11... | collective-permute-start | bytes 3145736 | tf_op jit(solution)/shard_map/ppermute | solution.py:148
  109.6 1.0 copy-start.3
  110.5 32.6 %all-to-all-start.3 = ((bf16[32,8,2048]{2,1,0:T(8,128)(2,1)}), bf16[32,8,2048]{2,1,0:T(8,128)(2,1)S(1)}, u32[]{:S(2)}, u32[]{:S(2)}) async-start(bf16[32,8,2048]{2,1,0:T(8,128)(2,1)} %bitcast.22), calls=%async_computation.3 | async-start | bytes 2097152 | tf_op jit(solution)/shard_map/all_to_all | solution.py:154
  115.8 8.9 %copy-start.1 = (bf16[1,192,4096]{2,1,0:T(8,128)(2,1)S(1)}, bf16[1,192,4096]{2,1,0:T(8,128)(2,1)}, u32[]{:S(2)}) copy-start(bf16[1,192,4096]{2,1,0:T(8,128)(2,1)} %param.13) | copy-start | bytes 4718596
  120.2 4.6 %collective-permute-start.1 = (bf16[256,2048]{1,0:T(8,128)(2,1)S(1)}, bf16[256,2048]{1,0:T(8,128)(2,1)S(1)}, u32[]{:S(2)}, u32[]{:S(2)}) collective-permute-start(bf16[256,2048]{1,0:T(8,128)(2,1)S(1)} %get-tuple-element.17), channel_id=1, source_target_pairs={{0,1},{1,0},{2,3},{3,2},{4,5},{5,4},{6,7},{7,6},{8,9},{9,8},{10,11... | collective-permute-start | bytes 3145736 | tf_op jit(solution)/shard_map/ppermute | solution.py:152
  174.2 18.2 %copy-start.8 = (bf16[4,4096]{1,0:T(4,128)(2,1)S(1)}, bf16[4,4096]{1,0:T(4,128)(2,1)}, u32[]{:S(2)}) copy-start(bf16[4,4096]{1,0:T(4,128)(2,1)} %resid_ref.1) | copy-start | bytes 98308

commit v2 on v1

v2 whole, which is shorter than its diff:
```python
import jax
import jax.numpy as jnp
from jax import lax
from jax.experimental import pallas as pl
from jax.experimental.pallas import tpu as pltpu
from jax.sharding import PartitionSpec as P

EXPERTS = 64
TOP = 8
CHUNKS = 2
META = 128
VMEM = pl.BlockSpec(memory_space=pltpu.VMEM)
HBM = pl.BlockSpec(memory_space=pltpu.HBM)
PARAMS = pltpu.CompilerParams(vmem_limit_bytes=20 * 1024 * 1024)
WHOLE = pltpu.CompilerParams(vmem_limit_bytes=62 * 1024 * 1024)
NT = (((1,), (1,)), ((), ()))


def dot_nt(a, b):
    return lax.dot_general(a, b, NT, preferred_element_type=jnp.float32)


def dot_nn(a, b):
    return jnp.dot(a, b, preferred_element_type=jnp.float32)


def norm_kernel(x_hbm, gain_hbm, ids_hbm, share_hbm, out_ref, x_ref, gain_ref, ids_ref, share_ref, sems):
    copies = [
        pltpu.make_async_copy(src, dst, sems.at[n])
        for n, (src, dst) in enumerate(
            [(x_hbm, x_ref), (gain_hbm, gain_ref), (ids_hbm, ids_ref), (share_hbm, share_ref)]
        )
    ]
    for copy in copies:
        copy.start()
    for copy in copies:
        copy.wait()
    part = x_ref.shape[1] // 2
    x = x_ref[...].astype(jnp.float32)
    inv = lax.rsqrt(jnp.mean(x * x, axis=1, keepdims=True) + 1e-06)
    normed = (x * inv * gain_ref[...].astype(jnp.float32)[None, :]).astype(jnp.bfloat16)
    ids = ids_ref[...].astype(jnp.float32)
    share = share_ref[...].astype(jnp.float32)
    lane = lax.broadcasted_iota(jnp.int32, (x.shape[0], META), 1)
    meta = jnp.zeros((x.shape[0], META), jnp.float32)
    for k in range(TOP):
        meta = jnp.where(lane == k, ids[:, k : k + 1], meta)
        meta = jnp.where(lane == TOP + k, share[:, k : k + 1], meta)
    meta = meta.astype(jnp.bfloat16)
    for j in range(out_ref.shape[0]):
        half = j % 2
        out_ref[j, :, :part] = normed[:, half * part : (half + 1) * part]
        out_ref[j, :, part:] = meta


def ranks(meta):
    tokens = meta.shape[0]
    meta = meta.astype(jnp.float32)
    lanes = lax.broadcasted_iota(jnp.int32, (tokens, EXPERTS), 1).astype(jnp.float32)
    named = jnp.zeros((tokens, EXPERTS), jnp.float32)
    share = jnp.zeros((tokens, EXPERTS), jnp.float32)
    for k in range(TOP):
        hit = meta[:, k : k + 1] == lanes
        named = jnp.where(hit, 1.0, named)
        share = jnp.where(hit, meta[:, TOP + k : TOP + k + 1], share)
    t_row = lax.broadcasted_iota(jnp.int32, (tokens, tokens), 0)
    t_col = lax.broadcasted_iota(jnp.int32, (tokens, tokens), 1)
    before = dot_nn((t_col < t_row).astype(jnp.bfloat16), named.astype(jnp.bfloat16))
    rank = jnp.where(named > 0.0, before, -1.0)
    return rank.astype(jnp.bfloat16), share.astype(jnp.bfloat16)


def picks(rows):
    per = rows // (EXPERTS // 2)
    slot = lax.broadcasted_iota(jnp.int32, (rows, EXPERTS), 0)
    expert = lax.broadcasted_iota(jnp.int32, (rows, EXPERTS), 1)
    return (expert == 2 * (slot // per) + lax.axis_index("expert") // 8).astype(jnp.bfloat16)


def pack_kernel(row_ref, quarter_ref, half_ref):
    tokens, (rows, part) = row_ref.shape[0], quarter_ref.shape
    width = half_ref.shape[1]
    per = rows // (EXPERTS // 2)
    _, b = place()
    rank, _ = ranks(row_ref[:, width:])
    rank_of = dot_nt(picks(rows), rank)
    slot = (lax.broadcasted_iota(jnp.int32, (rows, tokens), 0) % per).astype(jnp.float32)
    early = (rank_of == slot).astype(jnp.bfloat16)
    late = (rank_of == slot + float(per)).astype(jnp.bfloat16)
    quarter = row_ref[:, pl.ds(pl.multiple_of(b * part, part), part)]
    half_ref[...] = dot_nn(late, row_ref[:, :width]).astype(jnp.bfloat16)
    quarter_ref[...] = dot_nn(early, quarter).astype(jnp.bfloat16)


def weigh_kernel(row_ref, *outs):
    rank, share = ranks(row_ref[:, row_ref.shape[1] - META :])
    tokens, rows = outs[0].shape
    per = rows // (EXPERTS // 2)
    pick = picks(rows)
    rank_by, share_by = dot_nt(rank, pick), dot_nt(share, pick)
    slot = (lax.broadcasted_iota(jnp.int32, (tokens, rows), 1) % per).astype(jnp.float32)
    for n in range(CHUNKS):
        outs[n][...] = jnp.where(rank_by == slot + float(n * per), share_by, 0.0).astype(jnp.bfloat16)


def place():
    column = lax.axis_index("expert")
    return column % 2, (column // 2) % 2


def columns(ref, index, parts):
    part = ref.shape[1] // parts
    return ref[:, pl.ds(pl.multiple_of(index * part, part), part)]


def silu_mul(gate, up):
    return (gate / (1.0 + jnp.exp(-gate)) * up).astype(jnp.bfloat16)


def pair_first_kernel(own_ref, core_ref, gate_ref, up_ref, gate_out, up_out):
    c, b = place()
    own, other = own_ref[...], core_ref[...]
    mine, theirs = 2 * c + b, 2 * (1 - c) + b
    gate_out[...] = dot_nt(own, columns(gate_ref, mine, 4)) + dot_nt(other, columns(gate_ref, theirs, 4))
    up_out[...] = dot_nt(own, columns(up_ref, mine, 4)) + dot_nt(other, columns(up_ref, theirs, 4))


def pair_act_kernel(z_ref, diag_ref, gate_in, up_in, gate_ref, up_ref, down_ref, act_ref, give_ref):
    c, b = place()
    own, other = z_ref[...], diag_ref[...]
    mine, theirs = 2 * c + 1 - b, 2 * (1 - c) + 1 - b
    gate = gate_in[...] + dot_nt(own, columns(gate_ref, mine, 4)) + dot_nt(other, columns(gate_ref, theirs, 4))
    up = up_in[...] + dot_nt(own, columns(up_ref, mine, 4)) + dot_nt(other, columns(up_ref, theirs, 4))
    act = silu_mul(gate, up)
    act_ref[...] = act
    give_ref[...] = dot_nn(act, columns(down_ref, 1 - c, 2)).astype(jnp.bfloat16)


def half_first_kernel(own_ref, gate_ref, up_ref, gate_out, up_out):
    c, _ = place()
    own = own_ref[...]
    gate_out[...] = dot_nt(own, columns(gate_ref, c, 2))
    up_out[...] = dot_nt(own, columns(up_ref, c, 2))


def half_act_kernel(other_ref, gate_in, up_in, gate_ref, up_ref, down_ref, act_ref, give_ref):
    c, _ = place()
    other = other_ref[...]
    gate = gate_in[...] + dot_nt(other, columns(gate_ref, 1 - c, 2))
    up = up_in[...] + dot_nt(other, columns(up_ref, 1 - c, 2))
    act = silu_mul(gate, up)
    act_ref[...] = act
    give_ref[...] = dot_nn(act, columns(down_ref, 1 - c, 2)).astype(jnp.bfloat16)


def half_down_kernel(act_ref, down_ref, got_ref, out_ref):
    c, _ = place()
    total = dot_nn(act_ref[...], columns(down_ref, c, 2)) + got_ref[...].astype(jnp.float32)
    out_ref[...] = total.astype(jnp.bfloat16)


def pair_down_kernel(act_ref, down_ref, got_ref, mine_ref, send_ref):
    c, b = place()
    act = act_ref[...]
    send = dot_nn(act, columns(down_ref, 2 * c + 1 - b, 4)) + columns(got_ref, 1 - b, 2).astype(jnp.float32)
    send_ref[...] = send.astype(jnp.bfloat16)
    mine_ref[...] = dot_nn(act, columns(down_ref, 2 * c + b, 4)) + columns(got_ref, b, 2).astype(jnp.float32)


def add_kernel(mine_ref, got_ref, out_ref):
    out_ref[...] = (mine_ref[...] + got_ref[...].astype(jnp.float32)).astype(jnp.bfloat16)


def weighted_kernel(weight_ref, in_ref, out_ref):
    out_ref[...] = dot_nn(weight_ref[...], in_ref[...])


def combine_kernel(weight_ref, in_ref, whole_ref, out_ref):
    _, b = place()
    part = in_ref.shape[1]
    some = dot_nn(weight_ref[...], in_ref[...])
    out_ref[:, :part] = (whole_ref[:, :part] + jnp.where(b == 0, some, 0.0)).astype(jnp.bfloat16)
    out_ref[:, part:] = (whole_ref[:, part:] + jnp.where(b == 0, 0.0, some)).astype(jnp.bfloat16)


def final_kernel(resid_ref, got_ref, out_ref):
    part = got_ref.shape[2]
    for c in range(2):
        cols = slice(c * part, (c + 1) * part)
        total = resid_ref[:, cols].astype(jnp.float32)
        for j in range(c, got_ref.shape[0], 2):
            total = total + got_ref[j].astype(jnp.float32)
        out_ref[:, cols] = total.astype(jnp.bfloat16)


def call(kernel, out_shape, *args):
    return pl.pallas_call(
        kernel,
        out_shape=out_shape,
        in_specs=[VMEM] * len(args),
        out_specs=jax.tree.map(lambda _: VMEM, out_shape),
        compiler_params=PARAMS,
    )(*args)


def bf16(*shape):
    return jax.ShapeDtypeStruct(shape, jnp.bfloat16)


def f32(*shape):
    return jax.ShapeDtypeStruct(shape, jnp.float32)


def body(hidden_in, norm_gain, expert_ids, gate_share, w_gate, w_up, w_down):
    dp_count = lax.axis_size("dp")
    col_count = lax.axis_size("expert")
    tok_dev, width = hidden_in.shape
    units = w_gate.shape[1]
    tok_row = tok_dev * col_count
    half, part = width // 2, width // 4
    per = tok_row // 4 // CHUNKS
    rows = dp_count * per
    core = [(i, i ^ 1) for i in range(col_count)]
    pair = [(i, i ^ 2) for i in range(col_count)]
    gate_w, up_w, down_w = (w.reshape(units, width) for w in (w_gate, w_up, w_down))
    partial_sums = [f32(rows, units)] * 2
    activated = [bf16(rows, units), bf16(rows, half)]

    def over_dp(x):
        moved = lax.all_to_all(x.reshape(dp_count, per, x.shape[1]), "dp", split_axis=0, concat_axis=0, tiled=True)
        return moved.reshape(x.shape)

    def over_expert(x):
        return lax.all_to_all(x, "expert", split_axis=0, concat_axis=0, tiled=True)

    normed = pl.pallas_call(
        norm_kernel,
        out_shape=bf16(col_count, tok_dev, half + META),
        in_specs=[HBM] * 4,
        out_specs=VMEM,
        scratch_shapes=[
            pltpu.VMEM((tok_dev, width), jnp.bfloat16),
            pltpu.VMEM((width,), jnp.bfloat16),
            pltpu.VMEM((tok_dev, TOP), jnp.int32),
            pltpu.VMEM((tok_dev, TOP), jnp.bfloat16),
            pltpu.SemaphoreType.DMA((4,)),
        ],
        compiler_params=WHOLE,
    )(hidden_in, norm_gain, expert_ids, gate_share)
    row = over_expert(normed).reshape(tok_row, half + META)
    packed = call(pack_kernel, [bf16(rows, part), bf16(rows, half)], row)
    weights = call(weigh_kernel, [bf16(tok_row, rows)] * CHUNKS, row)

    own = over_dp(packed[0])
    from_z = lax.ppermute(own, "expert", pair)
    from_core = lax.ppermute(own, "expert", core)
    gate, up = call(pair_first_kernel, partial_sums, own, from_core, gate_w, up_w)
    from_diag = lax.ppermute(from_z, "expert", core)
    act, give = call(pair_act_kernel, activated, from_z, from_diag, gate, up, gate_w, up_w, down_w)
    second = over_dp(packed[1])
    got = lax.ppermute(give, "expert", core)
    value = call(half_down_kernel, bf16(rows, half), act, down_w, got)
    second, value = lax.optimization_barrier((second, value))
    whole = over_dp(value)

    other = lax.ppermute(second, "expert", core)
    gate, up = call(half_first_kernel, partial_sums, second, gate_w, up_w)
    act, give = call(half_act_kernel, activated, other, gate, up, gate_w, up_w, down_w)
    got = lax.ppermute(give, "expert", core)
    mine, send = call(pair_down_kernel, [f32(rows, part), bf16(rows, part)], act, down_w, got)
    value = call(add_kernel, bf16(rows, part), mine, lax.ppermute(send, "expert", pair))
    some = over_dp(value)

    whole = call(weighted_kernel, f32(tok_row, half), weights[0], whole)
    routed = call(combine_kernel, bf16(tok_row, half), weights[1], some, whole)
    shares = over_expert(routed.reshape(col_count, tok_dev, half))
    return call(final_kernel, bf16(tok_dev, width), hidden_in, shares)


def solution(mesh):
    rows = P(("dp", "expert"), None)
    blocks = P(("dp", "expert"), None, None)
    return jax.shard_map(
        body, mesh=mesh, in_specs=(rows, P(), rows, rows, blocks, blocks, blocks), out_specs=rows, check_vma=False
    )
```

time: 194 us -> 167 us (0.86)
  blocking collectives: 111 us -> 69 us
  starting transfers between devices: 22.9 us -> 38.9 us
  local copies, waits for them, and re-layouts: 3.9 us -> 1.18 us
  waiting for transfers between devices: 38.6 us -> 41.2 us
    all_gather x1 -> x0, blocking collectives: 26 us -> none  [body(): row = lax.all_gather(normed, 'expert', axis=0, tiled=True)]
    ppermute x4 -> x7, waiting for transfers between devices: 2.36 us -> 21.8 us  [the longest x1 11.9 us: body(): lax.ppermute(send, 'expert', pair)]
    all_to_all x2 -> x3, waiting for transfers between devices: 36.3 us -> 19.4 us  [over_dp(): lax.all_to_all(x.reshape(dp_count, per, x.shape[1]), 'dp', split_axis=0,...]
    all_to_all x3, blocking collectives: 85.2 us -> 69 us  [the longest x2 41.8 us: over_expert(): return lax.all_to_all(x, 'expert', split_axis=0, concat_axis=0, tiled=True)]
    ppermute x4 -> x7, starting transfers between devices: 12.1 us -> 20.9 us  [the longest x1 4.93 us: body(): other = lax.ppermute(second, 'expert', core)]
    all_to_all x2 -> x3, starting transfers between devices: 10.8 us -> 17.9 us  [over_dp(): lax.all_to_all(x.reshape(dp_count, per, x.shape[1]), 'dp', split_axis=0,...]
    unnamed x19 -> x14, local copies, waits for them, and re-layouts: 3.08 us -> 1.01 us
    pallas_call x8 -> x13, Pallas kernels: 14.7 us -> 15.5 us  [the longest x12 13.9 us: call(): pl.pallas_call(kernel, out_shape=out_shape, in_specs=[VMEM] * len(args),...]
  transfers between devices with their start and end apart: 6 -> 10, of which waited for: 3 -> 7; matrix products, arithmetic and copies ran while one was open for 0% -> 0% of each run, Pallas kernels for 6% -> 7%
where the time goes in v2:
time: 167 us; the launch traced here: 166 us
  blocking collectives  69 us (41%)
  waiting for transfers between devices  41.2 us (25%)
  starting transfers between devices  38.9 us (23%)
  Pallas kernels  15.5 us (9%)
    all_to_all x2, blocking collectives, over_expert(): return lax.all_to_all(x, 'expert', split_axis=0, concat_axis=0, tiled=True)  41.8 us
    all_to_all x1, blocking collectives, over_dp(): lax.all_to_all(x.reshape(dp_count, per, x.shape[1]), 'dp', split_axis=0,...  27.2 us
    all_to_all x3, waiting for transfers between devices, over_dp(): lax.all_to_all(x.reshape(dp_count, per, x.shape[1]), 'dp', split_axis=0,...  19.4 us
    all_to_all x3, starting transfers between devices, over_dp(): lax.all_to_all(x.reshape(dp_count, per, x.shape[1]), 'dp', split_axis=0,...  17.9 us
    pallas_call x12, Pallas kernels, call(): pl.pallas_call(kernel, out_shape=out_shape, in_specs=[VMEM] * len(args),...  13.9 us
    ppermute x1, waiting for transfers between devices, body(): lax.ppermute(send, 'expert', pair)  11.9 us
    ppermute x1, waiting for transfers between devices, body(): from_z = lax.ppermute(own, 'expert', pair)  5.08 us
    ppermute x1, starting transfers between devices, body(): other = lax.ppermute(second, 'expert', core)  4.93 us
  transfers between devices with their start and end apart: 10, of which 7 were waited for; matrix products, arithmetic and copies ran while one was open for 0% of the time, Pallas kernels for 7%

profile of v2, /device:TPU:1, one launch (start us, length us, event | category | flops | bytes accessed | tf_op | source)
XLA Modules:
  0.0 166.1 jit_solution(10707603641333968223)
XLA Ops:
  1.7 23.9 %all_to_all.30 = bf16[16,4,2176]{2,1,0:T(4,128)(2,1)S(1)} all-to-all(bf16[16,4,2176]{2,1,0:T(4,128)(2,1)} %shard_map.73), channel_id=1, replica_groups=mesh['dp'=32,'expert'=16] {'expert'}, dimensions={0} | all-to-all | bytes 557056 | tf_op jit(solution)/shard_map/all_to_all | solution.py:234
  26.6 27.2 %all_to_all.31 = bf16[32,8,1024]{2,1,0:T(8,128)(2,1)} all-to-all(bf16[32,8,1024]{2,1,0:T(8,128)(2,1)S(1)} %bitcast.26), channel_id=1, replica_groups=mesh['dp'=32,'expert'=16] {'dp'}, dimensions={0} | all-to-all | bytes 1048576 | tf_op jit(solution)/shard_map/all_to_all | solution.py:230
  53.8 1.9 %collective-permute-start = (bf16[256,1024]{1,0:T(8,128)(2,1)}, bf16[256,1024]{1,0:T(8,128)(2,1)}, u32[]{:S(2)}, u32[]{:S(2)}) collective-permute-start(bf16[256,1024]{1,0:T(8,128)(2,1)} %bitcast.3.own_ref), channel_id=1, source_target_pairs={{0,2},{1,3},{2,0},{3,1},{4,6},{5,7},{6,4},{7,5},{8,10},{9,11},{10,... | collective-permute-start | bytes 1572872 | tf_op jit(solution)/shard_map/ppermute | solution.py:255
  55.7 5.0 %all-to-all-start.1 = ((bf16[32,8,2048]{2,1,0:T(8,128)(2,1)}), bf16[32,8,2048]{2,1,0:T(8,128)(2,1)}, u32[]{:S(2)}, u32[]{:S(2)}) async-start(bf16[32,8,2048]{2,1,0:T(8,128)(2,1)} %bitcast.25), calls=%async_computation.1 | async-start | bytes 2097152 | tf_op jit(solution)/shard_map/all_to_all | solution.py:230
  60.7 3.1 %collective-permute-start.2 = (bf16[256,1024]{1,0:T(8,128)(2,1)}, bf16[256,1024]{1,0:T(8,128)(2,1)S(1)}, u32[]{:S(2)}, u32[]{:S(2)}) collective-permute-start(bf16[256,1024]{1,0:T(8,128)(2,1)} %bitcast.3.own_ref), channel_id=1, source_target_pairs={{0,1},{1,0},{2,3},{3,2},{4,5},{5,4},{6,7},{7,6},{8,9},{9,8},{10,11... | collective-permute-start | bytes 1572872 | tf_op jit(solution)/shard_map/ppermute | solution.py:256
  63.8 5.1 %collective-permute-done.z_ref = bf16[256,1024]{1,0:T(8,128)(2,1)} collective-permute-done((bf16[256,1024]{1,0:T(8,128)(2,1)}, bf16[256,1024]{1,0:T(8,128)(2,1)}, u32[]{:S(2)}, u32[]{:S(2)}) %collective-permute-start) | collective-permute-done | bytes 524320 | tf_op jit(solution)/shard_map/ppermute | solution.py:255
  68.8 3.4 %collective-permute-start.1 = (bf16[256,1024]{1,0:T(8,128)(2,1)}, bf16[256,1024]{1,0:T(8,128)(2,1)S(1)}, u32[]{:S(2)}, u32[]{:S(2)}) collective-permute-start(bf16[256,1024]{1,0:T(8,128)(2,1)} %collective-permute-done.z_ref), channel_id=1, source_target_pairs={{0,1},{1,0},{2,3},{3,2},{4,5},{5,4},{6,7},{7,6},{8,9},{9,8},{10,11... | collective-permute-start | bytes 1572872 | tf_op jit(solution)/shard_map/ppermute | solution.py:258
  72.2 1.9 %shard_map.76 = (f32[256,192]{1,0:T(8,128)S(1)}, f32[256,192]{1,0:T(8,128)S(1)}) custom-call(bf16[256,1024]{1,0:T(8,128)(2,1)} %bitcast.3.own_ref, bf16[256,1024]{1,0:T(8,128)(2,1)S(1)} %collective-permute-done.2.core_ref, bf16[192,4096]{1,0:T(8,128)(2,1)S(1)} %bitcast.11, bf16[192,4096]{1,0:T(8,128)(2,1)S(1)} %bitcast.15), custom_call_target="tpu_custom_call" | custom-call | tf_op jit(solution)/shard_map/pallas_call | solution.py:197
  74.2 2.2 %shard_map.77 = (bf16[256,192]{1,0:T(8,128)(2,1)S(1)}, bf16[256,2048]{1,0:T(8,128)(2,1)S(1)}) custom-call(bf16[256,1024]{1,0:T(8,128)(2,1)} %collective-permute-done.z_ref, bf16[256,1024]{1,0:T(8,128)(2,1)S(1)} %collective-permute-done.1.diag_ref, f32[256,192]{1,0:T(8,128)S(1)} %get-tuple-element.24.gate_in, f32[256,192]{1,0:T(8,128)S(1)} %get-tuple-element.25.up_in, ...), custom_call_target="tpu_custom_call" | custom-call | tf_op jit(solution)/shard_map/pallas_call | solution.py:197
  76.3 2.1 %collective-permute-start.3 = (bf16[256,2048]{1,0:T(8,128)(2,1)S(1)}, bf16[256,2048]{1,0:T(8,128)(2,1)S(1)}, u32[]{:S(2)}, u32[]{:S(2)}) collective-permute-start(bf16[256,2048]{1,0:T(8,128)(2,1)S(1)} %get-tuple-element.27), channel_id=1, source_target_pairs={{0,1},{1,0},{2,3},{3,2},{4,5},{5,4},{6,7},{7,6},{8,9},{9,8},{10,11... | collective-permute-start | bytes 3145736 | tf_op jit(solution)/shard_map/ppermute | solution.py:261
  78.4 2.5 %collective-permute-done.3.got_ref = bf16[256,2048]{1,0:T(8,128)(2,1)S(1)} collective-permute-done((bf16[256,2048]{1,0:T(8,128)(2,1)S(1)}, bf16[256,2048]{1,0:T(8,128)(2,1)S(1)}, u32[]{:S(2)}, u32[]{:S(2)}) %collective-permute-start.3) | collective-permute-done | bytes 1048608 | tf_op jit(solution)/shard_map/ppermute | solution.py:261
  82.3 4.3 %all-to-all-done.1 = bf16[32,8,2048]{2,1,0:T(8,128)(2,1)} async-done(((bf16[32,8,2048]{2,1,0:T(8,128)(2,1)}), bf16[32,8,2048]{2,1,0:T(8,128)(2,1)}, u32[]{:S(2)}, u32[]{:S(2)}) %all-to-all-start.1) | async-done | bytes 1048608 | tf_op jit(solution)/shard_map/all_to_all | solution.py:230
  86.6 4.9 %collective-permute-start.4 = (bf16[256,2048]{1,0:T(8,128)(2,1)}, bf16[256,2048]{1,0:T(8,128)(2,1)}, u32[]{:S(2)}, u32[]{:S(2)}) collective-permute-start(bf16[256,2048]{1,0:T(8,128)(2,1)} %bitcast.1.own_ref), channel_id=1, source_target_pairs={{0,1},{1,0},{2,3},{3,2},{4,5},{5,4},{6,7},{7,6},{8,9},{9,8},{10,11... | collective-permute-start | bytes 3145736 | tf_op jit(solution)/shard_map/ppermute | solution.py:266
  91.5 5.4 %all-to-all-start.4 = ((bf16[32,8,2048]{2,1,0:T(8,128)(2,1)}), bf16[32,8,2048]{2,1,0:T(8,128)(2,1)}, u32[]{:S(2)}, u32[]{:S(2)}) async-start(bf16[32,8,2048]{2,1,0:T(8,128)(2,1)} %bitcast.23), calls=%async_computation.4 | async-start | bytes 2097152 | tf_op jit(solution)/shard_map/all_to_all | solution.py:230
  97.0 2.1 %shard_map.79 = (f32[256,192]{1,0:T(8,128)S(1)}, f32[256,192]{1,0:T(8,128)S(1)}) custom-call(bf16[256,2048]{1,0:T(8,128)(2,1)} %bitcast.1.own_ref, bf16[192,4096]{1,0:T(8,128)(2,1)S(1)} %bitcast.13, bf16[192,4096]{1,0:T(8,128)(2,1)S(1)} %bitcast.17), custom_call_target="tpu_custom_call" | custom-call | tf_op jit(solution)/shard_map/pallas_call | solution.py:197
  99.1 2.3 %shard_map.80 = (bf16[256,192]{1,0:T(8,128)(2,1)S(1)}, bf16[256,2048]{1,0:T(8,128)(2,1)S(1)}) custom-call(bf16[256,2048]{1,0:T(8,128)(2,1)} %collective-permute-done.4.other_ref, f32[256,192]{1,0:T(8,128)S(1)} %get-tuple-element.29.gate_in, f32[256,192]{1,0:T(8,128)S(1)} %get-tuple-element.30.up_in, bf16[192,4096]{1,0:T(8,128)(2,1)S(1)} %bitcast.14, ...), custom_call_target="tpu_custom_call" | custom-call | tf_op jit(solution)/shard_map/pallas_call | solution.py:197
  101.4 2.2 %collective-permute-start.5 = (bf16[256,2048]{1,0:T(8,128)(2,1)S(1)}, bf16[256,2048]{1,0:T(8,128)(2,1)S(1)}, u32[]{:S(2)}, u32[]{:S(2)}) collective-permute-start(bf16[256,2048]{1,0:T(8,128)(2,1)S(1)} %get-tuple-element.32), channel_id=1, source_target_pairs={{0,1},{1,0},{2,3},{3,2},{4,5},{5,4},{6,7},{7,6},{8,9},{9,8},{10,11... | collective-permute-start | bytes 3145736 | tf_op jit(solution)/shard_map/ppermute | solution.py:269
  103.6 2.3 %collective-permute-done.5.got_ref = bf16[256,2048]{1,0:T(8,128)(2,1)S(1)} collective-permute-done((bf16[256,2048]{1,0:T(8,128)(2,1)S(1)}, bf16[256,2048]{1,0:T(8,128)(2,1)S(1)}, u32[]{:S(2)}, u32[]{:S(2)}) %collective-permute-start.5) | collective-permute-done | bytes 1048608 | tf_op jit(solution)/shard_map/ppermute | solution.py:269
  106.4 3.4 %collective-permute-start.6 = (bf16[256,1024]{1,0:T(8,128)(2,1)S(1)}, bf16[256,1024]{1,0:T(8,128)(2,1)S(1)}, u32[]{:S(2)}, u32[]{:S(2)}) collective-permute-start(bf16[256,1024]{1,0:T(8,128)(2,1)S(1)} %get-tuple-element.34), channel_id=1, source_target_pairs={{0,2},{1,3},{2,0},{3,1},{4,6},{5,7},{6,4},{7,5},{8,10},{9,11},{10,... | collective-permute-start | bytes 1572872 | tf_op jit(solution)/shard_map/ppermute | solution.py:271
  109.8 11.9 %collective-permute-done.6.got_ref = bf16[256,1024]{1,0:T(8,128)(2,1)S(1)} collective-permute-done((bf16[256,1024]{1,0:T(8,128)(2,1)S(1)}, bf16[256,1024]{1,0:T(8,128)(2,1)S(1)}, u32[]{:S(2)}, u32[]{:S(2)}) %collective-permute-start.6) | collective-permute-done | bytes 524320 | tf_op jit(solution)/shard_map/ppermute | solution.py:271
  122.5 1.7 %all-to-all-done.4 = bf16[32,8,2048]{2,1,0:T(8,128)(2,1)} async-done(((bf16[32,8,2048]{2,1,0:T(8,128)(2,1)}), bf16[32,8,2048]{2,1,0:T(8,128)(2,1)}, u32[]{:S(2)}, u32[]{:S(2)}) %all-to-all-start.4) | async-done | bytes 1048608 | tf_op jit(solution)/shard_map/all_to_all | solution.py:230
  124.2 7.5 %all-to-all-start.3 = ((bf16[32,8,1024]{2,1,0:T(8,128)(2,1)}), bf16[32,8,1024]{2,1,0:T(8,128)(2,1)S(1)}, u32[]{:S(2)}, u32[]{:S(2)}) async-start(bf16[32,8,1024]{2,1,0:T(8,128)(2,1)} %bitcast.7), calls=%async_computation.3 | async-start | bytes 1048576 | tf_op jit(solution)/shard_map/all_to_all | solution.py:230
  133.7 13.4 %all-to-all-done.3 = bf16[32,8,1024]{2,1,0:T(8,128)(2,1)S(1)} async-done(((bf16[32,8,1024]{2,1,0:T(8,128)(2,1)}), bf16[32,8,1024]{2,1,0:T(8,128)(2,1)S(1)}, u32[]{:S(2)}, u32[]{:S(2)}) %all-to-all-start.3) | async-done | bytes 524320 | tf_op jit(solution)/shard_map/all_to_all | solution.py:230
  147.4 18.0 %all_to_all.32.got_ref = bf16[16,4,2048]{2,1,0:T(4,128)(2,1)S(1)} all-to-all(bf16[16,4,2048]{2,1,0:T(4,128)(2,1)S(1)} %reshape.51), channel_id=1, replica_groups=mesh['dp'=32,'expert'=16] {'expert'}, dimensions={0} | all-to-all | bytes 524288 | tf_op jit(solution)/shard_map/all_to_all | solution.py:234
  (28 shorter events, 8.3 us)
Async XLA Ops:
  26.5 29.1 %copy-start.5 = (bf16[256,2048]{1,0:T(8,128)(2,1)}, bf16[256,2048]{1,0:T(8,128)(2,1)S(1)}, u32[]{:S(2)}) copy-start(bf16[256,2048]{1,0:T(8,128)(2,1)S(1)} %get-tuple-element.22) | copy-start | bytes 3145732
  26.6 45.7 %copy-start = (bf16[1,192,4096]{2,1,0:T(8,128)(2,1)S(1)}, bf16[1,192,4096]{2,1,0:T(8,128)(2,1)}, u32[]{:S(2)}) copy-start(bf16[1,192,4096]{2,1,0:T(8,128)(2,1)} %param.11) | copy-start | bytes 4718596
  26.6 45.7 %copy-start.1 = (bf16[1,192,4096]{2,1,0:T(8,128)(2,1)S(1)}, bf16[1,192,4096]{2,1,0:T(8,128)(2,1)}, u32[]{:S(2)}) copy-start(bf16[1,192,4096]{2,1,0:T(8,128)(2,1)} %param.12) | copy-start | bytes 4718596
  53.8 15.1 %collective-permute-start = (bf16[256,1024]{1,0:T(8,128)(2,1)}, bf16[256,1024]{1,0:T(8,128)(2,1)}, u32[]{:S(2)}, u32[]{:S(2)}) collective-permute-start(bf16[256,1024]{1,0:T(8,128)(2,1)} %bitcast.3.own_ref), channel_id=1, source_target_pairs={{0,2},{1,3},{2,0},{3,1},{4,6},{5,7},{6,4},{7,5},{8,10},{9,11},{10,... | collective-permute-start | bytes 1572872 | tf_op jit(solution)/shard_map/ppermute | solution.py:255
  55.7 30.9 %all-to-all-start.1 = ((bf16[32,8,2048]{2,1,0:T(8,128)(2,1)}), bf16[32,8,2048]{2,1,0:T(8,128)(2,1)}, u32[]{:S(2)}, u32[]{:S(2)}) async-start(bf16[32,8,2048]{2,1,0:T(8,128)(2,1)} %bitcast.25), calls=%async_computation.1 | async-start | bytes 2097152 | tf_op jit(solution)/shard_map/all_to_all | solution.py:230
  60.7 11.6 %collective-permute-start.2 = (bf16[256,1024]{1,0:T(8,128)(2,1)}, bf16[256,1024]{1,0:T(8,128)(2,1)S(1)}, u32[]{:S(2)}, u32[]{:S(2)}) collective-permute-start(bf16[256,1024]{1,0:T(8,128)(2,1)} %bitcast.3.own_ref), channel_id=1, source_target_pairs={{0,1},{1,0},{2,3},{3,2},{4,5},{5,4},{6,7},{7,6},{8,9},{9,8},{10,11... | collective-permute-start | bytes 1572872 | tf_op jit(solution)/shard_map/ppermute | solution.py:256
  68.8 5.3 %collective-permute-start.1 = (bf16[256,1024]{1,0:T(8,128)(2,1)}, bf16[256,1024]{1,0:T(8,128)(2,1)S(1)}, u32[]{:S(2)}, u32[]{:S(2)}) collective-permute-start(bf16[256,1024]{1,0:T(8,128)(2,1)} %collective-permute-done.z_ref), channel_id=1, source_target_pairs={{0,1},{1,0},{2,3},{3,2},{4,5},{5,4},{6,7},{7,6},{8,9},{9,8},{10,11... | collective-permute-start | bytes 1572872 | tf_op jit(solution)/shard_map/ppermute | solution.py:258
  72.2 1.9 %copy-start.2 = (bf16[1,192,4096]{2,1,0:T(8,128)(2,1)S(1)}, bf16[1,192,4096]{2,1,0:T(8,128)(2,1)}, u32[]{:S(2)}) copy-start(bf16[1,192,4096]{2,1,0:T(8,128)(2,1)} %param.13) | copy-start | bytes 4718596
  76.3 4.6 %collective-permute-start.3 = (bf16[256,2048]{1,0:T(8,128)(2,1)S(1)}, bf16[256,2048]{1,0:T(8,128)(2,1)S(1)}, u32[]{:S(2)}, u32[]{:S(2)}) collective-permute-start(bf16[256,2048]{1,0:T(8,128)(2,1)S(1)} %get-tuple-element.27), channel_id=1, source_target_pairs={{0,1},{1,0},{2,3},{3,2},{4,5},{5,4},{6,7},{7,6},{8,9},{9,8},{10,11... | collective-permute-start | bytes 3145736 | tf_op jit(solution)/shard_map/ppermute | solution.py:261
  81.3 1.0 copy-start.4
  86.6 12.5 %collective-permute-start.4 = (bf16[256,2048]{1,0:T(8,128)(2,1)}, bf16[256,2048]{1,0:T(8,128)(2,1)}, u32[]{:S(2)}, u32[]{:S(2)}) collective-permute-start(bf16[256,2048]{1,0:T(8,128)(2,1)} %bitcast.1.own_ref), channel_id=1, source_target_pairs={{0,1},{1,0},{2,3},{3,2},{4,5},{5,4},{6,7},{7,6},{8,9},{9,8},{10,11... | collective-permute-start | bytes 3145736 | tf_op jit(solution)/shard_map/ppermute | solution.py:266
  91.5 32.7 %all-to-all-start.4 = ((bf16[32,8,2048]{2,1,0:T(8,128)(2,1)}), bf16[32,8,2048]{2,1,0:T(8,128)(2,1)}, u32[]{:S(2)}, u32[]{:S(2)}) async-start(bf16[32,8,2048]{2,1,0:T(8,128)(2,1)} %bitcast.23), calls=%async_computation.4 | async-start | bytes 2097152 | tf_op jit(solution)/shard_map/all_to_all | solution.py:230
  97.0 2.1 %copy-start.3 = (bf16[1,192,4096]{2,1,0:T(8,128)(2,1)S(1)}, bf16[1,192,4096]{2,1,0:T(8,128)(2,1)}, u32[]{:S(2)}) copy-start(bf16[1,192,4096]{2,1,0:T(8,128)(2,1)} %param.13) | copy-start | bytes 4718596
  101.4 4.6 %collective-permute-start.5 = (bf16[256,2048]{1,0:T(8,128)(2,1)S(1)}, bf16[256,2048]{1,0:T(8,128)(2,1)S(1)}, u32[]{:S(2)}, u32[]{:S(2)}) collective-permute-start(bf16[256,2048]{1,0:T(8,128)(2,1)S(1)} %get-tuple-element.32), channel_id=1, source_target_pairs={{0,1},{1,0},{2,3},{3,2},{4,5},{5,4},{6,7},{7,6},{8,9},{9,8},{10,11... | collective-permute-start | bytes 3145736 | tf_op jit(solution)/shard_map/ppermute | solution.py:269
  106.4 15.2 %collective-permute-start.6 = (bf16[256,1024]{1,0:T(8,128)(2,1)S(1)}, bf16[256,1024]{1,0:T(8,128)(2,1)S(1)}, u32[]{:S(2)}, u32[]{:S(2)}) collective-permute-start(bf16[256,1024]{1,0:T(8,128)(2,1)S(1)} %get-tuple-element.34), channel_id=1, source_target_pairs={{0,2},{1,3},{2,0},{3,1},{4,6},{5,7},{6,4},{7,5},{8,10},{9,11},{10,... | collective-permute-start | bytes 1572872 | tf_op jit(solution)/shard_map/ppermute | solution.py:271
  124.2 22.9 %all-to-all-start.3 = ((bf16[32,8,1024]{2,1,0:T(8,128)(2,1)}), bf16[32,8,1024]{2,1,0:T(8,128)(2,1)S(1)}, u32[]{:S(2)}, u32[]{:S(2)}) async-start(bf16[32,8,1024]{2,1,0:T(8,128)(2,1)} %bitcast.7), calls=%async_computation.3 | async-start | bytes 1048576 | tf_op jit(solution)/shard_map/all_to_all | solution.py:230
  133.7 31.7 %copy-start.6 = (bf16[4,4096]{1,0:T(4,128)(2,1)S(1)}, bf16[4,4096]{1,0:T(4,128)(2,1)}, u32[]{:S(2)}) copy-start(bf16[4,4096]{1,0:T(4,128)(2,1)} %resid_ref.1) | copy-start | bytes 98308

commit v3 on v2

--- a/solution.py
+++ b/solution.py
@@ -35,7 +35,7 @@
         copy.start()
     for copy in copies:
         copy.wait()
-    part = x_ref.shape[1] // 2
+    part = x_ref.shape[1] // 4
     x = x_ref[...].astype(jnp.float32)
     inv = lax.rsqrt(jnp.mean(x * x, axis=1, keepdims=True) + 1e-06)
     normed = (x * inv * gain_ref[...].astype(jnp.float32)[None, :]).astype(jnp.bfloat16)
@@ -48,8 +48,8 @@
         meta = jnp.where(lane == TOP + k, share[:, k : k + 1], meta)
     meta = meta.astype(jnp.bfloat16)
     for j in range(out_ref.shape[0]):
-        half = j % 2
-        out_ref[j, :, :part] = normed[:, half * part : (half + 1) * part]
+        q = 2 * (j % 2) + (j // 2) % 2
+        out_ref[j, :, :part] = normed[:, q * part : (q + 1) * part]
         out_ref[j, :, part:] = meta
 
 
@@ -77,19 +77,25 @@
     return (expert == 2 * (slot // per) + lax.axis_index("expert") // 8).astype(jnp.bfloat16)
 
 
-def pack_kernel(row_ref, quarter_ref, half_ref):
-    tokens, (rows, part) = row_ref.shape[0], quarter_ref.shape
-    width = half_ref.shape[1]
+def pack_kernel(row_ref, early_ref, late_ref, quarter_ref):
+    tokens, (rows, part) = row_ref.shape[0], early_ref.shape
     per = rows // (EXPERTS // 2)
-    _, b = place()
-    rank, _ = ranks(row_ref[:, width:])
+    rank, _ = ranks(row_ref[:, part:])
     rank_of = dot_nt(picks(rows), rank)
     slot = (lax.broadcasted_iota(jnp.int32, (rows, tokens), 0) % per).astype(jnp.float32)
-    early = (rank_of == slot).astype(jnp.bfloat16)
-    late = (rank_of == slot + float(per)).astype(jnp.bfloat16)
-    quarter = row_ref[:, pl.ds(pl.multiple_of(b * part, part), part)]
-    half_ref[...] = dot_nn(late, row_ref[:, :width]).astype(jnp.bfloat16)
-    quarter_ref[...] = dot_nn(early, quarter).astype(jnp.bfloat16)
+    quarter_ref[...] = row_ref[:, :part]
+    early_ref[...] = dot_nn((rank_of == slot).astype(jnp.bfloat16), row_ref[:, :part]).astype(jnp.bfloat16)
+    late_ref[...] = (rank_of == slot + float(per)).astype(jnp.bfloat16)
+
+
+def late_kernel(late_ref, row_ref, other_ref, out_ref):
+    part = other_ref.shape[1]
+    _, b = place()
+    late = late_ref[...]
+    own = pl.ds(pl.multiple_of(b * part, part), part)
+    other = pl.ds(pl.multiple_of((1 - b) * part, part), part)
+    out_ref[:, own] = dot_nn(late, row_ref[:, :part]).astype(jnp.bfloat16)
+    out_ref[:, other] = dot_nn(late, other_ref[...]).astype(jnp.bfloat16)
 
 
 def weigh_kernel(row_ref, *outs):
@@ -171,24 +177,24 @@
     out_ref[...] = (mine_ref[...] + got_ref[...].astype(jnp.float32)).astype(jnp.bfloat16)
 
 
-def weighted_kernel(weight_ref, in_ref, out_ref):
-    out_ref[...] = dot_nn(weight_ref[...], in_ref[...])
-
-
-def combine_kernel(weight_ref, in_ref, whole_ref, out_ref):
+def weighted_kernel(weight_ref, in_ref, mine_ref, send_ref):
     _, b = place()
-    part = in_ref.shape[1]
-    some = dot_nn(weight_ref[...], in_ref[...])
-    out_ref[:, :part] = (whole_ref[:, :part] + jnp.where(b == 0, some, 0.0)).astype(jnp.bfloat16)
-    out_ref[:, part:] = (whole_ref[:, part:] + jnp.where(b == 0, 0.0, some)).astype(jnp.bfloat16)
+    weight = weight_ref[...]
+    mine_ref[...] = dot_nn(weight, columns(in_ref, b, 2))
+    send_ref[...] = dot_nn(weight, columns(in_ref, 1 - b, 2)).astype(jnp.bfloat16)
+
+
+def combine_kernel(weight_ref, in_ref, mine_ref, got_ref, out_ref):
+    total = dot_nn(weight_ref[...], in_ref[...]) + mine_ref[...] + got_ref[...].astype(jnp.float32)
+    out_ref[...] = total.astype(jnp.bfloat16)
 
 
 def final_kernel(resid_ref, got_ref, out_ref):
     part = got_ref.shape[2]
-    for c in range(2):
-        cols = slice(c * part, (c + 1) * part)
+    for q in range(4):
+        cols = slice(q * part, (q + 1) * part)
         total = resid_ref[:, cols].astype(jnp.float32)
-        for j in range(c, got_ref.shape[0], 2):
+        for j in range(2 * (q % 2) + q // 2, got_ref.shape[0], 4):
             total = total + got_ref[j].astype(jnp.float32)
         out_ref[:, cols] = total.astype(jnp.bfloat16)
 
@@ -235,7 +241,7 @@
 
     normed = pl.pallas_call(
         norm_kernel,
-        out_shape=bf16(col_count, tok_dev, half + META),
+        out_shape=bf16(col_count, tok_dev, part + META),
         in_specs=[HBM] * 4,
         out_specs=VMEM,
         scratch_shapes=[
@@ -247,11 +253,13 @@
         ],
         compiler_params=WHOLE,
     )(hidden_in, norm_gain, expert_ids, gate_share)
-    row = over_expert(normed).reshape(tok_row, half + META)
-    packed = call(pack_kernel, [bf16(rows, part), bf16(rows, half)], row)
+    row = over_expert(normed).reshape(tok_row, part + META)
+    early, late, quarter = call(pack_kernel, [bf16(rows, part), bf16(rows, tok_row), bf16(tok_row, part)], row)
+    other = lax.ppermute(quarter, "expert", pair)
+    packed = [early, call(late_kernel, bf16(rows, half), late, row, other)]
     weights = call(weigh_kernel, [bf16(tok_row, rows)] * CHUNKS, row)
 
-    own = over_dp(packed[0])
+    own, packed[1] = lax.optimization_barrier((over_dp(packed[0]), packed[1]))
     from_z = lax.ppermute(own, "expert", pair)
     from_core = lax.ppermute(own, "expert", core)
     gate, up = call(pair_first_kernel, partial_sums, own, from_core, gate_w, up_w)
@@ -271,9 +279,10 @@
     value = call(add_kernel, bf16(rows, part), mine, lax.ppermute(send, "expert", pair))
     some = over_dp(value)
 
-    whole = call(weighted_kernel, f32(tok_row, half), weights[0], whole)
-    routed = call(combine_kernel, bf16(tok_row, half), weights[1], some, whole)
-    shares = over_expert(routed.reshape(col_count, tok_dev, half))
+    mine, send = call(weighted_kernel, [f32(tok_row, part), bf16(tok_row, part)], weights[0], whole)
+    got = lax.ppermute(send, "expert", pair)
+    routed = call(combine_kernel, bf16(tok_row, part), weights[1], some, mine, got)
+    shares = over_expert(routed.reshape(col_count, tok_dev, part))
     return call(final_kernel, bf16(tok_dev, width), hidden_in, shares)
 
 

time: 167 us -> 162 us (0.970)
  blocking collectives: 69 us -> 36.4 us
  starting transfers between devices: 38.9 us -> 55.2 us
  waiting for transfers between devices: 41.2 us -> 50.4 us
    all_to_all x1 -> x0, blocking collectives: 27.2 us -> none  [over_dp(): lax.all_to_all(x.reshape(dp_count, per, x.shape[1]), 'dp', split_axis=0,...]
    all_to_all x3 -> x4, starting transfers between devices: 17.9 us -> 27.7 us  [over_dp(): lax.all_to_all(x.reshape(dp_count, per, x.shape[1]), 'dp', split_axis=0,...]
    ppermute x0 -> x2, waiting for transfers between devices: none -> 7.79 us  [the longest x1 5 us: body(): other = lax.ppermute(quarter, 'expert', pair)]
    all_to_all x2, blocking collectives: 41.8 us -> 36.4 us  [over_expert(): return lax.all_to_all(x, 'expert', split_axis=0, concat_axis=0, tiled=True)]
    ppermute x0 -> x2, starting transfers between devices: none -> 5.28 us  [the longest x1 3.21 us: body(): got = lax.ppermute(send, 'expert', pair)]
    all_to_all x3 -> x4, waiting for transfers between devices: 19.4 us -> 21.7 us  [over_dp(): lax.all_to_all(x.reshape(dp_count, per, x.shape[1]), 'dp', split_axis=0,...]
    pallas_call x12 -> x13, Pallas kernels: 13.9 us -> 14.8 us  [call(): pl.pallas_call(kernel, out_shape=out_shape, in_specs=[VMEM] * len(args),...]
  transfers between devices with their start and end apart: 10 -> 13, of which waited for: 7 -> 10; matrix products, arithmetic and copies ran while one was open for 0% -> 0% of each run, Pallas kernels for 7% -> 8%
where the time goes in v3:
time: 162 us; the launch traced here: 161 us
  starting transfers between devices  55.2 us (34%)
  waiting for transfers between devices  50.4 us (31%)
  blocking collectives  36.4 us (22%)
  Pallas kernels  16.4 us (10%)
  local copies, waits for them, and re-layouts  2.07 us (1%)
    all_to_all x2, blocking collectives, over_expert(): return lax.all_to_all(x, 'expert', split_axis=0, concat_axis=0, tiled=True)  36.4 us
    all_to_all x4, starting transfers between devices, over_dp(): lax.all_to_all(x.reshape(dp_count, per, x.shape[1]), 'dp', split_axis=0,...  27.7 us
    all_to_all x4, waiting for transfers between devices, over_dp(): lax.all_to_all(x.reshape(dp_count, per, x.shape[1]), 'dp', split_axis=0,...  21.7 us
    pallas_call x13, Pallas kernels, call(): pl.pallas_call(kernel, out_shape=out_shape, in_specs=[VMEM] * len(args),...  14.8 us
    ppermute x1, waiting for transfers between devices, body(): lax.ppermute(send, 'expert', pair)  12 us
    ppermute x1, starting transfers between devices, body(): other = lax.ppermute(second, 'expert', core)  5.27 us
    ppermute x1, waiting for transfers between devices, body(): other = lax.ppermute(quarter, 'expert', pair)  5 us
    ppermute x2, waiting for transfers between devices, body(): got = lax.ppermute(give, 'expert', core)  4.84 us
  transfers between devices with their start and end apart: 13, of which 10 were waited for; matrix products, arithmetic and copies ran while one was open for 0% of the time, Pallas kernels for 8%

profile of v3, /device:TPU:1, one launch (start us, length us, event | category | flops | bytes accessed | tf_op | source)
XLA Modules:
  0.0 160.8 jit_solution(10235298332088542596)
XLA Ops:
  1.6 21.2 %all_to_all.30 = bf16[16,4,1152]{2,1,0:T(4,128)(2,1)S(1)} all-to-all(bf16[16,4,1152]{2,1,0:T(4,128)(2,1)} %shard_map.73), channel_id=1, replica_groups=mesh['dp'=32,'expert'=16] {'expert'}, dimensions={0} | all-to-all | bytes 294912 | tf_op jit(solution)/shard_map/all_to_all | solution.py:240
  24.3 9.8 %all-to-all-start.1 = ((bf16[32,8,1024]{2,1,0:T(8,128)(2,1)}), bf16[32,8,1024]{2,1,0:T(8,128)(2,1)}, u32[]{:S(2)}, u32[]{:S(2)}) async-start(bf16[32,8,1024]{2,1,0:T(8,128)(2,1)} %bitcast), calls=%async_computation.1 | async-start | bytes 1048576 | tf_op jit(solution)/shard_map/all_to_all | solution.py:236
  34.1 2.1 %collective-permute-start = (bf16[64,1024]{1,0:T(8,128)(2,1)S(1)}, bf16[64,1024]{1,0:T(8,128)(2,1)S(1)}, u32[]{:S(2)}, u32[]{:S(2)}) collective-permute-start(bf16[64,1024]{1,0:T(8,128)(2,1)S(1)} %get-tuple-element.29), channel_id=1, source_target_pairs={{0,2},{1,3},{2,0},{3,1},{4,6},{5,7},{6,4},{7,5},{8,10},{9,11},{10,... | collective-permute-start | bytes 393224 | tf_op jit(solution)/shard_map/ppermute | solution.py:258
  36.2 5.0 %collective-permute-done.other_ref = bf16[64,1024]{1,0:T(8,128)(2,1)S(1)} collective-permute-done((bf16[64,1024]{1,0:T(8,128)(2,1)S(1)}, bf16[64,1024]{1,0:T(8,128)(2,1)S(1)}, u32[]{:S(2)}, u32[]{:S(2)}) %collective-permute-start) | collective-permute-done | bytes 131104 | tf_op jit(solution)/shard_map/ppermute | solution.py:258
  42.6 8.8 %all-to-all-done.1 = bf16[32,8,1024]{2,1,0:T(8,128)(2,1)} async-done(((bf16[32,8,1024]{2,1,0:T(8,128)(2,1)}), bf16[32,8,1024]{2,1,0:T(8,128)(2,1)}, u32[]{:S(2)}, u32[]{:S(2)}) %all-to-all-start.1) | async-done | bytes 524320 | tf_op jit(solution)/shard_map/all_to_all | solution.py:236
  53.3 4.9 %all-to-all-start.2 = ((bf16[32,8,2048]{2,1,0:T(8,128)(2,1)}), bf16[32,8,2048]{2,1,0:T(8,128)(2,1)}, u32[]{:S(2)}, u32[]{:S(2)}) async-start(bf16[32,8,2048]{2,1,0:T(8,128)(2,1)} %bitcast.23), calls=%async_computation.2 | async-start | bytes 2097152 | tf_op jit(solution)/shard_map/all_to_all | solution.py:236
  58.1 3.7 %collective-permute-start.3 = (bf16[256,1024]{1,0:T(8,128)(2,1)}, bf16[256,1024]{1,0:T(8,128)(2,1)S(1)}, u32[]{:S(2)}, u32[]{:S(2)}) collective-permute-start(bf16[256,1024]{1,0:T(8,128)(2,1)} %bitcast.1.own_ref), channel_id=1, source_target_pairs={{0,1},{1,0},{2,3},{3,2},{4,5},{5,4},{6,7},{7,6},{8,9},{9,8},{10,11... | collective-permute-start | bytes 1572872 | tf_op jit(solution)/shard_map/ppermute | solution.py:264
  61.8 4.0 %collective-permute-done.1.z_ref = bf16[256,1024]{1,0:T(8,128)(2,1)} collective-permute-done((bf16[256,1024]{1,0:T(8,128)(2,1)}, bf16[256,1024]{1,0:T(8,128)(2,1)}, u32[]{:S(2)}, u32[]{:S(2)}) %collective-permute-start.1) | collective-permute-done | bytes 524320 | tf_op jit(solution)/shard_map/ppermute | solution.py:263
  65.9 3.9 %collective-permute-start.2 = (bf16[256,1024]{1,0:T(8,128)(2,1)}, bf16[256,1024]{1,0:T(8,128)(2,1)S(1)}, u32[]{:S(2)}, u32[]{:S(2)}) collective-permute-start(bf16[256,1024]{1,0:T(8,128)(2,1)} %collective-permute-done.1.z_ref), channel_id=1, source_target_pairs={{0,1},{1,0},{2,3},{3,2},{4,5},{5,4},{6,7},{7,6},{8,9},{9,8},{10,11... | collective-permute-start | bytes 1572872 | tf_op jit(solution)/shard_map/ppermute | solution.py:266
  71.7 2.1 %shard_map.78 = (bf16[256,192]{1,0:T(8,128)(2,1)S(1)}, bf16[256,2048]{1,0:T(8,128)(2,1)S(1)}) custom-call(bf16[256,1024]{1,0:T(8,128)(2,1)} %collective-permute-done.1.z_ref, bf16[256,1024]{1,0:T(8,128)(2,1)S(1)} %collective-permute-done.2.diag_ref, f32[256,192]{1,0:T(8,128)S(1)} %get-tuple-element.32.gate_in, f32[256,192]{1,0:T(8,128)S(1)} %get-tuple-element.33.up_in, ...), custom_call_target="tpu_custom_call" | custom-call | tf_op jit(solution)/shard_map/pallas_call | solution.py:203
  76.0 2.5 %collective-permute-done.4.got_ref = bf16[256,2048]{1,0:T(8,128)(2,1)S(1)} collective-permute-done((bf16[256,2048]{1,0:T(8,128)(2,1)S(1)}, bf16[256,2048]{1,0:T(8,128)(2,1)S(1)}, u32[]{:S(2)}, u32[]{:S(2)}) %collective-permute-start.4) | collective-permute-done | bytes 1048608 | tf_op jit(solution)/shard_map/ppermute | solution.py:269
  79.9 3.9 %all-to-all-done.2 = bf16[32,8,2048]{2,1,0:T(8,128)(2,1)} async-done(((bf16[32,8,2048]{2,1,0:T(8,128)(2,1)}), bf16[32,8,2048]{2,1,0:T(8,128)(2,1)}, u32[]{:S(2)}, u32[]{:S(2)}) %all-to-all-start.2) | async-done | bytes 1048608 | tf_op jit(solution)/shard_map/all_to_all | solution.py:236
  83.8 5.3 %collective-permute-start.5 = (bf16[256,2048]{1,0:T(8,128)(2,1)}, bf16[256,2048]{1,0:T(8,128)(2,1)}, u32[]{:S(2)}, u32[]{:S(2)}) collective-permute-start(bf16[256,2048]{1,0:T(8,128)(2,1)} %bitcast.3.own_ref), channel_id=1, source_target_pairs={{0,1},{1,0},{2,3},{3,2},{4,5},{5,4},{6,7},{7,6},{8,9},{9,8},{10,11... | collective-permute-start | bytes 3145736 | tf_op jit(solution)/shard_map/ppermute | solution.py:274
  89.0 5.4 %all-to-all-start.4 = ((bf16[32,8,2048]{2,1,0:T(8,128)(2,1)}), bf16[32,8,2048]{2,1,0:T(8,128)(2,1)}, u32[]{:S(2)}, u32[]{:S(2)}) async-start(bf16[32,8,2048]{2,1,0:T(8,128)(2,1)} %bitcast.24), calls=%async_computation.4 | async-start | bytes 2097152 | tf_op jit(solution)/shard_map/all_to_all | solution.py:236
  96.6 2.3 %shard_map.81 = (bf16[256,192]{1,0:T(8,128)(2,1)S(1)}, bf16[256,2048]{1,0:T(8,128)(2,1)S(1)}) custom-call(bf16[256,2048]{1,0:T(8,128)(2,1)} %collective-permute-done.5.other_ref, f32[256,192]{1,0:T(8,128)S(1)} %get-tuple-element.37.gate_in, f32[256,192]{1,0:T(8,128)S(1)} %get-tuple-element.38.up_in, bf16[192,4096]{1,0:T(8,128)(2,1)S(1)} %bitcast.14, ...), custom_call_target="tpu_custom_call" | custom-call | tf_op jit(solution)/shard_map/pallas_call | solution.py:203
  98.9 2.2 %collective-permute-start.6 = (bf16[256,2048]{1,0:T(8,128)(2,1)S(1)}, bf16[256,2048]{1,0:T(8,128)(2,1)S(1)}, u32[]{:S(2)}, u32[]{:S(2)}) collective-permute-start(bf16[256,2048]{1,0:T(8,128)(2,1)S(1)} %get-tuple-element.40), channel_id=1, source_target_pairs={{0,1},{1,0},{2,3},{3,2},{4,5},{5,4},{6,7},{7,6},{8,9},{9,8},{10,11... | collective-permute-start | bytes 3145736 | tf_op jit(solution)/shard_map/ppermute | solution.py:277
  101.1 2.3 %collective-permute-done.6.got_ref = bf16[256,2048]{1,0:T(8,128)(2,1)S(1)} collective-permute-done((bf16[256,2048]{1,0:T(8,128)(2,1)S(1)}, bf16[256,2048]{1,0:T(8,128)(2,1)S(1)}, u32[]{:S(2)}, u32[]{:S(2)}) %collective-permute-start.6) | collective-permute-done | bytes 1048608 | tf_op jit(solution)/shard_map/ppermute | solution.py:277
  103.9 3.2 %collective-permute-start.7 = (bf16[256,1024]{1,0:T(8,128)(2,1)S(1)}, bf16[256,1024]{1,0:T(8,128)(2,1)S(1)}, u32[]{:S(2)}, u32[]{:S(2)}) collective-permute-start(bf16[256,1024]{1,0:T(8,128)(2,1)S(1)} %get-tuple-element.42), channel_id=1, source_target_pairs={{0,2},{1,3},{2,0},{3,1},{4,6},{5,7},{6,4},{7,5},{8,10},{9,11},{10,... | collective-permute-start | bytes 1572872 | tf_op jit(solution)/shard_map/ppermute | solution.py:279
  107.1 12.0 %collective-permute-done.7.got_ref = bf16[256,1024]{1,0:T(8,128)(2,1)S(1)} collective-permute-done((bf16[256,1024]{1,0:T(8,128)(2,1)S(1)}, bf16[256,1024]{1,0:T(8,128)(2,1)S(1)}, u32[]{:S(2)}, u32[]{:S(2)}) %collective-permute-start.7) | collective-permute-done | bytes 524320 | tf_op jit(solution)/shard_map/ppermute | solution.py:279
  121.7 7.6 %all-to-all-start.3 = ((bf16[32,8,1024]{2,1,0:T(8,128)(2,1)}), bf16[32,8,1024]{2,1,0:T(8,128)(2,1)S(1)}, u32[]{:S(2)}, u32[]{:S(2)}) async-start(bf16[32,8,1024]{2,1,0:T(8,128)(2,1)} %bitcast.7), calls=%async_computation.3 | async-start | bytes 1048576 | tf_op jit(solution)/shard_map/all_to_all | solution.py:236
  131.2 3.2 %collective-permute-start.8 = (bf16[64,1024]{1,0:T(8,128)(2,1)S(1)}, bf16[64,1024]{1,0:T(8,128)(2,1)S(1)}, u32[]{:S(2)}, u32[]{:S(2)}) collective-permute-start(bf16[64,1024]{1,0:T(8,128)(2,1)S(1)} %get-tuple-element.46), channel_id=1, source_target_pairs={{0,2},{1,3},{2,0},{3,1},{4,6},{5,7},{6,4},{7,5},{8,10},{9,11},{10,... | collective-permute-start | bytes 393224 | tf_op jit(solution)/shard_map/ppermute | solution.py:283
  134.4 2.8 %collective-permute-done.8.got_ref = bf16[64,1024]{1,0:T(8,128)(2,1)S(1)} collective-permute-done((bf16[64,1024]{1,0:T(8,128)(2,1)S(1)}, bf16[64,1024]{1,0:T(8,128)(2,1)S(1)}, u32[]{:S(2)}, u32[]{:S(2)}) %collective-permute-start.8) | collective-permute-done | bytes 131104 | tf_op jit(solution)/shard_map/ppermute | solution.py:283
  137.2 7.4 %all-to-all-done.3 = bf16[32,8,1024]{2,1,0:T(8,128)(2,1)S(1)} async-done(((bf16[32,8,1024]{2,1,0:T(8,128)(2,1)}), bf16[32,8,1024]{2,1,0:T(8,128)(2,1)S(1)}, u32[]{:S(2)}, u32[]{:S(2)}) %all-to-all-start.3) | async-done | bytes 524320 | tf_op jit(solution)/shard_map/all_to_all | solution.py:236
  144.9 15.3 %all_to_all.31.got_ref = bf16[16,4,1024]{2,1,0:T(4,128)(2,1)S(1)} all-to-all(bf16[16,4,1024]{2,1,0:T(4,128)(2,1)S(1)} %reshape.51), channel_id=1, replica_groups=mesh['dp'=32,'expert'=16] {'expert'}, dimensions={0} | all-to-all | bytes 262144 | tf_op jit(solution)/shard_map/all_to_all | solution.py:240
  (34 shorter events, 19.7 us)
Async XLA Ops:
  24.3 27.1 %all-to-all-start.1 = ((bf16[32,8,1024]{2,1,0:T(8,128)(2,1)}), bf16[32,8,1024]{2,1,0:T(8,128)(2,1)}, u32[]{:S(2)}, u32[]{:S(2)}) async-start(bf16[32,8,1024]{2,1,0:T(8,128)(2,1)} %bitcast), calls=%async_computation.1 | async-start | bytes 1048576 | tf_op jit(solution)/shard_map/all_to_all | solution.py:236
  34.1 7.1 %collective-permute-start = (bf16[64,1024]{1,0:T(8,128)(2,1)S(1)}, bf16[64,1024]{1,0:T(8,128)(2,1)S(1)}, u32[]{:S(2)}, u32[]{:S(2)}) collective-permute-start(bf16[64,1024]{1,0:T(8,128)(2,1)S(1)} %get-tuple-element.29), channel_id=1, source_target_pairs={{0,2},{1,3},{2,0},{3,1},{4,6},{5,7},{6,4},{7,5},{8,10},{9,11},{10,... | collective-permute-start | bytes 393224 | tf_op jit(solution)/shard_map/ppermute | solution.py:258
  41.2 28.6 %copy-start = (bf16[1,192,4096]{2,1,0:T(8,128)(2,1)S(1)}, bf16[1,192,4096]{2,1,0:T(8,128)(2,1)}, u32[]{:S(2)}) copy-start(bf16[1,192,4096]{2,1,0:T(8,128)(2,1)} %param.11) | copy-start | bytes 4718596
  41.2 28.6 %copy-start.1 = (bf16[1,192,4096]{2,1,0:T(8,128)(2,1)S(1)}, bf16[1,192,4096]{2,1,0:T(8,128)(2,1)}, u32[]{:S(2)}) copy-start(bf16[1,192,4096]{2,1,0:T(8,128)(2,1)} %param.12) | copy-start | bytes 4718596
  41.6 1.0 copy-start.4
  51.4 14.5 %collective-permute-start.1 = (bf16[256,1024]{1,0:T(8,128)(2,1)}, bf16[256,1024]{1,0:T(8,128)(2,1)}, u32[]{:S(2)}, u32[]{:S(2)}) collective-permute-start(bf16[256,1024]{1,0:T(8,128)(2,1)} %bitcast.1.own_ref), channel_id=1, source_target_pairs={{0,2},{1,3},{2,0},{3,1},{4,6},{5,7},{6,4},{7,5},{8,10},{9,11},{10,... | collective-permute-start | bytes 1572872 | tf_op jit(solution)/shard_map/ppermute | solution.py:263
  53.3 30.5 %all-to-all-start.2 = ((bf16[32,8,2048]{2,1,0:T(8,128)(2,1)}), bf16[32,8,2048]{2,1,0:T(8,128)(2,1)}, u32[]{:S(2)}, u32[]{:S(2)}) async-start(bf16[32,8,2048]{2,1,0:T(8,128)(2,1)} %bitcast.23), calls=%async_computation.2 | async-start | bytes 2097152 | tf_op jit(solution)/shard_map/all_to_all | solution.py:236
  58.1 11.7 %collective-permute-start.3 = (bf16[256,1024]{1,0:T(8,128)(2,1)}, bf16[256,1024]{1,0:T(8,128)(2,1)S(1)}, u32[]{:S(2)}, u32[]{:S(2)}) collective-permute-start(bf16[256,1024]{1,0:T(8,128)(2,1)} %bitcast.1.own_ref), channel_id=1, source_target_pairs={{0,1},{1,0},{2,3},{3,2},{4,5},{5,4},{6,7},{7,6},{8,9},{9,8},{10,11... | collective-permute-start | bytes 1572872 | tf_op jit(solution)/shard_map/ppermute | solution.py:264
  65.9 5.9 %collective-permute-start.2 = (bf16[256,1024]{1,0:T(8,128)(2,1)}, bf16[256,1024]{1,0:T(8,128)(2,1)S(1)}, u32[]{:S(2)}, u32[]{:S(2)}) collective-permute-start(bf16[256,1024]{1,0:T(8,128)(2,1)} %collective-permute-done.1.z_ref), channel_id=1, source_target_pairs={{0,1},{1,0},{2,3},{3,2},{4,5},{5,4},{6,7},{7,6},{8,9},{9,8},{10,11... | collective-permute-start | bytes 1572872 | tf_op jit(solution)/shard_map/ppermute | solution.py:266
  69.8 1.9 %copy-start.2 = (bf16[1,192,4096]{2,1,0:T(8,128)(2,1)S(1)}, bf16[1,192,4096]{2,1,0:T(8,128)(2,1)}, u32[]{:S(2)}) copy-start(bf16[1,192,4096]{2,1,0:T(8,128)(2,1)} %param.13) | copy-start | bytes 4718596
  73.9 4.6 %collective-permute-start.4 = (bf16[256,2048]{1,0:T(8,128)(2,1)S(1)}, bf16[256,2048]{1,0:T(8,128)(2,1)S(1)}, u32[]{:S(2)}, u32[]{:S(2)}) collective-permute-start(bf16[256,2048]{1,0:T(8,128)(2,1)S(1)} %get-tuple-element.35), channel_id=1, source_target_pairs={{0,1},{1,0},{2,3},{3,2},{4,5},{5,4},{6,7},{7,6},{8,9},{9,8},{10,11... | collective-permute-start | bytes 3145736 | tf_op jit(solution)/shard_map/ppermute | solution.py:269
  78.9 1.0 copy-start.5
  83.8 12.8 %collective-permute-start.5 = (bf16[256,2048]{1,0:T(8,128)(2,1)}, bf16[256,2048]{1,0:T(8,128)(2,1)}, u32[]{:S(2)}, u32[]{:S(2)}) collective-permute-start(bf16[256,2048]{1,0:T(8,128)(2,1)} %bitcast.3.own_ref), channel_id=1, source_target_pairs={{0,1},{1,0},{2,3},{3,2},{4,5},{5,4},{6,7},{7,6},{8,9},{9,8},{10,11... | collective-permute-start | bytes 3145736 | tf_op jit(solution)/shard_map/ppermute | solution.py:274
  89.0 32.7 %all-to-all-start.4 = ((bf16[32,8,2048]{2,1,0:T(8,128)(2,1)}), bf16[32,8,2048]{2,1,0:T(8,128)(2,1)}, u32[]{:S(2)}, u32[]{:S(2)}) async-start(bf16[32,8,2048]{2,1,0:T(8,128)(2,1)} %bitcast.24), calls=%async_computation.4 | async-start | bytes 2097152 | tf_op jit(solution)/shard_map/all_to_all | solution.py:236
  94.5 2.1 %copy-start.3 = (bf16[1,192,4096]{2,1,0:T(8,128)(2,1)S(1)}, bf16[1,192,4096]{2,1,0:T(8,128)(2,1)}, u32[]{:S(2)}) copy-start(bf16[1,192,4096]{2,1,0:T(8,128)(2,1)} %param.13) | copy-start | bytes 4718596
  98.9 4.6 %collective-permute-start.6 = (bf16[256,2048]{1,0:T(8,128)(2,1)S(1)}, bf16[256,2048]{1,0:T(8,128)(2,1)S(1)}, u32[]{:S(2)}, u32[]{:S(2)}) collective-permute-start(bf16[256,2048]{1,0:T(8,128)(2,1)S(1)} %get-tuple-element.40), channel_id=1, source_target_pairs={{0,1},{1,0},{2,3},{3,2},{4,5},{5,4},{6,7},{7,6},{8,9},{9,8},{10,11... | collective-permute-start | bytes 3145736 | tf_op jit(solution)/shard_map/ppermute | solution.py:277
  103.9 15.2 %collective-permute-start.7 = (bf16[256,1024]{1,0:T(8,128)(2,1)S(1)}, bf16[256,1024]{1,0:T(8,128)(2,1)S(1)}, u32[]{:S(2)}, u32[]{:S(2)}) collective-permute-start(bf16[256,1024]{1,0:T(8,128)(2,1)S(1)} %get-tuple-element.42), channel_id=1, source_target_pairs={{0,2},{1,3},{2,0},{3,1},{4,6},{5,7},{6,4},{7,5},{8,10},{9,11},{10,... | collective-permute-start | bytes 1572872 | tf_op jit(solution)/shard_map/ppermute | solution.py:279
  121.7 22.9 %all-to-all-start.3 = ((bf16[32,8,1024]{2,1,0:T(8,128)(2,1)}), bf16[32,8,1024]{2,1,0:T(8,128)(2,1)S(1)}, u32[]{:S(2)}, u32[]{:S(2)}) async-start(bf16[32,8,1024]{2,1,0:T(8,128)(2,1)} %bitcast.7), calls=%async_computation.3 | async-start | bytes 1048576 | tf_op jit(solution)/shard_map/all_to_all | solution.py:236
  129.3 30.9 %copy-start.6 = (bf16[4,4096]{1,0:T(4,128)(2,1)S(1)}, bf16[4,4096]{1,0:T(4,128)(2,1)}, u32[]{:S(2)}) copy-start(bf16[4,4096]{1,0:T(4,128)(2,1)} %resid_ref.1) | copy-start | bytes 98308
  131.2 6.0 %collective-permute-start.8 = (bf16[64,1024]{1,0:T(8,128)(2,1)S(1)}, bf16[64,1024]{1,0:T(8,128)(2,1)S(1)}, u32[]{:S(2)}, u32[]{:S(2)}) collective-permute-start(bf16[64,1024]{1,0:T(8,128)(2,1)S(1)} %get-tuple-element.46), channel_id=1, source_target_pairs={{0,2},{1,3},{2,0},{3,1},{4,6},{5,7},{6,4},{7,5},{8,10},{9,11},{10,... | collective-permute-start | bytes 393224 | tf_op jit(solution)/shard_map/ppermute | solution.py:283

commit v4 on v2

v4 whole, which is shorter than its diff:
```python
import jax
import jax.numpy as jnp
from jax import lax
from jax.experimental import pallas as pl
from jax.experimental.pallas import tpu as pltpu
from jax.sharding import PartitionSpec as P

EXPERTS = 64
TOP = 8
META = 128
GROUP = 4
VMEM = pl.BlockSpec(memory_space=pltpu.VMEM)
ANY = pl.BlockSpec(memory_space=pl.ANY)
HBM = pl.BlockSpec(memory_space=pltpu.HBM)
PARAMS = pltpu.CompilerParams(vmem_limit_bytes=20 * 1024 * 1024)
WHOLE = pltpu.CompilerParams(vmem_limit_bytes=62 * 1024 * 1024)
NT = (((1,), (1,)), ((), ()))


def dot_nt(a, b):
    return lax.dot_general(a, b, NT, preferred_element_type=jnp.float32)


def dot_tn(a, b):
    return lax.dot_general(a, b, (((0,), (0,)), ((), ())), preferred_element_type=jnp.float32)


def dot_nn(a, b):
    return jnp.dot(a, b, preferred_element_type=jnp.float32)


def norm_kernel(x_hbm, gain_hbm, ids_hbm, share_hbm, out_ref, x_ref, gain_ref, ids_ref, share_ref, sems):
    copies = [
        pltpu.make_async_copy(src, dst, sems.at[n])
        for n, (src, dst) in enumerate(
            [(x_hbm, x_ref), (gain_hbm, gain_ref), (ids_hbm, ids_ref), (share_hbm, share_ref)]
        )
    ]
    for copy in copies:
        copy.start()
    for copy in copies:
        copy.wait()
    part = x_ref.shape[1] // 2
    x = x_ref[...].astype(jnp.float32)
    inv = lax.rsqrt(jnp.mean(x * x, axis=1, keepdims=True) + 1e-06)
    normed = (x * inv * gain_ref[...].astype(jnp.float32)[None, :]).astype(jnp.bfloat16)
    ids = ids_ref[...].astype(jnp.float32)
    share = share_ref[...].astype(jnp.float32)
    lane = lax.broadcasted_iota(jnp.int32, (x.shape[0], META), 1)
    meta = jnp.zeros((x.shape[0], META), jnp.float32)
    for k in range(TOP):
        meta = jnp.where(lane == k, ids[:, k : k + 1], meta)
        meta = jnp.where(lane == TOP + k, share[:, k : k + 1], meta)
    meta = meta.astype(jnp.bfloat16)
    for j in range(out_ref.shape[0]):
        half = j % 2
        out_ref[j, :, :part] = normed[:, half * part : (half + 1) * part]
        out_ref[j, :, part:] = meta


def ranks(meta):
    tokens = meta.shape[0]
    meta = meta.astype(jnp.float32)
    lanes = lax.broadcasted_iota(jnp.int32, (tokens, EXPERTS), 1).astype(jnp.float32)
    named = jnp.zeros((tokens, EXPERTS), jnp.float32)
    share = jnp.zeros((tokens, EXPERTS), jnp.float32)
    for k in range(TOP):
        hit = meta[:, k : k + 1] == lanes
        named = jnp.where(hit, 1.0, named)
        share = jnp.where(hit, meta[:, TOP + k : TOP + k + 1], share)
    t_row = lax.broadcasted_iota(jnp.int32, (tokens, tokens), 0)
    t_col = lax.broadcasted_iota(jnp.int32, (tokens, tokens), 1)
    before = dot_nn((t_col < t_row).astype(jnp.bfloat16), named.astype(jnp.bfloat16))
    rank = jnp.where(named > 0.0, before, -1.0)
    return rank.astype(jnp.bfloat16), share.astype(jnp.bfloat16)


def picks(rows):
    per = rows // (EXPERTS // 2)
    slot = lax.broadcasted_iota(jnp.int32, (rows, EXPERTS), 0)
    expert = lax.broadcasted_iota(jnp.int32, (rows, EXPERTS), 1)
    return (expert == 2 * (slot // per) + lax.axis_index("expert") // 8).astype(jnp.bfloat16)


def pack_kernel(row_ref, out_ref):
    tokens, (rows, part) = row_ref.shape[0], out_ref.shape
    per = rows // (EXPERTS // 2)
    rank, _ = ranks(row_ref[:, part:])
    slot = (lax.broadcasted_iota(jnp.int32, (rows, tokens), 0) % per).astype(jnp.float32)
    chosen = (dot_nt(picks(rows), rank) == slot).astype(jnp.bfloat16)
    out_ref[...] = dot_nn(chosen, row_ref[:, :part]).astype(jnp.bfloat16)


def weigh_kernel(row_ref, out_ref):
    rank, share = ranks(row_ref[:, row_ref.shape[1] - META :])
    tokens, rows = out_ref.shape
    per = rows // (EXPERTS // 2)
    pick = picks(rows)
    slot = (lax.broadcasted_iota(jnp.int32, (tokens, rows), 1) % per).astype(jnp.float32)
    out_ref[...] = jnp.where(dot_nt(rank, pick) == slot, dot_nt(share, pick), 0.0).astype(jnp.bfloat16)


def place():
    column = lax.axis_index("expert")
    return column % 2, (column // 2) % 2


def columns(ref, index, parts):
    part = ref.shape[1] // parts
    return ref[:, pl.ds(pl.multiple_of(index * part, part), part)]


def silu_mul(gate, up):
    return (gate / (1.0 + jnp.exp(-gate)) * up).astype(jnp.bfloat16)


def half_first_kernel(own_ref, gate_ref, up_ref, gate_out, up_out):
    c, _ = place()
    own = own_ref[...]
    gate_out[...] = dot_nt(columns(gate_ref, c, 2), own)
    up_out[...] = dot_nt(columns(up_ref, c, 2), own)


def half_act_kernel(other_ref, gate_in, up_in, gate_ref, up_ref, act_ref):
    c, _ = place()
    other = other_ref[...]
    gate = gate_in[...] + dot_nt(columns(gate_ref, 1 - c, 2), other)
    up = up_in[...] + dot_nt(columns(up_ref, 1 - c, 2), other)
    act_ref[...] = silu_mul(gate, up)


def own_part():
    c, b = place()
    return 2 * c + b


def give_kernel(down_ref, *outs):
    c, b = place()
    outs[0][...] = columns(down_ref, 2 * (1 - c) + b, GROUP)
    outs[1][...] = columns(down_ref, 2 * c + 1 - b, GROUP)
    outs[2][...] = columns(down_ref, 2 * (1 - c) + 1 - b, GROUP)


def touch_kernel(*refs):
    refs[-1][...] = jnp.zeros_like(refs[-1])


def down_kernel(*refs):
    acts, down_ref, others, out_ref = refs[:GROUP], refs[GROUP], refs[GROUP + 1 : 2 * GROUP], refs[-1]
    total = dot_tn(acts[0][...], columns(down_ref, own_part(), GROUP))
    for act, down in zip(acts[1:], others):
        total = total + dot_tn(act[...], down[...])
    out_ref[...] = total.astype(jnp.bfloat16)


def combine_kernel(weight_ref, in_ref, out_ref):
    out_ref[...] = dot_nn(weight_ref[...], in_ref[...]).astype(jnp.bfloat16)


def final_kernel(resid_ref, got_ref, out_ref):
    part = got_ref.shape[2]
    for q in range(GROUP):
        cols = slice(q * part, (q + 1) * part)
        total = resid_ref[:, cols].astype(jnp.float32)
        for i in range(2 * (q % 2) + q // 2, got_ref.shape[0], GROUP):
            total = total + got_ref[i].astype(jnp.float32)
        out_ref[:, cols] = total.astype(jnp.bfloat16)


def call(kernel, out_shape, *args):
    return pl.pallas_call(
        kernel,
        out_shape=out_shape,
        in_specs=[VMEM] * len(args),
        out_specs=jax.tree.map(lambda _: VMEM, out_shape),
        compiler_params=PARAMS,
    )(*args)


def bf16(*shape):
    return jax.ShapeDtypeStruct(shape, jnp.bfloat16)


def f32(*shape):
    return jax.ShapeDtypeStruct(shape, jnp.float32)


def body(hidden_in, norm_gain, expert_ids, gate_share, w_gate, w_up, w_down):
    dp_count = lax.axis_size("dp")
    col_count = lax.axis_size("expert")
    tok_dev, width = hidden_in.shape
    units = w_gate.shape[1]
    tok_row = tok_dev * col_count
    half, part = width // 2, width // GROUP
    per = tok_row // 4
    rows = dp_count * per
    def swap(x, k):
        return lax.ppermute(x, "expert", [(i, i ^ k) for i in range(col_count)])

    gate_w, up_w, down_w = (w.reshape(units, width) for w in (w_gate, w_up, w_down))
    partial_sums = [f32(units, rows)] * 2

    def over_dp(x):
        moved = lax.all_to_all(x.reshape(dp_count, per, x.shape[1]), "dp", split_axis=0, concat_axis=0, tiled=True)
        return moved.reshape(x.shape)

    def over_expert(x):
        return lax.all_to_all(x, "expert", split_axis=0, concat_axis=0, tiled=True)

    normed = pl.pallas_call(
        norm_kernel,
        out_shape=bf16(col_count, tok_dev, half + META),
        in_specs=[HBM] * 4,
        out_specs=VMEM,
        scratch_shapes=[
            pltpu.VMEM((tok_dev, width), jnp.bfloat16),
            pltpu.VMEM((width,), jnp.bfloat16),
            pltpu.VMEM((tok_dev, TOP), jnp.int32),
            pltpu.VMEM((tok_dev, TOP), jnp.bfloat16),
            pltpu.SemaphoreType.DMA((4,)),
        ],
        compiler_params=WHOLE,
    )(hidden_in, norm_gain, expert_ids, gate_share)
    row = over_expert(normed).reshape(tok_row, half + META)
    packed = call(pack_kernel, bf16(rows, half), row)
    weights = call(weigh_kernel, bf16(tok_row, rows), row)
    gives = call(give_kernel, [bf16(units, part)] * (GROUP - 1), down_w)
    downs = [swap(g, k + 1) for k, g in enumerate(gives)]
    token = pl.pallas_call(
        touch_kernel, out_shape=f32(8, 128), in_specs=[ANY] * (GROUP - 1) + [VMEM] * 2, out_specs=VMEM, compiler_params=PARAMS
    )(*downs, gate_w, up_w)

    own, token = lax.optimization_barrier((over_dp(packed), token))
    other = swap(own, 1)
    gate, up = call(half_first_kernel, partial_sums, own, gate_w, up_w)
    act = call(half_act_kernel, bf16(units, rows), other, gate, up, gate_w, up_w)
    from_z = swap(act, 2)
    acts = [act, swap(act, 1), from_z, swap(from_z, 1)]
    value = call(down_kernel, bf16(rows, part), *acts, down_w, *downs, token)
    routed = call(combine_kernel, bf16(tok_row, part), weights, over_dp(value))
    shares = over_expert(routed.reshape(col_count, tok_dev, part))
    return call(final_kernel, bf16(tok_dev, width), hidden_in, shares)


def solution(mesh):
    rows = P(("dp", "expert"), None)
    blocks = P(("dp", "expert"), None, None)
    return jax.shard_map(
        body, mesh=mesh, in_specs=(rows, P(), rows, rows, blocks, blocks, blocks), out_specs=rows, check_vma=False
    )
```

time: 167 us -> 160 us (0.958)
  blocking collectives: 69 us -> 38.2 us
  waiting for transfers between devices: 41.2 us -> 71.4 us
  starting transfers between devices: 38.9 us -> 33 us
  Pallas kernels: 15.5 us -> 11.1 us
  local copies, waits for them, and re-layouts: 1.18 us -> 5.11 us
    all_to_all x3 -> x2, waiting for transfers between devices: 19.4 us -> 50.1 us  [over_dp(): lax.all_to_all(x.reshape(dp_count, per, x.shape[1]), 'dp', split_axis=0,...]
    all_to_all x1 -> x0, blocking collectives: 27.2 us -> none  [over_dp(): lax.all_to_all(x.reshape(dp_count, per, x.shape[1]), 'dp', split_axis=0,...]
    pallas_call x12 -> x8, Pallas kernels: 13.9 us -> 9.42 us  [call(): pl.pallas_call(kernel, out_shape=out_shape, in_specs=[VMEM] * len(args),...]
    unnamed x14 -> x24, local copies, waits for them, and re-layouts: 1.01 us -> 4.98 us
    all_to_all x2, blocking collectives: 41.8 us -> 38.2 us  [over_expert(): return lax.all_to_all(x, 'expert', split_axis=0, concat_axis=0, tiled=True)]
    ppermute x7, starting transfers between devices: 20.9 us -> 17.7 us  [swap(): return lax.ppermute(x, 'expert', [(i, i ^ k) for i in range(col_count)])]
    all_to_all x3 -> x2, starting transfers between devices: 17.9 us -> 15.3 us  [over_dp(): lax.all_to_all(x.reshape(dp_count, per, x.shape[1]), 'dp', split_axis=0,...]
  transfers between devices with their start and end apart: 10 -> 9, of which waited for: 7 -> 7; matrix products, arithmetic and copies ran while one was open for 0% -> 0% of each run, Pallas kernels for 7% -> 2%
where the time goes in v4:
time: 160 us; the launch traced here: 159 us
  waiting for transfers between devices  71.4 us (45%)
  blocking collectives  38.2 us (24%)
  starting transfers between devices  33 us (21%)
  Pallas kernels  11.1 us (7%)
  local copies, waits for them, and re-layouts  5.11 us (3%)
    all_to_all x2, waiting for transfers between devices, over_dp(): lax.all_to_all(x.reshape(dp_count, per, x.shape[1]), 'dp', split_axis=0,...  50.1 us
    all_to_all x2, blocking collectives, over_expert(): return lax.all_to_all(x, 'expert', split_axis=0, concat_axis=0, tiled=True)  38.2 us
    ppermute x7, waiting for transfers between devices, swap(): return lax.ppermute(x, 'expert', [(i, i ^ k) for i in range(col_count)])  21.3 us
    ppermute x7, starting transfers between devices, swap(): return lax.ppermute(x, 'expert', [(i, i ^ k) for i in range(col_count)])  17.7 us
    all_to_all x2, starting transfers between devices, over_dp(): lax.all_to_all(x.reshape(dp_count, per, x.shape[1]), 'dp', split_axis=0,...  15.3 us
    pallas_call x8, Pallas kernels, call(): pl.pallas_call(kernel, out_shape=out_shape, in_specs=[VMEM] * len(args),...  9.42 us
    unnamed x24, local copies, waits for them, and re-layouts  4.98 us
  transfers between devices with their start and end apart: 9, of which 7 were waited for; matrix products, arithmetic and copies ran while one was open for 0% of the time, Pallas kernels for 2%

profile of v4, /device:TPU:1, one launch (start us, length us, event | category | flops | bytes accessed | tf_op | source)
XLA Modules:
  0.0 159.0 jit_solution(14873254332042522333)
XLA Ops:
  0.0 1.7 %shard_map.73 = bf16[16,4,2176]{2,1,0:T(4,128)(2,1)} custom-call(bf16[4,4096]{1,0:T(4,128)(2,1)} %resid_ref.1, bf16[4096]{0:T(1024)(128)(2,1)} %gain_hbm.1, s32[4,8]{1,0:T(4,128)} %ids_hbm.1, bf16[4,8]{1,0:T(4,128)(2,1)} %share_hbm.1), custom_call_target="tpu_custom_call" | custom-call | tf_op jit(solution)/shard_map/pallas_call | solution.py:210
  1.7 23.9 %all_to_all.20 = bf16[16,4,2176]{2,1,0:T(4,128)(2,1)S(1)} all-to-all(bf16[16,4,2176]{2,1,0:T(4,128)(2,1)} %shard_map.73), channel_id=1, replica_groups=mesh['dp'=32,'expert'=16] {'expert'}, dimensions={0} | all-to-all | bytes 557056 | tf_op jit(solution)/shard_map/all_to_all | solution.py:208
  25.6 1.1 shard_map.75
  26.7 1.3 copy-done.2
  28.0 10.1 %all-to-all-start.1 = ((bf16[32,16,2048]{2,1,0:T(8,128)(2,1)}), bf16[32,16,2048]{2,1,0:T(8,128)(2,1)}, u32[]{:S(2)}, u32[]{:S(2)}) async-start(bf16[32,16,2048]{2,1,0:T(8,128)(2,1)} %bitcast.13), calls=%async_computation.1 | async-start | bytes 4194304 | tf_op jit(solution)/shard_map/all_to_all | solution.py:204
  38.1 1.4 copy-done.3
  39.6 1.9 %collective-permute-start = (bf16[192,1024]{1,0:T(8,128)(2,1)S(1)}, bf16[192,1024]{1,0:T(8,128)(2,1)S(1)}, u32[]{:S(2)}, u32[]{:S(2)}) collective-permute-start(bf16[192,1024]{1,0:T(8,128)(2,1)S(1)} %get-tuple-element.12), channel_id=1, source_target_pairs={{0,1},{1,0},{2,3},{3,2},{4,5},{5,4},{6,7},{7,6},{8,9},{9,8},{10,11... | collective-permute-start | bytes 1179656 | tf_op jit(solution)/shard_map/ppermute | solution.py:198
  41.5 1.9 %collective-permute-start.1 = (bf16[192,1024]{1,0:T(8,128)(2,1)S(1)}, bf16[192,1024]{1,0:T(8,128)(2,1)S(1)}, u32[]{:S(2)}, u32[]{:S(2)}) collective-permute-start(bf16[192,1024]{1,0:T(8,128)(2,1)S(1)} %get-tuple-element.13), channel_id=1, source_target_pairs={{0,2},{1,3},{2,0},{3,1},{4,6},{5,7},{6,4},{7,5},{8,10},{9,11},{10,... | collective-permute-start | bytes 1179656 | tf_op jit(solution)/shard_map/ppermute | solution.py:198
  43.4 4.0 %collective-permute-start.2 = (bf16[192,1024]{1,0:T(8,128)(2,1)S(1)}, bf16[192,1024]{1,0:T(8,128)(2,1)S(1)}, u32[]{:S(2)}, u32[]{:S(2)}) collective-permute-start(bf16[192,1024]{1,0:T(8,128)(2,1)S(1)} %get-tuple-element.14), channel_id=1, source_target_pairs={{0,3},{1,2},{2,1},{3,0},{4,7},{5,6},{6,5},{7,4},{8,11},{9,10},{10,... | collective-permute-start | bytes 1179656 | tf_op jit(solution)/shard_map/ppermute | solution.py:198
  47.5 6.2 %collective-permute-done.1.refs_1_.refs_6_ = bf16[192,1024]{1,0:T(8,128)(2,1)S(1)} collective-permute-done((bf16[192,1024]{1,0:T(8,128)(2,1)S(1)}, bf16[192,1024]{1,0:T(8,128)(2,1)S(1)}, u32[]{:S(2)}, u32[]{:S(2)}) %collective-permute-start.1) | collective-permute-done | bytes 393248 | tf_op jit(solution)/shard_map/ppermute | solution.py:198
  53.7 9.4 %collective-permute-done.2.refs_2_.refs_7_ = bf16[192,1024]{1,0:T(8,128)(2,1)S(1)} collective-permute-done((bf16[192,1024]{1,0:T(8,128)(2,1)S(1)}, bf16[192,1024]{1,0:T(8,128)(2,1)S(1)}, u32[]{:S(2)}, u32[]{:S(2)}) %collective-permute-start.2) | collective-permute-done | bytes 393248 | tf_op jit(solution)/shard_map/ppermute | solution.py:198
  65.3 24.2 %all-to-all-done.1 = bf16[32,16,2048]{2,1,0:T(8,128)(2,1)} async-done(((bf16[32,16,2048]{2,1,0:T(8,128)(2,1)}), bf16[32,16,2048]{2,1,0:T(8,128)(2,1)}, u32[]{:S(2)}, u32[]{:S(2)}) %all-to-all-start.1) | async-done | bytes 2097184 | tf_op jit(solution)/shard_map/all_to_all | solution.py:204
  89.5 2.5 %collective-permute-start.3 = (bf16[512,2048]{1,0:T(8,128)(2,1)}, bf16[512,2048]{1,0:T(8,128)(2,1)S(1)}, u32[]{:S(2)}, u32[]{:S(2)}) collective-permute-start(bf16[512,2048]{1,0:T(8,128)(2,1)} %bitcast.1.own_ref), channel_id=1, source_target_pairs={{0,1},{1,0},{2,3},{3,2},{4,5},{5,4},{6,7},{7,6},{8,9},{9,8},{10,11... | collective-permute-start | bytes 6291464 | tf_op jit(solution)/shard_map/ppermute | solution.py:198
  92.1 3.1 %shard_map.78 = (f32[192,512]{1,0:T(8,128)S(1)}, f32[192,512]{1,0:T(8,128)S(1)}) custom-call(bf16[512,2048]{1,0:T(8,128)(2,1)} %bitcast.1.own_ref, bf16[192,4096]{1,0:T(8,128)(2,1)S(1)} %bitcast.8, bf16[192,4096]{1,0:T(8,128)(2,1)S(1)} %bitcast.11), custom_call_target="tpu_custom_call" | custom-call | tf_op jit(solution)/shard_map/pallas_call | solution.py:171
  96.1 1.5 shard_map.79.refs_0_
  97.6 1.9 %collective-permute-start.5 = (bf16[192,512]{1,0:T(8,128)(2,1)S(1)}, bf16[192,512]{1,0:T(8,128)(2,1)S(1)}, u32[]{:S(2)}, u32[]{:S(2)}) collective-permute-start(bf16[192,512]{1,0:T(8,128)(2,1)S(1)} %shard_map.79.refs_0_), channel_id=1, source_target_pairs={{0,2},{1,3},{2,0},{3,1},{4,6},{5,7},{6,4},{7,5},{8,10},{9,11},{10,... | collective-permute-start | bytes 589832 | tf_op jit(solution)/shard_map/ppermute | solution.py:198
  99.5 2.3 %collective-permute-start.4 = (bf16[192,512]{1,0:T(8,128)(2,1)S(1)}, bf16[192,512]{1,0:T(8,128)(2,1)S(1)}, u32[]{:S(2)}, u32[]{:S(2)}) collective-permute-start(bf16[192,512]{1,0:T(8,128)(2,1)S(1)} %shard_map.79.refs_0_), channel_id=1, source_target_pairs={{0,1},{1,0},{2,3},{3,2},{4,5},{5,4},{6,7},{7,6},{8,9},{9,8},{10,11... | collective-permute-start | bytes 589832 | tf_op jit(solution)/shard_map/ppermute | solution.py:198
  101.8 3.8 %collective-permute-done.5.refs_2_ = bf16[192,512]{1,0:T(8,128)(2,1)S(1)} collective-permute-done((bf16[192,512]{1,0:T(8,128)(2,1)S(1)}, bf16[192,512]{1,0:T(8,128)(2,1)S(1)}, u32[]{:S(2)}, u32[]{:S(2)}) %collective-permute-start.5) | collective-permute-done | bytes 196640 | tf_op jit(solution)/shard_map/ppermute | solution.py:198
  105.6 3.1 %collective-permute-start.6 = (bf16[192,512]{1,0:T(8,128)(2,1)S(1)}, bf16[192,512]{1,0:T(8,128)(2,1)S(1)}, u32[]{:S(2)}, u32[]{:S(2)}) collective-permute-start(bf16[192,512]{1,0:T(8,128)(2,1)S(1)} %collective-permute-done.5.refs_2_), channel_id=1, source_target_pairs={{0,1},{1,0},{2,3},{3,2},{4,5},{5,4},{6,7},{7,6},{8,9},{9,8},{10,11... | collective-permute-start | bytes 589832 | tf_op jit(solution)/shard_map/ppermute | solution.py:198
  108.7 1.0 collective-permute-done.6.refs_3_
  109.8 2.3 %shard_map.80 = bf16[512,1024]{1,0:T(8,128)(2,1)} custom-call(bf16[192,512]{1,0:T(8,128)(2,1)S(1)} %shard_map.79.refs_0_, bf16[192,512]{1,0:T(8,128)(2,1)S(1)} %collective-permute-done.4.refs_1_, bf16[192,512]{1,0:T(8,128)(2,1)S(1)} %collective-permute-done.5.refs_2_, bf16[192,512]{1,0:T(8,128)(2,1)S(1)} %collective-permute-done.6.refs_3_, ...), custom_call_target="tpu_custom_call" | custom-call | tf_op jit(solution)/shard_map/pallas_call | solution.py:171
  112.1 5.3 %all-to-all-start.2 = ((bf16[32,16,1024]{2,1,0:T(8,128)(2,1)}), bf16[32,16,1024]{2,1,0:T(8,128)(2,1)S(1)}, u32[]{:S(2)}, u32[]{:S(2)}) async-start(bf16[32,16,1024]{2,1,0:T(8,128)(2,1)} %bitcast.5), calls=%async_computation.2 | async-start | bytes 2097152 | tf_op jit(solution)/shard_map/all_to_all | solution.py:204
  117.7 25.9 %all-to-all-done.2 = bf16[32,16,1024]{2,1,0:T(8,128)(2,1)S(1)} async-done(((bf16[32,16,1024]{2,1,0:T(8,128)(2,1)}), bf16[32,16,1024]{2,1,0:T(8,128)(2,1)S(1)}, u32[]{:S(2)}, u32[]{:S(2)}) %all-to-all-start.2) | async-done | bytes 1048608 | tf_op jit(solution)/shard_map/all_to_all | solution.py:204
  144.0 14.3 %all_to_all.21.got_ref = bf16[16,4,1024]{2,1,0:T(4,128)(2,1)S(1)} all-to-all(bf16[16,4,1024]{2,1,0:T(4,128)(2,1)S(1)} %reshape.35), channel_id=1, replica_groups=mesh['dp'=32,'expert'=16] {'expert'}, dimensions={0} | all-to-all | bytes 262144 | tf_op jit(solution)/shard_map/all_to_all | solution.py:208
  (32 shorter events, 4.7 us)
Async XLA Ops:
  26.7 1.3 copy-start.2
  28.0 35.1 %copy-start = (bf16[1,192,4096]{2,1,0:T(8,128)(2,1)S(1)}, bf16[1,192,4096]{2,1,0:T(8,128)(2,1)}, u32[]{:S(2)}) copy-start(bf16[1,192,4096]{2,1,0:T(8,128)(2,1)} %param.11) | copy-start | bytes 4718596
  28.0 35.1 %copy-start.1 = (bf16[1,192,4096]{2,1,0:T(8,128)(2,1)S(1)}, bf16[1,192,4096]{2,1,0:T(8,128)(2,1)}, u32[]{:S(2)}) copy-start(bf16[1,192,4096]{2,1,0:T(8,128)(2,1)} %param.12) | copy-start | bytes 4718596
  28.0 61.5 %all-to-all-start.1 = ((bf16[32,16,2048]{2,1,0:T(8,128)(2,1)}), bf16[32,16,2048]{2,1,0:T(8,128)(2,1)}, u32[]{:S(2)}, u32[]{:S(2)}) async-start(bf16[32,16,2048]{2,1,0:T(8,128)(2,1)} %bitcast.13), calls=%async_computation.1 | async-start | bytes 4194304 | tf_op jit(solution)/shard_map/all_to_all | solution.py:204
  38.1 1.4 copy-start.3
  39.6 7.9 %collective-permute-start = (bf16[192,1024]{1,0:T(8,128)(2,1)S(1)}, bf16[192,1024]{1,0:T(8,128)(2,1)S(1)}, u32[]{:S(2)}, u32[]{:S(2)}) collective-permute-start(bf16[192,1024]{1,0:T(8,128)(2,1)S(1)} %get-tuple-element.12), channel_id=1, source_target_pairs={{0,1},{1,0},{2,3},{3,2},{4,5},{5,4},{6,7},{7,6},{8,9},{9,8},{10,11... | collective-permute-start | bytes 1179656 | tf_op jit(solution)/shard_map/ppermute | solution.py:198
  41.5 12.2 %collective-permute-start.1 = (bf16[192,1024]{1,0:T(8,128)(2,1)S(1)}, bf16[192,1024]{1,0:T(8,128)(2,1)S(1)}, u32[]{:S(2)}, u32[]{:S(2)}) collective-permute-start(bf16[192,1024]{1,0:T(8,128)(2,1)S(1)} %get-tuple-element.13), channel_id=1, source_target_pairs={{0,2},{1,3},{2,0},{3,1},{4,6},{5,7},{6,4},{7,5},{8,10},{9,11},{10,... | collective-permute-start | bytes 1179656 | tf_op jit(solution)/shard_map/ppermute | solution.py:198
  43.4 19.6 %collective-permute-start.2 = (bf16[192,1024]{1,0:T(8,128)(2,1)S(1)}, bf16[192,1024]{1,0:T(8,128)(2,1)S(1)}, u32[]{:S(2)}, u32[]{:S(2)}) collective-permute-start(bf16[192,1024]{1,0:T(8,128)(2,1)S(1)} %get-tuple-element.14), channel_id=1, source_target_pairs={{0,3},{1,2},{2,1},{3,0},{4,7},{5,6},{6,5},{7,4},{8,11},{9,10},{10,... | collective-permute-start | bytes 1179656 | tf_op jit(solution)/shard_map/ppermute | solution.py:198
  63.1 0.8 copy-start.5
  63.8 0.7 copy-start.7
  64.6 0.8 copy-start.9
  89.5 6.5 %collective-permute-start.3 = (bf16[512,2048]{1,0:T(8,128)(2,1)}, bf16[512,2048]{1,0:T(8,128)(2,1)S(1)}, u32[]{:S(2)}, u32[]{:S(2)}) collective-permute-start(bf16[512,2048]{1,0:T(8,128)(2,1)} %bitcast.1.own_ref), channel_id=1, source_target_pairs={{0,1},{1,0},{2,3},{3,2},{4,5},{5,4},{6,7},{7,6},{8,9},{9,8},{10,11... | collective-permute-start | bytes 6291464 | tf_op jit(solution)/shard_map/ppermute | solution.py:198
  96.1 13.7 %copy-start.4 = (bf16[1,192,4096]{2,1,0:T(8,128)(2,1)S(1)}, bf16[1,192,4096]{2,1,0:T(8,128)(2,1)}, u32[]{:S(2)}) copy-start(bf16[1,192,4096]{2,1,0:T(8,128)(2,1)} %param.13) | copy-start | bytes 4718596
  96.1 13.7 %copy-start.6 = (bf16[192,1024]{1,0:T(8,128)(2,1)S(1)}, bf16[192,1024]{1,0:T(8,128)(2,1)}, u32[]{:S(2)}) copy-start(bf16[192,1024]{1,0:T(8,128)(2,1)} %copy-done.5) | copy-start | bytes 1179652
  96.1 13.7 %copy-start.8 = (bf16[192,1024]{1,0:T(8,128)(2,1)S(1)}, bf16[192,1024]{1,0:T(8,128)(2,1)}, u32[]{:S(2)}) copy-start(bf16[192,1024]{1,0:T(8,128)(2,1)} %copy-done.7) | copy-start | bytes 1179652
  96.1 13.7 %copy-start.10 = (bf16[192,1024]{1,0:T(8,128)(2,1)S(1)}, bf16[192,1024]{1,0:T(8,128)(2,1)}, u32[]{:S(2)}) copy-start(bf16[192,1024]{1,0:T(8,128)(2,1)} %copy-done.9) | copy-start | bytes 1179652
  97.6 8.0 %collective-permute-start.5 = (bf16[192,512]{1,0:T(8,128)(2,1)S(1)}, bf16[192,512]{1,0:T(8,128)(2,1)S(1)}, u32[]{:S(2)}, u32[]{:S(2)}) collective-permute-start(bf16[192,512]{1,0:T(8,128)(2,1)S(1)} %shard_map.79.refs_0_), channel_id=1, source_target_pairs={{0,2},{1,3},{2,0},{3,1},{4,6},{5,7},{6,4},{7,5},{8,10},{9,11},{10,... | collective-permute-start | bytes 589832 | tf_op jit(solution)/shard_map/ppermute | solution.py:198
  99.5 9.2 %collective-permute-start.4 = (bf16[192,512]{1,0:T(8,128)(2,1)S(1)}, bf16[192,512]{1,0:T(8,128)(2,1)S(1)}, u32[]{:S(2)}, u32[]{:S(2)}) collective-permute-start(bf16[192,512]{1,0:T(8,128)(2,1)S(1)} %shard_map.79.refs_0_), channel_id=1, source_target_pairs={{0,1},{1,0},{2,3},{3,2},{4,5},{5,4},{6,7},{7,6},{8,9},{9,8},{10,11... | collective-permute-start | bytes 589832 | tf_op jit(solution)/shard_map/ppermute | solution.py:198
  105.6 4.2 %collective-permute-start.6 = (bf16[192,512]{1,0:T(8,128)(2,1)S(1)}, bf16[192,512]{1,0:T(8,128)(2,1)S(1)}, u32[]{:S(2)}, u32[]{:S(2)}) collective-permute-start(bf16[192,512]{1,0:T(8,128)(2,1)S(1)} %collective-permute-done.5.refs_2_), channel_id=1, source_target_pairs={{0,1},{1,0},{2,3},{3,2},{4,5},{5,4},{6,7},{7,6},{8,9},{9,8},{10,11... | collective-permute-start | bytes 589832 | tf_op jit(solution)/shard_map/ppermute | solution.py:198
  112.1 46.2 %copy-start.11 = (bf16[4,4096]{1,0:T(4,128)(2,1)S(1)}, bf16[4,4096]{1,0:T(4,128)(2,1)}, u32[]{:S(2)}) copy-start(bf16[4,4096]{1,0:T(4,128)(2,1)} %resid_ref.1) | copy-start | bytes 98308
  112.1 31.6 %all-to-all-start.2 = ((bf16[32,16,1024]{2,1,0:T(8,128)(2,1)}), bf16[32,16,1024]{2,1,0:T(8,128)(2,1)S(1)}, u32[]{:S(2)}, u32[]{:S(2)}) async-start(bf16[32,16,1024]{2,1,0:T(8,128)(2,1)} %bitcast.5), calls=%async_computation.2 | async-start | bytes 2097152 | tf_op jit(solution)/shard_map/all_to_all | solution.py:204

commit v5 on v4

--- a/solution.py
+++ b/solution.py
@@ -124,9 +124,10 @@
 def half_act_kernel(other_ref, gate_in, up_in, gate_ref, up_ref, act_ref):
     c, _ = place()
     other = other_ref[...]
-    gate = gate_in[...] + dot_nt(columns(gate_ref, 1 - c, 2), other)
-    up = up_in[...] + dot_nt(columns(up_ref, 1 - c, 2), other)
-    act_ref[...] = silu_mul(gate, up)
+    units = gate_ref.shape[0]
+    both = jnp.concatenate([columns(gate_ref, 1 - c, 2), columns(up_ref, 1 - c, 2)], axis=0)
+    both = dot_nt(both, other)
+    act_ref[...] = silu_mul(gate_in[...] + both[:units], up_in[...] + both[units:])
 
 
 def own_part():
@@ -147,10 +148,9 @@
 
 def down_kernel(*refs):
     acts, down_ref, others, out_ref = refs[:GROUP], refs[GROUP], refs[GROUP + 1 : 2 * GROUP], refs[-1]
-    total = dot_tn(acts[0][...], columns(down_ref, own_part(), GROUP))
-    for act, down in zip(acts[1:], others):
-        total = total + dot_tn(act[...], down[...])
-    out_ref[...] = total.astype(jnp.bfloat16)
+    downs = [columns(down_ref, own_part(), GROUP)] + [down[...] for down in others]
+    act = jnp.concatenate([act[...] for act in acts], axis=0)
+    out_ref[...] = dot_tn(act, jnp.concatenate(downs, axis=0)).astype(jnp.bfloat16)
 
 
 def combine_kernel(weight_ref, in_ref, out_ref):

time: 160 us -> 159 us (level)
  no operation moved by 1% of the time
where the time goes in v5:
time: 159 us; the launch traced here: 158 us
  waiting for transfers between devices  71.3 us (45%)
  blocking collectives  38.2 us (24%)
  starting transfers between devices  33.1 us (21%)
  Pallas kernels  10.3 us (6%)
  local copies, waits for them, and re-layouts  5.11 us (3%)
    all_to_all x2, waiting for transfers between devices, over_dp(): lax.all_to_all(x.reshape(dp_count, per, x.shape[1]), 'dp', split_axis=0,...  50.1 us
    all_to_all x2, blocking collectives, over_expert(): return lax.all_to_all(x, 'expert', split_axis=0, concat_axis=0, tiled=True)  38.2 us
    ppermute x7, waiting for transfers between devices, swap(): return lax.ppermute(x, 'expert', [(i, i ^ k) for i in range(col_count)])  21.3 us
    ppermute x7, starting transfers between devices, swap(): return lax.ppermute(x, 'expert', [(i, i ^ k) for i in range(col_count)])  17.7 us
    all_to_all x2, starting transfers between devices, over_dp(): lax.all_to_all(x.reshape(dp_count, per, x.shape[1]), 'dp', split_axis=0,...  15.3 us
    pallas_call x8, Pallas kernels, call(): pl.pallas_call(kernel, out_shape=out_shape, in_specs=[VMEM] * len(args),...  8.65 us
    unnamed x24, local copies, waits for them, and re-layouts  4.98 us
  transfers between devices with their start and end apart: 9, of which 7 were waited for; matrix products, arithmetic and copies ran while one was open for 0% of the time, Pallas kernels for 2%

profile of v5, /device:TPU:1, one launch (start us, length us, event | category | flops | bytes accessed | tf_op | source)
XLA Modules:
  0.0 158.2 jit_solution(10627447108049096328)
XLA Ops:
  0.0 1.7 %shard_map.73 = bf16[16,4,2176]{2,1,0:T(4,128)(2,1)} custom-call(bf16[4,4096]{1,0:T(4,128)(2,1)} %resid_ref.1, bf16[4096]{0:T(1024)(128)(2,1)} %gain_hbm.1, s32[4,8]{1,0:T(4,128)} %ids_hbm.1, bf16[4,8]{1,0:T(4,128)(2,1)} %share_hbm.1), custom_call_target="tpu_custom_call" | custom-call | tf_op jit(solution)/shard_map/pallas_call | solution.py:210
  1.7 23.9 %all_to_all.20 = bf16[16,4,2176]{2,1,0:T(4,128)(2,1)S(1)} all-to-all(bf16[16,4,2176]{2,1,0:T(4,128)(2,1)} %shard_map.73), channel_id=1, replica_groups=mesh['dp'=32,'expert'=16] {'expert'}, dimensions={0} | all-to-all | bytes 557056 | tf_op jit(solution)/shard_map/all_to_all | solution.py:208
  25.6 1.1 shard_map.75
  26.7 1.3 copy-done.2
  28.0 10.1 %all-to-all-start.1 = ((bf16[32,16,2048]{2,1,0:T(8,128)(2,1)}), bf16[32,16,2048]{2,1,0:T(8,128)(2,1)}, u32[]{:S(2)}, u32[]{:S(2)}) async-start(bf16[32,16,2048]{2,1,0:T(8,128)(2,1)} %bitcast.13), calls=%async_computation.1 | async-start | bytes 4194304 | tf_op jit(solution)/shard_map/all_to_all | solution.py:204
  38.1 1.4 copy-done.3
  39.6 1.9 %collective-permute-start = (bf16[192,1024]{1,0:T(8,128)(2,1)S(1)}, bf16[192,1024]{1,0:T(8,128)(2,1)S(1)}, u32[]{:S(2)}, u32[]{:S(2)}) collective-permute-start(bf16[192,1024]{1,0:T(8,128)(2,1)S(1)} %get-tuple-element.12), channel_id=1, source_target_pairs={{0,1},{1,0},{2,3},{3,2},{4,5},{5,4},{6,7},{7,6},{8,9},{9,8},{10,11... | collective-permute-start | bytes 1179656 | tf_op jit(solution)/shard_map/ppermute | solution.py:198
  41.5 1.9 %collective-permute-start.1 = (bf16[192,1024]{1,0:T(8,128)(2,1)S(1)}, bf16[192,1024]{1,0:T(8,128)(2,1)S(1)}, u32[]{:S(2)}, u32[]{:S(2)}) collective-permute-start(bf16[192,1024]{1,0:T(8,128)(2,1)S(1)} %get-tuple-element.13), channel_id=1, source_target_pairs={{0,2},{1,3},{2,0},{3,1},{4,6},{5,7},{6,4},{7,5},{8,10},{9,11},{10,... | collective-permute-start | bytes 1179656 | tf_op jit(solution)/shard_map/ppermute | solution.py:198
  43.4 4.0 %collective-permute-start.2 = (bf16[192,1024]{1,0:T(8,128)(2,1)S(1)}, bf16[192,1024]{1,0:T(8,128)(2,1)S(1)}, u32[]{:S(2)}, u32[]{:S(2)}) collective-permute-start(bf16[192,1024]{1,0:T(8,128)(2,1)S(1)} %get-tuple-element.14), channel_id=1, source_target_pairs={{0,3},{1,2},{2,1},{3,0},{4,7},{5,6},{6,5},{7,4},{8,11},{9,10},{10,... | collective-permute-start | bytes 1179656 | tf_op jit(solution)/shard_map/ppermute | solution.py:198
  47.5 6.2 %collective-permute-done.1.refs_1_.refs_6_ = bf16[192,1024]{1,0:T(8,128)(2,1)S(1)} collective-permute-done((bf16[192,1024]{1,0:T(8,128)(2,1)S(1)}, bf16[192,1024]{1,0:T(8,128)(2,1)S(1)}, u32[]{:S(2)}, u32[]{:S(2)}) %collective-permute-start.1) | collective-permute-done | bytes 393248 | tf_op jit(solution)/shard_map/ppermute | solution.py:198
  53.7 9.4 %collective-permute-done.2.refs_2_.refs_7_ = bf16[192,1024]{1,0:T(8,128)(2,1)S(1)} collective-permute-done((bf16[192,1024]{1,0:T(8,128)(2,1)S(1)}, bf16[192,1024]{1,0:T(8,128)(2,1)S(1)}, u32[]{:S(2)}, u32[]{:S(2)}) %collective-permute-start.2) | collective-permute-done | bytes 393248 | tf_op jit(solution)/shard_map/ppermute | solution.py:198
  65.3 24.2 %all-to-all-done.1 = bf16[32,16,2048]{2,1,0:T(8,128)(2,1)} async-done(((bf16[32,16,2048]{2,1,0:T(8,128)(2,1)}), bf16[32,16,2048]{2,1,0:T(8,128)(2,1)}, u32[]{:S(2)}, u32[]{:S(2)}) %all-to-all-start.1) | async-done | bytes 2097184 | tf_op jit(solution)/shard_map/all_to_all | solution.py:204
  89.5 2.5 %collective-permute-start.3 = (bf16[512,2048]{1,0:T(8,128)(2,1)}, bf16[512,2048]{1,0:T(8,128)(2,1)S(1)}, u32[]{:S(2)}, u32[]{:S(2)}) collective-permute-start(bf16[512,2048]{1,0:T(8,128)(2,1)} %bitcast.1.own_ref), channel_id=1, source_target_pairs={{0,1},{1,0},{2,3},{3,2},{4,5},{5,4},{6,7},{7,6},{8,9},{9,8},{10,11... | collective-permute-start | bytes 6291464 | tf_op jit(solution)/shard_map/ppermute | solution.py:198
  92.1 3.1 %shard_map.78 = (f32[192,512]{1,0:T(8,128)S(1)}, f32[192,512]{1,0:T(8,128)S(1)}) custom-call(bf16[512,2048]{1,0:T(8,128)(2,1)} %bitcast.1.own_ref, bf16[192,4096]{1,0:T(8,128)(2,1)S(1)} %bitcast.8, bf16[192,4096]{1,0:T(8,128)(2,1)S(1)} %bitcast.11), custom_call_target="tpu_custom_call" | custom-call | tf_op jit(solution)/shard_map/pallas_call | solution.py:171
  96.1 1.0 shard_map.79.refs_0_
  97.1 1.9 %collective-permute-start.5 = (bf16[192,512]{1,0:T(8,128)(2,1)S(1)}, bf16[192,512]{1,0:T(8,128)(2,1)S(1)}, u32[]{:S(2)}, u32[]{:S(2)}) collective-permute-start(bf16[192,512]{1,0:T(8,128)(2,1)S(1)} %shard_map.79.refs_0_), channel_id=1, source_target_pairs={{0,2},{1,3},{2,0},{3,1},{4,6},{5,7},{6,4},{7,5},{8,10},{9,11},{10,... | collective-permute-start | bytes 589832 | tf_op jit(solution)/shard_map/ppermute | solution.py:198
  99.0 2.3 %collective-permute-start.4 = (bf16[192,512]{1,0:T(8,128)(2,1)S(1)}, bf16[192,512]{1,0:T(8,128)(2,1)S(1)}, u32[]{:S(2)}, u32[]{:S(2)}) collective-permute-start(bf16[192,512]{1,0:T(8,128)(2,1)S(1)} %shard_map.79.refs_0_), channel_id=1, source_target_pairs={{0,1},{1,0},{2,3},{3,2},{4,5},{5,4},{6,7},{7,6},{8,9},{9,8},{10,11... | collective-permute-start | bytes 589832 | tf_op jit(solution)/shard_map/ppermute | solution.py:198
  101.3 3.8 %collective-permute-done.5.refs_2_ = bf16[192,512]{1,0:T(8,128)(2,1)S(1)} collective-permute-done((bf16[192,512]{1,0:T(8,128)(2,1)S(1)}, bf16[192,512]{1,0:T(8,128)(2,1)S(1)}, u32[]{:S(2)}, u32[]{:S(2)}) %collective-permute-start.5) | collective-permute-done | bytes 196640 | tf_op jit(solution)/shard_map/ppermute | solution.py:198
  105.1 3.1 %collective-permute-start.6 = (bf16[192,512]{1,0:T(8,128)(2,1)S(1)}, bf16[192,512]{1,0:T(8,128)(2,1)S(1)}, u32[]{:S(2)}, u32[]{:S(2)}) collective-permute-start(bf16[192,512]{1,0:T(8,128)(2,1)S(1)} %collective-permute-done.5.refs_2_), channel_id=1, source_target_pairs={{0,1},{1,0},{2,3},{3,2},{4,5},{5,4},{6,7},{7,6},{8,9},{9,8},{10,11... | collective-permute-start | bytes 589832 | tf_op jit(solution)/shard_map/ppermute | solution.py:198
  108.2 1.0 collective-permute-done.6.refs_3_
  109.3 2.0 %shard_map.80 = bf16[512,1024]{1,0:T(8,128)(2,1)} custom-call(bf16[192,512]{1,0:T(8,128)(2,1)S(1)} %shard_map.79.refs_0_, bf16[192,512]{1,0:T(8,128)(2,1)S(1)} %collective-permute-done.4.refs_1_, bf16[192,512]{1,0:T(8,128)(2,1)S(1)} %collective-permute-done.5.refs_2_, bf16[192,512]{1,0:T(8,128)(2,1)S(1)} %collective-permute-done.6.refs_3_, ...), custom_call_target="tpu_custom_call" | custom-call | tf_op jit(solution)/shard_map/pallas_call | solution.py:171
  111.3 5.3 %all-to-all-start.2 = ((bf16[32,16,1024]{2,1,0:T(8,128)(2,1)}), bf16[32,16,1024]{2,1,0:T(8,128)(2,1)S(1)}, u32[]{:S(2)}, u32[]{:S(2)}) async-start(bf16[32,16,1024]{2,1,0:T(8,128)(2,1)} %bitcast.5), calls=%async_computation.2 | async-start | bytes 2097152 | tf_op jit(solution)/shard_map/all_to_all | solution.py:204
  117.0 25.9 %all-to-all-done.2 = bf16[32,16,1024]{2,1,0:T(8,128)(2,1)S(1)} async-done(((bf16[32,16,1024]{2,1,0:T(8,128)(2,1)}), bf16[32,16,1024]{2,1,0:T(8,128)(2,1)S(1)}, u32[]{:S(2)}, u32[]{:S(2)}) %all-to-all-start.2) | async-done | bytes 1048608 | tf_op jit(solution)/shard_map/all_to_all | solution.py:204
  143.2 14.3 %all_to_all.21.got_ref = bf16[16,4,1024]{2,1,0:T(4,128)(2,1)S(1)} all-to-all(bf16[16,4,1024]{2,1,0:T(4,128)(2,1)S(1)} %reshape.35), channel_id=1, replica_groups=mesh['dp'=32,'expert'=16] {'expert'}, dimensions={0} | all-to-all | bytes 262144 | tf_op jit(solution)/shard_map/all_to_all | solution.py:208
  (32 shorter events, 4.7 us)
Async XLA Ops:
  26.7 1.3 copy-start.2
  28.0 35.1 %copy-start = (bf16[1,192,4096]{2,1,0:T(8,128)(2,1)S(1)}, bf16[1,192,4096]{2,1,0:T(8,128)(2,1)}, u32[]{:S(2)}) copy-start(bf16[1,192,4096]{2,1,0:T(8,128)(2,1)} %param.11) | copy-start | bytes 4718596
  28.0 35.1 %copy-start.1 = (bf16[1,192,4096]{2,1,0:T(8,128)(2,1)S(1)}, bf16[1,192,4096]{2,1,0:T(8,128)(2,1)}, u32[]{:S(2)}) copy-start(bf16[1,192,4096]{2,1,0:T(8,128)(2,1)} %param.12) | copy-start | bytes 4718596
  28.0 61.5 %all-to-all-start.1 = ((bf16[32,16,2048]{2,1,0:T(8,128)(2,1)}), bf16[32,16,2048]{2,1,0:T(8,128)(2,1)}, u32[]{:S(2)}, u32[]{:S(2)}) async-start(bf16[32,16,2048]{2,1,0:T(8,128)(2,1)} %bitcast.13), calls=%async_computation.1 | async-start | bytes 4194304 | tf_op jit(solution)/shard_map/all_to_all | solution.py:204
  38.1 1.4 copy-start.3
  39.6 7.9 %collective-permute-start = (bf16[192,1024]{1,0:T(8,128)(2,1)S(1)}, bf16[192,1024]{1,0:T(8,128)(2,1)S(1)}, u32[]{:S(2)}, u32[]{:S(2)}) collective-permute-start(bf16[192,1024]{1,0:T(8,128)(2,1)S(1)} %get-tuple-element.12), channel_id=1, source_target_pairs={{0,1},{1,0},{2,3},{3,2},{4,5},{5,4},{6,7},{7,6},{8,9},{9,8},{10,11... | collective-permute-start | bytes 1179656 | tf_op jit(solution)/shard_map/ppermute | solution.py:198
  41.5 12.2 %collective-permute-start.1 = (bf16[192,1024]{1,0:T(8,128)(2,1)S(1)}, bf16[192,1024]{1,0:T(8,128)(2,1)S(1)}, u32[]{:S(2)}, u32[]{:S(2)}) collective-permute-start(bf16[192,1024]{1,0:T(8,128)(2,1)S(1)} %get-tuple-element.13), channel_id=1, source_target_pairs={{0,2},{1,3},{2,0},{3,1},{4,6},{5,7},{6,4},{7,5},{8,10},{9,11},{10,... | collective-permute-start | bytes 1179656 | tf_op jit(solution)/shard_map/ppermute | solution.py:198
  43.4 19.6 %collective-permute-start.2 = (bf16[192,1024]{1,0:T(8,128)(2,1)S(1)}, bf16[192,1024]{1,0:T(8,128)(2,1)S(1)}, u32[]{:S(2)}, u32[]{:S(2)}) collective-permute-start(bf16[192,1024]{1,0:T(8,128)(2,1)S(1)} %get-tuple-element.14), channel_id=1, source_target_pairs={{0,3},{1,2},{2,1},{3,0},{4,7},{5,6},{6,5},{7,4},{8,11},{9,10},{10,... | collective-permute-start | bytes 1179656 | tf_op jit(solution)/shard_map/ppermute | solution.py:198
  63.1 0.8 copy-start.5
  63.8 0.7 copy-start.7
  64.6 0.8 copy-start.9
  89.5 6.5 %collective-permute-start.3 = (bf16[512,2048]{1,0:T(8,128)(2,1)}, bf16[512,2048]{1,0:T(8,128)(2,1)S(1)}, u32[]{:S(2)}, u32[]{:S(2)}) collective-permute-start(bf16[512,2048]{1,0:T(8,128)(2,1)} %bitcast.1.own_ref), channel_id=1, source_target_pairs={{0,1},{1,0},{2,3},{3,2},{4,5},{5,4},{6,7},{7,6},{8,9},{9,8},{10,11... | collective-permute-start | bytes 6291464 | tf_op jit(solution)/shard_map/ppermute | solution.py:198
  96.1 13.2 %copy-start.4 = (bf16[1,192,4096]{2,1,0:T(8,128)(2,1)S(1)}, bf16[1,192,4096]{2,1,0:T(8,128)(2,1)}, u32[]{:S(2)}) copy-start(bf16[1,192,4096]{2,1,0:T(8,128)(2,1)} %param.13) | copy-start | bytes 4718596
  96.1 13.2 %copy-start.6 = (bf16[192,1024]{1,0:T(8,128)(2,1)S(1)}, bf16[192,1024]{1,0:T(8,128)(2,1)}, u32[]{:S(2)}) copy-start(bf16[192,1024]{1,0:T(8,128)(2,1)} %copy-done.5) | copy-start | bytes 1179652
  96.1 13.2 %copy-start.8 = (bf16[192,1024]{1,0:T(8,128)(2,1)S(1)}, bf16[192,1024]{1,0:T(8,128)(2,1)}, u32[]{:S(2)}) copy-start(bf16[192,1024]{1,0:T(8,128)(2,1)} %copy-done.7) | copy-start | bytes 1179652
  96.1 13.2 %copy-start.10 = (bf16[192,1024]{1,0:T(8,128)(2,1)S(1)}, bf16[192,1024]{1,0:T(8,128)(2,1)}, u32[]{:S(2)}) copy-start(bf16[192,1024]{1,0:T(8,128)(2,1)} %copy-done.9) | copy-start | bytes 1179652
  97.1 8.0 %collective-permute-start.5 = (bf16[192,512]{1,0:T(8,128)(2,1)S(1)}, bf16[192,512]{1,0:T(8,128)(2,1)S(1)}, u32[]{:S(2)}, u32[]{:S(2)}) collective-permute-start(bf16[192,512]{1,0:T(8,128)(2,1)S(1)} %shard_map.79.refs_0_), channel_id=1, source_target_pairs={{0,2},{1,3},{2,0},{3,1},{4,6},{5,7},{6,4},{7,5},{8,10},{9,11},{10,... | collective-permute-start | bytes 589832 | tf_op jit(solution)/shard_map/ppermute | solution.py:198
  99.0 9.2 %collective-permute-start.4 = (bf16[192,512]{1,0:T(8,128)(2,1)S(1)}, bf16[192,512]{1,0:T(8,128)(2,1)S(1)}, u32[]{:S(2)}, u32[]{:S(2)}) collective-permute-start(bf16[192,512]{1,0:T(8,128)(2,1)S(1)} %shard_map.79.refs_0_), channel_id=1, source_target_pairs={{0,1},{1,0},{2,3},{3,2},{4,5},{5,4},{6,7},{7,6},{8,9},{9,8},{10,11... | collective-permute-start | bytes 589832 | tf_op jit(solution)/shard_map/ppermute | solution.py:198
  105.1 4.2 %collective-permute-start.6 = (bf16[192,512]{1,0:T(8,128)(2,1)S(1)}, bf16[192,512]{1,0:T(8,128)(2,1)S(1)}, u32[]{:S(2)}, u32[]{:S(2)}) collective-permute-start(bf16[192,512]{1,0:T(8,128)(2,1)S(1)} %collective-permute-done.5.refs_2_), channel_id=1, source_target_pairs={{0,1},{1,0},{2,3},{3,2},{4,5},{5,4},{6,7},{7,6},{8,9},{9,8},{10,11... | collective-permute-start | bytes 589832 | tf_op jit(solution)/shard_map/ppermute | solution.py:198
  111.3 46.3 %copy-start.11 = (bf16[4,4096]{1,0:T(4,128)(2,1)S(1)}, bf16[4,4096]{1,0:T(4,128)(2,1)}, u32[]{:S(2)}) copy-start(bf16[4,4096]{1,0:T(4,128)(2,1)} %resid_ref.1) | copy-start | bytes 98308
  111.3 31.6 %all-to-all-start.2 = ((bf16[32,16,1024]{2,1,0:T(8,128)(2,1)}), bf16[32,16,1024]{2,1,0:T(8,128)(2,1)S(1)}, u32[]{:S(2)}, u32[]{:S(2)}) async-start(bf16[32,16,1024]{2,1,0:T(8,128)(2,1)} %bitcast.5), calls=%async_computation.2 | async-start | bytes 2097152 | tf_op jit(solution)/shard_map/all_to_all | solution.py:204

commit v6 on v5

--- a/solution.py
+++ b/solution.py
@@ -146,11 +146,15 @@
     refs[-1][...] = jnp.zeros_like(refs[-1])
 
 
-def down_kernel(*refs):
-    acts, down_ref, others, out_ref = refs[:GROUP], refs[GROUP], refs[GROUP + 1 : 2 * GROUP], refs[-1]
-    downs = [columns(down_ref, own_part(), GROUP)] + [down[...] for down in others]
-    act = jnp.concatenate([act[...] for act in acts], axis=0)
-    out_ref[...] = dot_tn(act, jnp.concatenate(downs, axis=0)).astype(jnp.bfloat16)
+def near_kernel(own_act, core_act, down_ref, core_ref, token_ref, out_ref):
+    act = jnp.concatenate([own_act[...], core_act[...]], axis=0)
+    out_ref[...] = dot_tn(act, jnp.concatenate([columns(down_ref, own_part(), GROUP), core_ref[...]], axis=0))
+
+
+def far_kernel(near_ref, z_act, diag_act, z_ref, diag_ref, out_ref):
+    act = jnp.concatenate([z_act[...], diag_act[...]], axis=0)
+    total = near_ref[...] + dot_tn(act, jnp.concatenate([z_ref[...], diag_ref[...]], axis=0))
+    out_ref[...] = total.astype(jnp.bfloat16)
 
 
 def combine_kernel(weight_ref, in_ref, out_ref):
@@ -236,7 +240,8 @@
     act = call(half_act_kernel, bf16(units, rows), other, gate, up, gate_w, up_w)
     from_z = swap(act, 2)
     acts = [act, swap(act, 1), from_z, swap(from_z, 1)]
-    value = call(down_kernel, bf16(rows, part), *acts, down_w, *downs, token)
+    near = call(near_kernel, f32(rows, part), acts[0], acts[1], down_w, downs[0], token)
+    value = call(far_kernel, bf16(rows, part), near, acts[2], acts[3], downs[1], downs[2])
     routed = call(combine_kernel, bf16(tok_row, part), weights, over_dp(value))
     shares = over_expert(routed.reshape(col_count, tok_dev, part))
     return call(final_kernel, bf16(tok_dev, width), hidden_in, shares)

time: 159 us -> 159 us (level)
    pallas_call x8 -> x9, Pallas kernels: 8.65 us -> 9.11 us  [call(): pl.pallas_call(kernel, out_shape=out_shape, in_specs=[VMEM] * len(args),...]
  transfers between devices with their start and end apart: 9 -> 9, of which waited for: 7 -> 7; matrix products, arithmetic and copies ran while one was open for 0% -> 0% of each run, Pallas kernels for 2% -> 3%
where the time goes in v6:
time: 159 us; the launch traced here: 158 us
  waiting for transfers between devices  70.6 us (44%)
  blocking collectives  38.2 us (24%)
  starting transfers between devices  33.2 us (21%)
  Pallas kernels  10.8 us (7%)
  local copies, waits for them, and re-layouts  5.11 us (3%)
    all_to_all x2, waiting for transfers between devices, over_dp(): lax.all_to_all(x.reshape(dp_count, per, x.shape[1]), 'dp', split_axis=0,...  50.1 us
    all_to_all x2, blocking collectives, over_expert(): return lax.all_to_all(x, 'expert', split_axis=0, concat_axis=0, tiled=True)  38.2 us
    ppermute x7, waiting for transfers between devices, swap(): return lax.ppermute(x, 'expert', [(i, i ^ k) for i in range(col_count)])  20.5 us
    ppermute x7, starting transfers between devices, swap(): return lax.ppermute(x, 'expert', [(i, i ^ k) for i in range(col_count)])  17.9 us
    all_to_all x2, starting transfers between devices, over_dp(): lax.all_to_all(x.reshape(dp_count, per, x.shape[1]), 'dp', split_axis=0,...  15.3 us
    pallas_call x9, Pallas kernels, call(): pl.pallas_call(kernel, out_shape=out_shape, in_specs=[VMEM] * len(args),...  9.11 us
    unnamed x24, local copies, waits for them, and re-layouts  4.98 us
  transfers between devices with their start and end apart: 9, of which 7 were waited for; matrix products, arithmetic and copies ran while one was open for 0% of the time, Pallas kernels for 3%

profile of v6, /device:TPU:1, one launch (start us, length us, event | category | flops | bytes accessed | tf_op | source)
XLA Modules:
  0.0 158.1 jit_solution(772442051982472811)
XLA Ops:
  0.0 1.7 %shard_map.73 = bf16[16,4,2176]{2,1,0:T(4,128)(2,1)} custom-call(bf16[4,4096]{1,0:T(4,128)(2,1)} %resid_ref.1, bf16[4096]{0:T(1024)(128)(2,1)} %gain_hbm.1, s32[4,8]{1,0:T(4,128)} %ids_hbm.1, bf16[4,8]{1,0:T(4,128)(2,1)} %share_hbm.1), custom_call_target="tpu_custom_call" | custom-call | tf_op jit(solution)/shard_map/pallas_call | solution.py:214
  1.7 23.9 %all_to_all.20 = bf16[16,4,2176]{2,1,0:T(4,128)(2,1)S(1)} all-to-all(bf16[16,4,2176]{2,1,0:T(4,128)(2,1)} %shard_map.73), channel_id=1, replica_groups=mesh['dp'=32,'expert'=16] {'expert'}, dimensions={0} | all-to-all | bytes 557056 | tf_op jit(solution)/shard_map/all_to_all | solution.py:212
  25.6 1.1 shard_map.75
  26.7 1.3 copy-done.2
  28.0 10.1 %all-to-all-start.1 = ((bf16[32,16,2048]{2,1,0:T(8,128)(2,1)}), bf16[32,16,2048]{2,1,0:T(8,128)(2,1)}, u32[]{:S(2)}, u32[]{:S(2)}) async-start(bf16[32,16,2048]{2,1,0:T(8,128)(2,1)} %bitcast.13), calls=%async_computation.1 | async-start | bytes 4194304 | tf_op jit(solution)/shard_map/all_to_all | solution.py:208
  38.1 1.4 copy-done.3
  39.6 1.9 %collective-permute-start = (bf16[192,1024]{1,0:T(8,128)(2,1)S(1)}, bf16[192,1024]{1,0:T(8,128)(2,1)S(1)}, u32[]{:S(2)}, u32[]{:S(2)}) collective-permute-start(bf16[192,1024]{1,0:T(8,128)(2,1)S(1)} %get-tuple-element.12), channel_id=1, source_target_pairs={{0,1},{1,0},{2,3},{3,2},{4,5},{5,4},{6,7},{7,6},{8,9},{9,8},{10,11... | collective-permute-start | bytes 1179656 | tf_op jit(solution)/shard_map/ppermute | solution.py:202
  41.5 1.9 %collective-permute-start.1 = (bf16[192,1024]{1,0:T(8,128)(2,1)S(1)}, bf16[192,1024]{1,0:T(8,128)(2,1)S(1)}, u32[]{:S(2)}, u32[]{:S(2)}) collective-permute-start(bf16[192,1024]{1,0:T(8,128)(2,1)S(1)} %get-tuple-element.13), channel_id=1, source_target_pairs={{0,2},{1,3},{2,0},{3,1},{4,6},{5,7},{6,4},{7,5},{8,10},{9,11},{10,... | collective-permute-start | bytes 1179656 | tf_op jit(solution)/shard_map/ppermute | solution.py:202
  43.4 4.0 %collective-permute-start.2 = (bf16[192,1024]{1,0:T(8,128)(2,1)S(1)}, bf16[192,1024]{1,0:T(8,128)(2,1)S(1)}, u32[]{:S(2)}, u32[]{:S(2)}) collective-permute-start(bf16[192,1024]{1,0:T(8,128)(2,1)S(1)} %get-tuple-element.14), channel_id=1, source_target_pairs={{0,3},{1,2},{2,1},{3,0},{4,7},{5,6},{6,5},{7,4},{8,11},{9,10},{10,... | collective-permute-start | bytes 1179656 | tf_op jit(solution)/shard_map/ppermute | solution.py:202
  47.5 6.2 %collective-permute-done.1.refs_1_.z_ref = bf16[192,1024]{1,0:T(8,128)(2,1)S(1)} collective-permute-done((bf16[192,1024]{1,0:T(8,128)(2,1)S(1)}, bf16[192,1024]{1,0:T(8,128)(2,1)S(1)}, u32[]{:S(2)}, u32[]{:S(2)}) %collective-permute-start.1) | collective-permute-done | bytes 393248 | tf_op jit(solution)/shard_map/ppermute | solution.py:202
  53.7 9.4 %collective-permute-done.2.refs_2_.diag_ref = bf16[192,1024]{1,0:T(8,128)(2,1)S(1)} collective-permute-done((bf16[192,1024]{1,0:T(8,128)(2,1)S(1)}, bf16[192,1024]{1,0:T(8,128)(2,1)S(1)}, u32[]{:S(2)}, u32[]{:S(2)}) %collective-permute-start.2) | collective-permute-done | bytes 393248 | tf_op jit(solution)/shard_map/ppermute | solution.py:202
  65.3 24.2 %all-to-all-done.1 = bf16[32,16,2048]{2,1,0:T(8,128)(2,1)} async-done(((bf16[32,16,2048]{2,1,0:T(8,128)(2,1)}), bf16[32,16,2048]{2,1,0:T(8,128)(2,1)}, u32[]{:S(2)}, u32[]{:S(2)}) %all-to-all-start.1) | async-done | bytes 2097184 | tf_op jit(solution)/shard_map/all_to_all | solution.py:208
  89.5 2.5 %collective-permute-start.3 = (bf16[512,2048]{1,0:T(8,128)(2,1)}, bf16[512,2048]{1,0:T(8,128)(2,1)S(1)}, u32[]{:S(2)}, u32[]{:S(2)}) collective-permute-start(bf16[512,2048]{1,0:T(8,128)(2,1)} %bitcast.1.own_ref), channel_id=1, source_target_pairs={{0,1},{1,0},{2,3},{3,2},{4,5},{5,4},{6,7},{7,6},{8,9},{9,8},{10,11... | collective-permute-start | bytes 6291464 | tf_op jit(solution)/shard_map/ppermute | solution.py:202
  92.1 3.1 %shard_map.78 = (f32[192,512]{1,0:T(8,128)S(1)}, f32[192,512]{1,0:T(8,128)S(1)}) custom-call(bf16[512,2048]{1,0:T(8,128)(2,1)} %bitcast.1.own_ref, bf16[192,4096]{1,0:T(8,128)(2,1)S(1)} %bitcast.8, bf16[192,4096]{1,0:T(8,128)(2,1)S(1)} %bitcast.11), custom_call_target="tpu_custom_call" | custom-call | tf_op jit(solution)/shard_map/pallas_call | solution.py:175
  95.2 0.9 collective-permute-done.3.other_ref
  96.1 1.0 shard_map.79.own_act
  97.1 2.1 %collective-permute-start.5 = (bf16[192,512]{1,0:T(8,128)(2,1)S(1)}, bf16[192,512]{1,0:T(8,128)(2,1)S(1)}, u32[]{:S(2)}, u32[]{:S(2)}) collective-permute-start(bf16[192,512]{1,0:T(8,128)(2,1)S(1)} %shard_map.79.own_act), channel_id=1, source_target_pairs={{0,2},{1,3},{2,0},{3,1},{4,6},{5,7},{6,4},{7,5},{8,10},{9,11},{10,... | collective-permute-start | bytes 589832 | tf_op jit(solution)/shard_map/ppermute | solution.py:202
  99.2 2.3 %collective-permute-start.4 = (bf16[192,512]{1,0:T(8,128)(2,1)S(1)}, bf16[192,512]{1,0:T(8,128)(2,1)S(1)}, u32[]{:S(2)}, u32[]{:S(2)}) collective-permute-start(bf16[192,512]{1,0:T(8,128)(2,1)S(1)} %shard_map.79.own_act), channel_id=1, source_target_pairs={{0,1},{1,0},{2,3},{3,2},{4,5},{5,4},{6,7},{7,6},{8,9},{9,8},{10,11... | collective-permute-start | bytes 589832 | tf_op jit(solution)/shard_map/ppermute | solution.py:202
  101.5 3.8 %collective-permute-done.5.z_act = bf16[192,512]{1,0:T(8,128)(2,1)S(1)} collective-permute-done((bf16[192,512]{1,0:T(8,128)(2,1)S(1)}, bf16[192,512]{1,0:T(8,128)(2,1)S(1)}, u32[]{:S(2)}, u32[]{:S(2)}) %collective-permute-start.5) | collective-permute-done | bytes 196640 | tf_op jit(solution)/shard_map/ppermute | solution.py:202
  105.3 3.1 %collective-permute-start.6 = (bf16[192,512]{1,0:T(8,128)(2,1)S(1)}, bf16[192,512]{1,0:T(8,128)(2,1)S(1)}, u32[]{:S(2)}, u32[]{:S(2)}) collective-permute-start(bf16[192,512]{1,0:T(8,128)(2,1)S(1)} %collective-permute-done.5.z_act), channel_id=1, source_target_pairs={{0,1},{1,0},{2,3},{3,2},{4,5},{5,4},{6,7},{7,6},{8,9},{9,8},{10,11... | collective-permute-start | bytes 589832 | tf_op jit(solution)/shard_map/ppermute | solution.py:202
  109.4 1.7 %shard_map.81 = bf16[512,1024]{1,0:T(8,128)(2,1)} custom-call(f32[512,1024]{1,0:T(8,128)S(1)} %shard_map.80.near_ref, bf16[192,512]{1,0:T(8,128)(2,1)S(1)} %collective-permute-done.5.z_act, bf16[192,512]{1,0:T(8,128)(2,1)S(1)} %collective-permute-done.6.diag_act, bf16[192,1024]{1,0:T(8,128)(2,1)S(1)} %copy-done.6, bf16[192,1024]{1,0:T(8,128)(2,1)S(1)} %copy-done.10), custom_call_target="tpu_custom_call" | custom-call | tf_op jit(solution)/shard_map/pallas_call | solution.py:175
  111.2 5.3 %all-to-all-start.2 = ((bf16[32,16,1024]{2,1,0:T(8,128)(2,1)}), bf16[32,16,1024]{2,1,0:T(8,128)(2,1)S(1)}, u32[]{:S(2)}, u32[]{:S(2)}) async-start(bf16[32,16,1024]{2,1,0:T(8,128)(2,1)} %bitcast.5), calls=%async_computation.2 | async-start | bytes 2097152 | tf_op jit(solution)/shard_map/all_to_all | solution.py:208
  116.8 25.9 %all-to-all-done.2 = bf16[32,16,1024]{2,1,0:T(8,128)(2,1)S(1)} async-done(((bf16[32,16,1024]{2,1,0:T(8,128)(2,1)}), bf16[32,16,1024]{2,1,0:T(8,128)(2,1)S(1)}, u32[]{:S(2)}, u32[]{:S(2)}) %all-to-all-start.2) | async-done | bytes 1048608 | tf_op jit(solution)/shard_map/all_to_all | solution.py:208
  143.1 14.3 %all_to_all.21.got_ref = bf16[16,4,1024]{2,1,0:T(4,128)(2,1)S(1)} all-to-all(bf16[16,4,1024]{2,1,0:T(4,128)(2,1)S(1)} %reshape.35), channel_id=1, replica_groups=mesh['dp'=32,'expert'=16] {'expert'}, dimensions={0} | all-to-all | bytes 262144 | tf_op jit(solution)/shard_map/all_to_all | solution.py:212
  (33 shorter events, 4.9 us)
Async XLA Ops:
  26.7 1.3 copy-start.2
  28.0 35.1 %copy-start = (bf16[1,192,4096]{2,1,0:T(8,128)(2,1)S(1)}, bf16[1,192,4096]{2,1,0:T(8,128)(2,1)}, u32[]{:S(2)}) copy-start(bf16[1,192,4096]{2,1,0:T(8,128)(2,1)} %param.11) | copy-start | bytes 4718596
  28.0 35.1 %copy-start.1 = (bf16[1,192,4096]{2,1,0:T(8,128)(2,1)S(1)}, bf16[1,192,4096]{2,1,0:T(8,128)(2,1)}, u32[]{:S(2)}) copy-start(bf16[1,192,4096]{2,1,0:T(8,128)(2,1)} %param.12) | copy-start | bytes 4718596
  28.0 61.5 %all-to-all-start.1 = ((bf16[32,16,2048]{2,1,0:T(8,128)(2,1)}), bf16[32,16,2048]{2,1,0:T(8,128)(2,1)}, u32[]{:S(2)}, u32[]{:S(2)}) async-start(bf16[32,16,2048]{2,1,0:T(8,128)(2,1)} %bitcast.13), calls=%async_computation.1 | async-start | bytes 4194304 | tf_op jit(solution)/shard_map/all_to_all | solution.py:208
  38.1 1.4 copy-start.3
  39.6 7.9 %collective-permute-start = (bf16[192,1024]{1,0:T(8,128)(2,1)S(1)}, bf16[192,1024]{1,0:T(8,128)(2,1)S(1)}, u32[]{:S(2)}, u32[]{:S(2)}) collective-permute-start(bf16[192,1024]{1,0:T(8,128)(2,1)S(1)} %get-tuple-element.12), channel_id=1, source_target_pairs={{0,1},{1,0},{2,3},{3,2},{4,5},{5,4},{6,7},{7,6},{8,9},{9,8},{10,11... | collective-permute-start | bytes 1179656 | tf_op jit(solution)/shard_map/ppermute | solution.py:202
  41.5 12.2 %collective-permute-start.1 = (bf16[192,1024]{1,0:T(8,128)(2,1)S(1)}, bf16[192,1024]{1,0:T(8,128)(2,1)S(1)}, u32[]{:S(2)}, u32[]{:S(2)}) collective-permute-start(bf16[192,1024]{1,0:T(8,128)(2,1)S(1)} %get-tuple-element.13), channel_id=1, source_target_pairs={{0,2},{1,3},{2,0},{3,1},{4,6},{5,7},{6,4},{7,5},{8,10},{9,11},{10,... | collective-permute-start | bytes 1179656 | tf_op jit(solution)/shard_map/ppermute | solution.py:202
  43.4 19.6 %collective-permute-start.2 = (bf16[192,1024]{1,0:T(8,128)(2,1)S(1)}, bf16[192,1024]{1,0:T(8,128)(2,1)S(1)}, u32[]{:S(2)}, u32[]{:S(2)}) collective-permute-start(bf16[192,1024]{1,0:T(8,128)(2,1)S(1)} %get-tuple-element.14), channel_id=1, source_target_pairs={{0,3},{1,2},{2,1},{3,0},{4,7},{5,6},{6,5},{7,4},{8,11},{9,10},{10,... | collective-permute-start | bytes 1179656 | tf_op jit(solution)/shard_map/ppermute | solution.py:202
  63.1 0.8 copy-start.5
  63.8 0.8 copy-start.7
  64.6 0.7 copy-start.9
  89.5 6.5 %collective-permute-start.3 = (bf16[512,2048]{1,0:T(8,128)(2,1)}, bf16[512,2048]{1,0:T(8,128)(2,1)S(1)}, u32[]{:S(2)}, u32[]{:S(2)}) collective-permute-start(bf16[512,2048]{1,0:T(8,128)(2,1)} %bitcast.1.own_ref), channel_id=1, source_target_pairs={{0,1},{1,0},{2,3},{3,2},{4,5},{5,4},{6,7},{7,6},{8,9},{9,8},{10,11... | collective-permute-start | bytes 6291464 | tf_op jit(solution)/shard_map/ppermute | solution.py:202
  96.1 12.3 %copy-start.4 = (bf16[1,192,4096]{2,1,0:T(8,128)(2,1)S(1)}, bf16[1,192,4096]{2,1,0:T(8,128)(2,1)}, u32[]{:S(2)}) copy-start(bf16[1,192,4096]{2,1,0:T(8,128)(2,1)} %param.13) | copy-start | bytes 4718596
  96.1 12.3 %copy-start.8 = (bf16[192,1024]{1,0:T(8,128)(2,1)S(1)}, bf16[192,1024]{1,0:T(8,128)(2,1)}, u32[]{:S(2)}) copy-start(bf16[192,1024]{1,0:T(8,128)(2,1)} %copy-done.7) | copy-start | bytes 1179652
  97.1 12.3 %copy-start.6 = (bf16[192,1024]{1,0:T(8,128)(2,1)S(1)}, bf16[192,1024]{1,0:T(8,128)(2,1)}, u32[]{:S(2)}) copy-start(bf16[192,1024]{1,0:T(8,128)(2,1)} %copy-done.5) | copy-start | bytes 1179652
  97.1 12.3 %copy-start.10 = (bf16[192,1024]{1,0:T(8,128)(2,1)S(1)}, bf16[192,1024]{1,0:T(8,128)(2,1)}, u32[]{:S(2)}) copy-start(bf16[192,1024]{1,0:T(8,128)(2,1)} %copy-done.9) | copy-start | bytes 1179652
  97.1 8.1 %collective-permute-start.5 = (bf16[192,512]{1,0:T(8,128)(2,1)S(1)}, bf16[192,512]{1,0:T(8,128)(2,1)S(1)}, u32[]{:S(2)}, u32[]{:S(2)}) collective-permute-start(bf16[192,512]{1,0:T(8,128)(2,1)S(1)} %shard_map.79.own_act), channel_id=1, source_target_pairs={{0,2},{1,3},{2,0},{3,1},{4,6},{5,7},{6,4},{7,5},{8,10},{9,11},{10,... | collective-permute-start | bytes 589832 | tf_op jit(solution)/shard_map/ppermute | solution.py:202
  99.2 9.2 %collective-permute-start.4 = (bf16[192,512]{1,0:T(8,128)(2,1)S(1)}, bf16[192,512]{1,0:T(8,128)(2,1)S(1)}, u32[]{:S(2)}, u32[]{:S(2)}) collective-permute-start(bf16[192,512]{1,0:T(8,128)(2,1)S(1)} %shard_map.79.own_act), channel_id=1, source_target_pairs={{0,1},{1,0},{2,3},{3,2},{4,5},{5,4},{6,7},{7,6},{8,9},{9,8},{10,11... | collective-permute-start | bytes 589832 | tf_op jit(solution)/shard_map/ppermute | solution.py:202
  105.3 4.2 %collective-permute-start.6 = (bf16[192,512]{1,0:T(8,128)(2,1)S(1)}, bf16[192,512]{1,0:T(8,128)(2,1)S(1)}, u32[]{:S(2)}, u32[]{:S(2)}) collective-permute-start(bf16[192,512]{1,0:T(8,128)(2,1)S(1)} %collective-permute-done.5.z_act), channel_id=1, source_target_pairs={{0,1},{1,0},{2,3},{3,2},{4,5},{5,4},{6,7},{7,6},{8,9},{9,8},{10,11... | collective-permute-start | bytes 589832 | tf_op jit(solution)/shard_map/ppermute | solution.py:202
  111.2 46.2 %copy-start.11 = (bf16[4,4096]{1,0:T(4,128)(2,1)S(1)}, bf16[4,4096]{1,0:T(4,128)(2,1)}, u32[]{:S(2)}) copy-start(bf16[4,4096]{1,0:T(4,128)(2,1)} %resid_ref.1) | copy-start | bytes 98308
  111.2 31.6 %all-to-all-start.2 = ((bf16[32,16,1024]{2,1,0:T(8,128)(2,1)}), bf16[32,16,1024]{2,1,0:T(8,128)(2,1)S(1)}, u32[]{:S(2)}, u32[]{:S(2)}) async-start(bf16[32,16,1024]{2,1,0:T(8,128)(2,1)} %bitcast.5), calls=%async_computation.2 | async-start | bytes 2097152 | tf_op jit(solution)/shard_map/all_to_all | solution.py:208

commit v7 on v6

--- a/solution.py
+++ b/solution.py
@@ -38,24 +38,27 @@
     ]
     for copy in copies:
         copy.start()
-    for copy in copies:
+    for copy in copies[2:]:
         copy.wait()
     part = x_ref.shape[1] // 2
-    x = x_ref[...].astype(jnp.float32)
-    inv = lax.rsqrt(jnp.mean(x * x, axis=1, keepdims=True) + 1e-06)
-    normed = (x * inv * gain_ref[...].astype(jnp.float32)[None, :]).astype(jnp.bfloat16)
     ids = ids_ref[...].astype(jnp.float32)
     share = share_ref[...].astype(jnp.float32)
-    lane = lax.broadcasted_iota(jnp.int32, (x.shape[0], META), 1)
-    meta = jnp.zeros((x.shape[0], META), jnp.float32)
+    lane = lax.broadcasted_iota(jnp.int32, (x_ref.shape[0], META), 1)
+    meta = jnp.zeros((x_ref.shape[0], META), jnp.float32)
     for k in range(TOP):
         meta = jnp.where(lane == k, ids[:, k : k + 1], meta)
         meta = jnp.where(lane == TOP + k, share[:, k : k + 1], meta)
     meta = meta.astype(jnp.bfloat16)
     for j in range(out_ref.shape[0]):
+        out_ref[j, :, part:] = meta
+    for copy in copies[:2]:
+        copy.wait()
+    x = x_ref[...].astype(jnp.float32)
+    inv = lax.rsqrt(jnp.mean(x * x, axis=1, keepdims=True) + 1e-06)
+    normed = (x * inv * gain_ref[...].astype(jnp.float32)[None, :]).astype(jnp.bfloat16)
+    for j in range(out_ref.shape[0]):
         half = j % 2
         out_ref[j, :, :part] = normed[:, half * part : (half + 1) * part]
-        out_ref[j, :, part:] = meta
 
 
 def ranks(meta):

time: 159 us -> 159 us (level)
  no operation moved by 1% of the time
where the time goes in v7:
time: 159 us; the launch traced here: 158 us
  waiting for transfers between devices  70.6 us (44%)
  blocking collectives  38.2 us (24%)
  starting transfers between devices  33.2 us (21%)
  Pallas kernels  10.8 us (7%)
  local copies, waits for them, and re-layouts  5.11 us (3%)
    all_to_all x2, waiting for transfers between devices, over_dp(): lax.all_to_all(x.reshape(dp_count, per, x.shape[1]), 'dp', split_axis=0,...  50.1 us
    all_to_all x2, blocking collectives, over_expert(): return lax.all_to_all(x, 'expert', split_axis=0, concat_axis=0, tiled=True)  38.2 us
    ppermute x7, waiting for transfers between devices, swap(): return lax.ppermute(x, 'expert', [(i, i ^ k) for i in range(col_count)])  20.5 us
    ppermute x7, starting transfers between devices, swap(): return lax.ppermute(x, 'expert', [(i, i ^ k) for i in range(col_count)])  17.8 us
    all_to_all x2, starting transfers between devices, over_dp(): lax.all_to_all(x.reshape(dp_count, per, x.shape[1]), 'dp', split_axis=0,...  15.3 us
    pallas_call x9, Pallas kernels, call(): pl.pallas_call(kernel, out_shape=out_shape, in_specs=[VMEM] * len(args),...  9.12 us
    unnamed x24, local copies, waits for them, and re-layouts  4.98 us
  transfers between devices with their start and end apart: 9, of which 7 were waited for; matrix products, arithmetic and copies ran while one was open for 0% of the time, Pallas kernels for 3%

profile of v7, /device:TPU:1, one launch (start us, length us, event | category | flops | bytes accessed | tf_op | source)
XLA Modules:
  0.0 158.1 jit_solution(15375610019910938834)
XLA Ops:
  0.0 1.7 %shard_map.73 = bf16[16,4,2176]{2,1,0:T(4,128)(2,1)} custom-call(bf16[4,4096]{1,0:T(4,128)(2,1)} %resid_ref.1, bf16[4096]{0:T(1024)(128)(2,1)} %gain_hbm.1, s32[4,8]{1,0:T(4,128)} %ids_hbm.1, bf16[4,8]{1,0:T(4,128)(2,1)} %share_hbm.1), custom_call_target="tpu_custom_call" | custom-call | tf_op jit(solution)/shard_map/pallas_call | solution.py:217
  1.7 23.9 %all_to_all.20 = bf16[16,4,2176]{2,1,0:T(4,128)(2,1)S(1)} all-to-all(bf16[16,4,2176]{2,1,0:T(4,128)(2,1)} %shard_map.73), channel_id=1, replica_groups=mesh['dp'=32,'expert'=16] {'expert'}, dimensions={0} | all-to-all | bytes 557056 | tf_op jit(solution)/shard_map/all_to_all | solution.py:215
  25.7 1.1 shard_map.75
  26.8 1.3 copy-done.2
  28.1 10.1 %all-to-all-start.1 = ((bf16[32,16,2048]{2,1,0:T(8,128)(2,1)}), bf16[32,16,2048]{2,1,0:T(8,128)(2,1)}, u32[]{:S(2)}, u32[]{:S(2)}) async-start(bf16[32,16,2048]{2,1,0:T(8,128)(2,1)} %bitcast.13), calls=%async_computation.1 | async-start | bytes 4194304 | tf_op jit(solution)/shard_map/all_to_all | solution.py:211
  38.2 1.4 copy-done.3
  39.6 1.9 %collective-permute-start = (bf16[192,1024]{1,0:T(8,128)(2,1)S(1)}, bf16[192,1024]{1,0:T(8,128)(2,1)S(1)}, u32[]{:S(2)}, u32[]{:S(2)}) collective-permute-start(bf16[192,1024]{1,0:T(8,128)(2,1)S(1)} %get-tuple-element.12), channel_id=1, source_target_pairs={{0,1},{1,0},{2,3},{3,2},{4,5},{5,4},{6,7},{7,6},{8,9},{9,8},{10,11... | collective-permute-start | bytes 1179656 | tf_op jit(solution)/shard_map/ppermute | solution.py:205
  41.6 1.9 %collective-permute-start.1 = (bf16[192,1024]{1,0:T(8,128)(2,1)S(1)}, bf16[192,1024]{1,0:T(8,128)(2,1)S(1)}, u32[]{:S(2)}, u32[]{:S(2)}) collective-permute-start(bf16[192,1024]{1,0:T(8,128)(2,1)S(1)} %get-tuple-element.13), channel_id=1, source_target_pairs={{0,2},{1,3},{2,0},{3,1},{4,6},{5,7},{6,4},{7,5},{8,10},{9,11},{10,... | collective-permute-start | bytes 1179656 | tf_op jit(solution)/shard_map/ppermute | solution.py:205
  43.5 4.0 %collective-permute-start.2 = (bf16[192,1024]{1,0:T(8,128)(2,1)S(1)}, bf16[192,1024]{1,0:T(8,128)(2,1)S(1)}, u32[]{:S(2)}, u32[]{:S(2)}) collective-permute-start(bf16[192,1024]{1,0:T(8,128)(2,1)S(1)} %get-tuple-element.14), channel_id=1, source_target_pairs={{0,3},{1,2},{2,1},{3,0},{4,7},{5,6},{6,5},{7,4},{8,11},{9,10},{10,... | collective-permute-start | bytes 1179656 | tf_op jit(solution)/shard_map/ppermute | solution.py:205
  47.5 6.2 %collective-permute-done.1.refs_1_.z_ref = bf16[192,1024]{1,0:T(8,128)(2,1)S(1)} collective-permute-done((bf16[192,1024]{1,0:T(8,128)(2,1)S(1)}, bf16[192,1024]{1,0:T(8,128)(2,1)S(1)}, u32[]{:S(2)}, u32[]{:S(2)}) %collective-permute-start.1) | collective-permute-done | bytes 393248 | tf_op jit(solution)/shard_map/ppermute | solution.py:205
  53.7 9.4 %collective-permute-done.2.refs_2_.diag_ref = bf16[192,1024]{1,0:T(8,128)(2,1)S(1)} collective-permute-done((bf16[192,1024]{1,0:T(8,128)(2,1)S(1)}, bf16[192,1024]{1,0:T(8,128)(2,1)S(1)}, u32[]{:S(2)}, u32[]{:S(2)}) %collective-permute-start.2) | collective-permute-done | bytes 393248 | tf_op jit(solution)/shard_map/ppermute | solution.py:205
  65.4 24.2 %all-to-all-done.1 = bf16[32,16,2048]{2,1,0:T(8,128)(2,1)} async-done(((bf16[32,16,2048]{2,1,0:T(8,128)(2,1)}), bf16[32,16,2048]{2,1,0:T(8,128)(2,1)}, u32[]{:S(2)}, u32[]{:S(2)}) %all-to-all-start.1) | async-done | bytes 2097184 | tf_op jit(solution)/shard_map/all_to_all | solution.py:211
  89.6 2.5 %collective-permute-start.3 = (bf16[512,2048]{1,0:T(8,128)(2,1)}, bf16[512,2048]{1,0:T(8,128)(2,1)S(1)}, u32[]{:S(2)}, u32[]{:S(2)}) collective-permute-start(bf16[512,2048]{1,0:T(8,128)(2,1)} %bitcast.1.own_ref), channel_id=1, source_target_pairs={{0,1},{1,0},{2,3},{3,2},{4,5},{5,4},{6,7},{7,6},{8,9},{9,8},{10,11... | collective-permute-start | bytes 6291464 | tf_op jit(solution)/shard_map/ppermute | solution.py:205
  92.1 3.1 %shard_map.78 = (f32[192,512]{1,0:T(8,128)S(1)}, f32[192,512]{1,0:T(8,128)S(1)}) custom-call(bf16[512,2048]{1,0:T(8,128)(2,1)} %bitcast.1.own_ref, bf16[192,4096]{1,0:T(8,128)(2,1)S(1)} %bitcast.8, bf16[192,4096]{1,0:T(8,128)(2,1)S(1)} %bitcast.11), custom_call_target="tpu_custom_call" | custom-call | tf_op jit(solution)/shard_map/pallas_call | solution.py:178
  95.3 0.9 collective-permute-done.3.other_ref
  96.1 1.0 shard_map.79.own_act
  97.2 2.1 %collective-permute-start.5 = (bf16[192,512]{1,0:T(8,128)(2,1)S(1)}, bf16[192,512]{1,0:T(8,128)(2,1)S(1)}, u32[]{:S(2)}, u32[]{:S(2)}) collective-permute-start(bf16[192,512]{1,0:T(8,128)(2,1)S(1)} %shard_map.79.own_act), channel_id=1, source_target_pairs={{0,2},{1,3},{2,0},{3,1},{4,6},{5,7},{6,4},{7,5},{8,10},{9,11},{10,... | collective-permute-start | bytes 589832 | tf_op jit(solution)/shard_map/ppermute | solution.py:205
  99.3 2.3 %collective-permute-start.4 = (bf16[192,512]{1,0:T(8,128)(2,1)S(1)}, bf16[192,512]{1,0:T(8,128)(2,1)S(1)}, u32[]{:S(2)}, u32[]{:S(2)}) collective-permute-start(bf16[192,512]{1,0:T(8,128)(2,1)S(1)} %shard_map.79.own_act), channel_id=1, source_target_pairs={{0,1},{1,0},{2,3},{3,2},{4,5},{5,4},{6,7},{7,6},{8,9},{9,8},{10,11... | collective-permute-start | bytes 589832 | tf_op jit(solution)/shard_map/ppermute | solution.py:205
  101.5 3.8 %collective-permute-done.5.z_act = bf16[192,512]{1,0:T(8,128)(2,1)S(1)} collective-permute-done((bf16[192,512]{1,0:T(8,128)(2,1)S(1)}, bf16[192,512]{1,0:T(8,128)(2,1)S(1)}, u32[]{:S(2)}, u32[]{:S(2)}) %collective-permute-start.5) | collective-permute-done | bytes 196640 | tf_op jit(solution)/shard_map/ppermute | solution.py:205
  105.3 3.1 %collective-permute-start.6 = (bf16[192,512]{1,0:T(8,128)(2,1)S(1)}, bf16[192,512]{1,0:T(8,128)(2,1)S(1)}, u32[]{:S(2)}, u32[]{:S(2)}) collective-permute-start(bf16[192,512]{1,0:T(8,128)(2,1)S(1)} %collective-permute-done.5.z_act), channel_id=1, source_target_pairs={{0,1},{1,0},{2,3},{3,2},{4,5},{5,4},{6,7},{7,6},{8,9},{9,8},{10,11... | collective-permute-start | bytes 589832 | tf_op jit(solution)/shard_map/ppermute | solution.py:205
  109.5 1.7 %shard_map.81 = bf16[512,1024]{1,0:T(8,128)(2,1)} custom-call(f32[512,1024]{1,0:T(8,128)S(1)} %shard_map.80.near_ref, bf16[192,512]{1,0:T(8,128)(2,1)S(1)} %collective-permute-done.5.z_act, bf16[192,512]{1,0:T(8,128)(2,1)S(1)} %collective-permute-done.6.diag_act, bf16[192,1024]{1,0:T(8,128)(2,1)S(1)} %copy-done.6, bf16[192,1024]{1,0:T(8,128)(2,1)S(1)} %copy-done.10), custom_call_target="tpu_custom_call" | custom-call | tf_op jit(solution)/shard_map/pallas_call | solution.py:178
  111.2 5.3 %all-to-all-start.2 = ((bf16[32,16,1024]{2,1,0:T(8,128)(2,1)}), bf16[32,16,1024]{2,1,0:T(8,128)(2,1)S(1)}, u32[]{:S(2)}, u32[]{:S(2)}) async-start(bf16[32,16,1024]{2,1,0:T(8,128)(2,1)} %bitcast.5), calls=%async_computation.2 | async-start | bytes 2097152 | tf_op jit(solution)/shard_map/all_to_all | solution.py:211
  116.9 25.9 %all-to-all-done.2 = bf16[32,16,1024]{2,1,0:T(8,128)(2,1)S(1)} async-done(((bf16[32,16,1024]{2,1,0:T(8,128)(2,1)}), bf16[32,16,1024]{2,1,0:T(8,128)(2,1)S(1)}, u32[]{:S(2)}, u32[]{:S(2)}) %all-to-all-start.2) | async-done | bytes 1048608 | tf_op jit(solution)/shard_map/all_to_all | solution.py:211
  143.2 14.3 %all_to_all.21.got_ref = bf16[16,4,1024]{2,1,0:T(4,128)(2,1)S(1)} all-to-all(bf16[16,4,1024]{2,1,0:T(4,128)(2,1)S(1)} %reshape.35), channel_id=1, replica_groups=mesh['dp'=32,'expert'=16] {'expert'}, dimensions={0} | all-to-all | bytes 262144 | tf_op jit(solution)/shard_map/all_to_all | solution.py:215
  (33 shorter events, 4.9 us)
Async XLA Ops:
  26.8 1.3 copy-start.2
  28.1 35.1 %copy-start = (bf16[1,192,4096]{2,1,0:T(8,128)(2,1)S(1)}, bf16[1,192,4096]{2,1,0:T(8,128)(2,1)}, u32[]{:S(2)}) copy-start(bf16[1,192,4096]{2,1,0:T(8,128)(2,1)} %param.11) | copy-start | bytes 4718596
  28.1 35.1 %copy-start.1 = (bf16[1,192,4096]{2,1,0:T(8,128)(2,1)S(1)}, bf16[1,192,4096]{2,1,0:T(8,128)(2,1)}, u32[]{:S(2)}) copy-start(bf16[1,192,4096]{2,1,0:T(8,128)(2,1)} %param.12) | copy-start | bytes 4718596
  28.1 61.5 %all-to-all-start.1 = ((bf16[32,16,2048]{2,1,0:T(8,128)(2,1)}), bf16[32,16,2048]{2,1,0:T(8,128)(2,1)}, u32[]{:S(2)}, u32[]{:S(2)}) async-start(bf16[32,16,2048]{2,1,0:T(8,128)(2,1)} %bitcast.13), calls=%async_computation.1 | async-start | bytes 4194304 | tf_op jit(solution)/shard_map/all_to_all | solution.py:211
  38.1 1.4 copy-start.3
  39.6 7.9 %collective-permute-start = (bf16[192,1024]{1,0:T(8,128)(2,1)S(1)}, bf16[192,1024]{1,0:T(8,128)(2,1)S(1)}, u32[]{:S(2)}, u32[]{:S(2)}) collective-permute-start(bf16[192,1024]{1,0:T(8,128)(2,1)S(1)} %get-tuple-element.12), channel_id=1, source_target_pairs={{0,1},{1,0},{2,3},{3,2},{4,5},{5,4},{6,7},{7,6},{8,9},{9,8},{10,11... | collective-permute-start | bytes 1179656 | tf_op jit(solution)/shard_map/ppermute | solution.py:205
  41.6 12.2 %collective-permute-start.1 = (bf16[192,1024]{1,0:T(8,128)(2,1)S(1)}, bf16[192,1024]{1,0:T(8,128)(2,1)S(1)}, u32[]{:S(2)}, u32[]{:S(2)}) collective-permute-start(bf16[192,1024]{1,0:T(8,128)(2,1)S(1)} %get-tuple-element.13), channel_id=1, source_target_pairs={{0,2},{1,3},{2,0},{3,1},{4,6},{5,7},{6,4},{7,5},{8,10},{9,11},{10,... | collective-permute-start | bytes 1179656 | tf_op jit(solution)/shard_map/ppermute | solution.py:205
  43.5 19.6 %collective-permute-start.2 = (bf16[192,1024]{1,0:T(8,128)(2,1)S(1)}, bf16[192,1024]{1,0:T(8,128)(2,1)S(1)}, u32[]{:S(2)}, u32[]{:S(2)}) collective-permute-start(bf16[192,1024]{1,0:T(8,128)(2,1)S(1)} %get-tuple-element.14), channel_id=1, source_target_pairs={{0,3},{1,2},{2,1},{3,0},{4,7},{5,6},{6,5},{7,4},{8,11},{9,10},{10,... | collective-permute-start | bytes 1179656 | tf_op jit(solution)/shard_map/ppermute | solution.py:205
  63.1 0.8 copy-start.5
  63.9 0.8 copy-start.7
  64.6 0.7 copy-start.9
  89.6 6.5 %collective-permute-start.3 = (bf16[512,2048]{1,0:T(8,128)(2,1)}, bf16[512,2048]{1,0:T(8,128)(2,1)S(1)}, u32[]{:S(2)}, u32[]{:S(2)}) collective-permute-start(bf16[512,2048]{1,0:T(8,128)(2,1)} %bitcast.1.own_ref), channel_id=1, source_target_pairs={{0,1},{1,0},{2,3},{3,2},{4,5},{5,4},{6,7},{7,6},{8,9},{9,8},{10,11... | collective-permute-start | bytes 6291464 | tf_op jit(solution)/shard_map/ppermute | solution.py:205
  96.1 12.3 %copy-start.4 = (bf16[1,192,4096]{2,1,0:T(8,128)(2,1)S(1)}, bf16[1,192,4096]{2,1,0:T(8,128)(2,1)}, u32[]{:S(2)}) copy-start(bf16[1,192,4096]{2,1,0:T(8,128)(2,1)} %param.13) | copy-start | bytes 4718596
  96.1 12.3 %copy-start.8 = (bf16[192,1024]{1,0:T(8,128)(2,1)S(1)}, bf16[192,1024]{1,0:T(8,128)(2,1)}, u32[]{:S(2)}) copy-start(bf16[192,1024]{1,0:T(8,128)(2,1)} %copy-done.7) | copy-start | bytes 1179652
  97.2 12.3 %copy-start.6 = (bf16[192,1024]{1,0:T(8,128)(2,1)S(1)}, bf16[192,1024]{1,0:T(8,128)(2,1)}, u32[]{:S(2)}) copy-start(bf16[192,1024]{1,0:T(8,128)(2,1)} %copy-done.5) | copy-start | bytes 1179652
  97.2 12.3 %copy-start.10 = (bf16[192,1024]{1,0:T(8,128)(2,1)S(1)}, bf16[192,1024]{1,0:T(8,128)(2,1)}, u32[]{:S(2)}) copy-start(bf16[192,1024]{1,0:T(8,128)(2,1)} %copy-done.9) | copy-start | bytes 1179652
  97.2 8.1 %collective-permute-start.5 = (bf16[192,512]{1,0:T(8,128)(2,1)S(1)}, bf16[192,512]{1,0:T(8,128)(2,1)S(1)}, u32[]{:S(2)}, u32[]{:S(2)}) collective-permute-start(bf16[192,512]{1,0:T(8,128)(2,1)S(1)} %shard_map.79.own_act), channel_id=1, source_target_pairs={{0,2},{1,3},{2,0},{3,1},{4,6},{5,7},{6,4},{7,5},{8,10},{9,11},{10,... | collective-permute-start | bytes 589832 | tf_op jit(solution)/shard_map/ppermute | solution.py:205
  99.3 9.2 %collective-permute-start.4 = (bf16[192,512]{1,0:T(8,128)(2,1)S(1)}, bf16[192,512]{1,0:T(8,128)(2,1)S(1)}, u32[]{:S(2)}, u32[]{:S(2)}) collective-permute-start(bf16[192,512]{1,0:T(8,128)(2,1)S(1)} %shard_map.79.own_act), channel_id=1, source_target_pairs={{0,1},{1,0},{2,3},{3,2},{4,5},{5,4},{6,7},{7,6},{8,9},{9,8},{10,11... | collective-permute-start | bytes 589832 | tf_op jit(solution)/shard_map/ppermute | solution.py:205
  105.3 4.2 %collective-permute-start.6 = (bf16[192,512]{1,0:T(8,128)(2,1)S(1)}, bf16[192,512]{1,0:T(8,128)(2,1)S(1)}, u32[]{:S(2)}, u32[]{:S(2)}) collective-permute-start(bf16[192,512]{1,0:T(8,128)(2,1)S(1)} %collective-permute-done.5.z_act), channel_id=1, source_target_pairs={{0,1},{1,0},{2,3},{3,2},{4,5},{5,4},{6,7},{7,6},{8,9},{9,8},{10,11... | collective-permute-start | bytes 589832 | tf_op jit(solution)/shard_map/ppermute | solution.py:205
  111.2 46.3 %copy-start.11 = (bf16[4,4096]{1,0:T(4,128)(2,1)S(1)}, bf16[4,4096]{1,0:T(4,128)(2,1)}, u32[]{:S(2)}) copy-start(bf16[4,4096]{1,0:T(4,128)(2,1)} %resid_ref.1) | copy-start | bytes 98308
  111.2 31.6 %all-to-all-start.2 = ((bf16[32,16,1024]{2,1,0:T(8,128)(2,1)}), bf16[32,16,1024]{2,1,0:T(8,128)(2,1)S(1)}, u32[]{:S(2)}, u32[]{:S(2)}) async-start(bf16[32,16,1024]{2,1,0:T(8,128)(2,1)} %bitcast.5), calls=%async_computation.2 | async-start | bytes 2097152 | tf_op jit(solution)/shard_map/all_to_all | solution.py:211
